TPU v7x, 32 devices: a whole 2x2x4 slice. The times are simulated.
32 devices in a mesh: grp: 4 (over y, core), ctx: 8 (over z, x).
Axes of the slice: x: 2, y: 2, z: 4, core: 2. Of those that a mesh axis runs over, the one named last changes fastest.
Arguments:
- tokens: bfloat16 [16, 4224, 512], P('grp', 'ctx'), may hold values from -6 to 6
- query_counts: int32 [16], P('grp'), may hold values from 1 to 128, as said below
- cotangent: bfloat16 [16, 4224, 512], P('grp', 'ctx'), may hold values from -6 to 6
- query_weight: bfloat16 [512, 512], replicated, may hold values from -0.25 to 0.25
- key_weight: bfloat16 [512, 512], replicated, may hold values from -0.25 to 0.25
- value_weight: bfloat16 [512, 512], replicated, may hold values from -0.25 to 0.25
- output_weight: bfloat16 [512, 512], replicated, may hold values from -4 to 4
- inner_weight: bfloat16 [512, 1024], replicated, may hold values from -0.25 to 0.25
- inner_bias: bfloat16 [1024], replicated, may hold values from -1.5 to 1.5
- outer_weight: bfloat16 [1024, 512], replicated, may hold values from -0.1875 to 0.1875
- outer_bias: bfloat16 [512], replicated, may hold values from -1.5 to 1.5
- first_gain: bfloat16 [512], replicated, may hold values from 0.25 to 1.75
- first_shift: bfloat16 [512], replicated, may hold values from -1.5 to 1.5
- second_gain: bfloat16 [512], replicated, may hold values from 0.25 to 1.75
- second_shift: bfloat16 [512], replicated, may hold values from -1.5 to 1.5
Outputs:
- layer_out: bfloat16 [16, 4224, 512], P('grp', 'ctx')
- grad_tokens: float32 [16, 4224, 512], P('grp', 'ctx')
- grad_query: float32 [512, 512], replicated
- grad_key: float32 [512, 512], replicated
- grad_value: float32 [512, 512], replicated
- grad_output: float32 [512, 512], replicated
- grad_inner: float32 [512, 1024], replicated
- grad_inner_bias: float32 [1024], replicated
- grad_outer: float32 [1024, 512], replicated
- grad_outer_bias: float32 [512], replicated
- grad_first_gain: float32 [512], replicated
- grad_first_shift: float32 [512], replicated
- grad_second_gain: float32 [512], replicated
- grad_second_shift: float32 [512], replicated
Inputs may be any that keep to these rules, and one draw needn't show every extreme that they name: `query_counts`: for every g, among neighbourhoods g * 4 to g * 4 + 3 at least one has exactly 128 live queries.
All inputs are finite; a program needn't handle non-finite values.
Results may differ from a plain program's by a relative error of at most 0.013.
Values may be sent and summed in bfloat16 or wider, within the bound.
No kernel may reach another device: no remote copies, remote signals or barrier semaphores. Data moves between devices by JAX's collectives and lax.ppermute only.
A program may use at most 832 MiB of HBM per device.

v0:
```python
from functools import partial

import jax
import jax.numpy as jnp
from jax import lax
from jax.sharding import PartitionSpec as P

HEADS = 4
CTX = 4096
QUERIES = 128
NBLK = 4
HD = 128


EPSILON = 1e-05


def product(left, right):
    return jnp.dot(left, right, preferred_element_type=jnp.float32)


def contract_rows(left, right):
    return lax.dot_general(
        left, right, (((0,), (0,)), ((), ())), preferred_element_type=jnp.float32
    )


def contract_last(left, right):
    return lax.dot_general(
        left, right, (((1,), (1,)), ((), ())), preferred_element_type=jnp.float32
    )


def norm_forward(values, gain, shift):
    center = values - jnp.mean(values, axis=-1, keepdims=True)
    inverse = lax.rsqrt(jnp.mean(center * center, axis=-1, keepdims=True) + EPSILON)
    normed = center * inverse
    return (normed * gain + shift, normed, inverse)


def norm_backward(upstream, normed, inverse, gain):
    scaled = upstream * gain
    plain_mean = jnp.mean(scaled, axis=-1, keepdims=True)
    cross_mean = jnp.mean(scaled * normed, axis=-1, keepdims=True)
    value_grad = inverse * (scaled - plain_mean - normed * cross_mean)
    return (value_grad, jnp.sum(upstream * normed, axis=0), jnp.sum(upstream, axis=0))


def on_device(
    tokens,
    query_counts,
    cotangent,
    query_weight,
    key_weight,
    value_weight,
    output_weight,
    inner_weight,
    inner_bias,
    outer_weight,
    outer_bias,
    first_gain,
    first_shift,
    second_gain,
    second_shift,
):
    member = lax.axis_index("ctx")
    ctx_count = lax.axis_size("ctx")
    context_dev = CTX // ctx_count
    query_dev = QUERIES // ctx_count
    nb_dev = tokens.shape[0]
    rows_dev = tokens.shape[1]
    width = tokens.shape[2]
    heads_count = HEADS
    head_width = HD
    block_count = nb_dev // NBLK
    scale = head_width ** (-0.5)
    total_rows = nb_dev * rows_dev
    tokens_flat = tokens.reshape(total_rows, width)
    context_rows = tokens[:, :context_dev]
    context_flat = context_rows.reshape(nb_dev * context_dev, width)
    queries = (
        product(tokens_flat, query_weight).astype(jnp.bfloat16).reshape(nb_dev, rows_dev, width)
    )
    keys_own = (
        product(context_flat, key_weight).astype(jnp.bfloat16).reshape(nb_dev, context_dev, width)
    )
    values_own = (
        product(context_flat, value_weight).astype(jnp.bfloat16).reshape(nb_dev, context_dev, width)
    )
    sources = (keys_own, values_own)

    def to_blocks(array):
        return array.reshape((block_count, NBLK) + array.shape[1:])

    def fetch(source):
        keys_mine, values_mine = source
        keys_flat, values_flat = (
            lax.all_gather(keys_mine, "ctx", axis=1, tiled=True),
            lax.all_gather(values_mine, "ctx", axis=1, tiled=True),
        )
        return (keys_flat, values_flat, keys_mine, values_mine)

    def split_heads(array):
        return array.reshape(array.shape[0], array.shape[1], heads_count, head_width)

    def attend(carry, operands):
        queries_blk, source = operands
        keys_flat, values_flat, keys_mine, values_mine = fetch(source)
        query_heads = split_heads(queries_blk)
        scores = (
            jnp.einsum(
                "nrhd,nkhd->nhrk",
                query_heads,
                split_heads(keys_flat),
                preferred_element_type=jnp.float32,
            )
            * scale
        )
        log_total = jax.nn.logsumexp(scores, axis=-1, keepdims=True)
        soft_low = jnp.exp(scores - log_total).astype(jnp.bfloat16)
        mixed = jnp.einsum(
            "nhrk,nkhd->nrhd",
            soft_low,
            split_heads(values_flat),
            preferred_element_type=jnp.float32,
        )
        attended_blk = mixed.reshape(NBLK, rows_dev, width).astype(jnp.bfloat16)
        return (carry, (attended_blk, log_total[..., 0]))

    zero = jnp.zeros((), jnp.float32)
    _, (attended_b, lse_b) = lax.scan(
        attend, zero, (to_blocks(queries), jax.tree.map(to_blocks, sources))
    )
    attended_flat = attended_b.reshape(total_rows, width)
    slot_local = jnp.arange(rows_dev, dtype=jnp.int32) - context_dev
    slot_global = member * query_dev + slot_local
    live_rows = jnp.logical_or(
        slot_local[None, :] < 0, slot_global[None, :] < query_counts[:, None]
    )
    live_flat = live_rows.astype(jnp.float32).reshape(total_rows, 1)
    inner_bias_f = inner_bias.astype(jnp.float32)
    outer_bias_f = outer_bias.astype(jnp.float32)
    first_gain_f = first_gain.astype(jnp.float32)
    second_gain_f = second_gain.astype(jnp.float32)
    first_sum = tokens_flat.astype(jnp.float32) + product(attended_flat, output_weight)
    hidden, normed_one, inverse_one = norm_forward(
        first_sum, first_gain_f, first_shift.astype(jnp.float32)
    )
    hidden_low = hidden.astype(jnp.bfloat16)
    inner = product(hidden_low, inner_weight) + inner_bias_f
    gelu_value, gelu_back = jax.vjp(partial(jax.nn.gelu, approximate=False), inner)
    activated = gelu_value.astype(jnp.bfloat16)
    second_sum = hidden + product(activated, outer_weight) + outer_bias_f
    result, normed_two, inverse_two = norm_forward(
        second_sum, second_gain_f, second_shift.astype(jnp.float32)
    )
    layer_out = (result * live_flat).astype(jnp.bfloat16).reshape(nb_dev, rows_dev, width)
    upstream = cotangent.reshape(total_rows, width).astype(jnp.float32) * live_flat
    second_grad, grad_second_gain, grad_second_shift = norm_backward(
        upstream, normed_two, inverse_two, second_gain_f
    )
    outer_grad = second_grad.astype(jnp.bfloat16)
    grad_outer = contract_rows(activated, outer_grad)
    grad_outer_bias = jnp.sum(outer_grad.astype(jnp.float32), axis=0)
    inner_grad = gelu_back(contract_last(outer_grad, outer_weight))[0].astype(jnp.bfloat16)
    grad_inner = contract_rows(hidden_low, inner_grad)
    grad_inner_bias = jnp.sum(inner_grad.astype(jnp.float32), axis=0)
    hidden_grad = second_grad + contract_last(inner_grad, inner_weight)
    first_grad, grad_first_gain, grad_first_shift = norm_backward(
        hidden_grad, normed_one, inverse_one, first_gain_f
    )
    branch_grad = first_grad.astype(jnp.bfloat16)
    grad_output = contract_rows(attended_flat, branch_grad)
    attended_grad = (
        contract_last(branch_grad, output_weight)
        .astype(jnp.bfloat16)
        .reshape(nb_dev, rows_dev, width)
    )

    def attend_back(carry, operands):
        queries_blk, grads_blk, lse_blk, source = operands
        keys_flat, values_flat, keys_mine, values_mine = fetch(source)
        query_heads = split_heads(queries_blk)
        grad_heads = split_heads(grads_blk)
        key_heads = split_heads(keys_flat)
        value_heads = split_heads(values_flat)
        scores = (
            jnp.einsum(
                "nrhd,nkhd->nhrk", query_heads, key_heads, preferred_element_type=jnp.float32
            )
            * scale
        )
        soft = jnp.exp(scores - lse_blk[..., None])
        soft_grad = jnp.einsum(
            "nrhd,nkhd->nhrk", grad_heads, value_heads, preferred_element_type=jnp.float32
        )
        row_delta = jnp.sum(soft * soft_grad, axis=-1)
        score_grad = (soft * (soft_grad - row_delta[..., None])).astype(jnp.bfloat16)
        query_grad = (
            jnp.einsum("nhrk,nkhd->nrhd", score_grad, key_heads, preferred_element_type=jnp.float32)
            * scale
        )
        query_grad = query_grad.reshape(NBLK, rows_dev, width).astype(jnp.bfloat16)
        soft_low = soft.astype(jnp.bfloat16)
        key_part = (
            jnp.einsum(
                "nhrk,nrhd->nkhd", score_grad, query_heads, preferred_element_type=jnp.float32
            )
            * scale
        )
        value_part = jnp.einsum(
            "nhrk,nrhd->nkhd", soft_low, grad_heads, preferred_element_type=jnp.float32
        )
        key_sum, value_sum = (
            lax.psum_scatter(
                key_part.reshape(NBLK, -1, width), "ctx", scatter_dimension=1, tiled=True
            ),
            lax.psum_scatter(
                value_part.reshape(NBLK, -1, width), "ctx", scatter_dimension=1, tiled=True
            ),
        )
        key_grad = key_sum.astype(jnp.bfloat16)
        value_grad = value_sum.astype(jnp.bfloat16)
        return (carry, (query_grad, key_grad, value_grad))

    _, (query_grad_b, key_grad_b, value_grad_b) = lax.scan(
        attend_back,
        zero,
        (to_blocks(queries), to_blocks(attended_grad), lse_b, jax.tree.map(to_blocks, sources)),
    )
    query_grad = query_grad_b.reshape(total_rows, width)
    key_grad = key_grad_b.reshape(nb_dev * context_dev, width)
    value_grad = value_grad_b.reshape(nb_dev * context_dev, width)
    grad_query = contract_rows(tokens_flat, query_grad)
    grad_key = contract_rows(context_flat, key_grad)
    grad_value = contract_rows(context_flat, value_grad)
    token_grad = (first_grad + contract_last(query_grad, query_weight)).reshape(
        nb_dev, rows_dev, width
    )
    context_back = (
        contract_last(key_grad, key_weight) + contract_last(value_grad, value_weight)
    ).reshape(nb_dev, context_dev, width)
    grad_tokens = jnp.concatenate(
        [token_grad[:, :context_dev] + context_back, token_grad[:, context_dev:]], axis=1
    )
    finals = lax.psum(
        (
            grad_query,
            grad_key,
            grad_value,
            grad_output,
            grad_inner,
            grad_inner_bias,
            grad_outer,
            grad_outer_bias,
            grad_first_gain,
            grad_first_shift,
            grad_second_gain,
            grad_second_shift,
        ),
        ("grp", "ctx"),
    )
    return (layer_out, grad_tokens) + tuple(finals)


def solution(mesh):
    return jax.shard_map(
        on_device,
        mesh=mesh,
        in_specs=(
            P("grp", "ctx", None),
            P("grp"),
            P("grp", "ctx", None),
            P(),
            P(),
            P(),
            P(),
            P(),
            P(),
            P(),
            P(),
            P(),
            P(),
            P(),
            P(),
        ),
        out_specs=(
            P("grp", "ctx", None),
            P("grp", "ctx", None),
            P(),
            P(),
            P(),
            P(),
            P(),
            P(),
            P(),
            P(),
            P(),
            P(),
            P(),
            P(),
        ),
        check_vma=False,
    )
```

profile of v0, /device:TPU:0, one launch (start us, length us, event | category | flops | bytes accessed | tf_op | source)
XLA Modules:
  0.0 1978.9 jit_solution(8288357140683012218)
XLA Ops:
  12.7 4.2 copy.37
  20.6 4.3 copy.36
  34.4 5.1 reshape.230
  43.5 204.0 %all-gather.5.cloned.1.call-done = bf16[4,4096,512]{1,2,0:T(8,128)(2,1)} async-done(((bf16[4,512,512]{1,2,0:T(8,128)(2,1)}), bf16[4,4096,512]{1,2,0:T(8,128)(2,1)}) %all-gather.5.cloned.1.call-update) | async-done | bytes 16777232 | tf_op jit(solution)/shard_map/while/body/eval_jaxpr/all_gather | solution.py:98
  247.5 56.0 %multiply_reduce_fusion.1 = (f32[4,4,528]{2,1,0:T(4,128)S(1)}, f32[4,4,528,4096]{3,2,1,0:T(8,128)}) fusion(bf16[4,4096,4,128]{1,3,2,0:T(8,128)(2,1)} %bitcast.111, bf16[4,528,4,128]{3,2,1,0:T(4,128)(2,1)} %reshape.230), kind=kOutput, calls=%fused_computation.4 | convolution fusion | flops 8927567872 | bytes 157385728 | tf_op jit(solution)/shard_map/while/body/eval_jaxpr/nrhd,nkhd->nhrk/dot_general | solution.py:111
  303.5 42.9 %exponential_reduce_fusion = f32[4,4,528]{2,1,0:T(4,128)S(1)} fusion(f32[4,4,528,4096]{3,2,1,0:T(8,128)} %get-tuple-element.113, f32[4,4,528]{2,1,0:T(4,128)S(1)} %is-finite_select_fusion), kind=kLoop, calls=%fused_computation.3 | loop fusion | flops 103800576 | bytes 138479616 | tf_op jit(solution)/shard_map/while/body/eval_jaxpr/reduce_sum | solution.py:119
  346.4 129.6 %all-gather.3.cloned.1.call-done = bf16[4,4096,512]{1,2,0:T(8,128)(2,1)} async-done(((bf16[4,512,512]{1,2,0:T(8,128)(2,1)}), bf16[4,4096,512]{1,2,0:T(8,128)(2,1)}) %all-gather.3.cloned.1.call-update) | async-done | bytes 16777232 | tf_op jit(solution)/shard_map/while/body/eval_jaxpr/all_gather | solution.py:99
  476.1 50.2 %convert_bitcast_fusion = bf16[4,528,4,128]{3,1,2,0:T(8,128)(2,1)} fusion(bf16[4,4096,4,128]{1,3,2,0:T(8,128)(2,1)} %bitcast.94, f32[4,4,528,4096]{3,2,1,0:T(8,128)} %get-tuple-element.113, f32[4,4,528]{2,1,0:T(4,128)S(1)} %log_add_fusion), kind=kOutput, calls=%fused_computation.67 | convolution fusion | flops 8963260416 | bytes 157385728 | tf_op jit(solution)/shard_map/while/body/eval_jaxpr/nhrk,nkhd->nrhd/dot_general | solution.py:121
  531.3 24.0 %multiply_convert_fusion.1 = (bf16[2112,1024]{1,0:T(8,128)(2,1)S(1)}, f32[2112,1024]{1,0:T(8,128)}, f32[2112,1024]{1,0:T(8,128)}) fusion(f32[1024]{0:T(1024)S(1)} %convert_element_type.135, bf16[512,1024]{1,0:T(8,128)(2,1)S(1)} %copy-done, f32[2112,512]{1,0:T(8,128)S(1)} %get-tuple-element.115, f32[512]{0:T(512)S(1)} %convert_element_type.133, ...), kind=kOutput, calls=%fused_computation.13 | convolution fusion | flops 2362736640 | bytes 27025920 | tf_op jit(solution)/shard_map/dot_general | solution.py:19
  566.7 11.2 convert_reduce_fusion
  577.9 4.7 multiply_reduce_fusion.3
  593.3 59.5 %fusion.1 = f32[4,4,128,4096]{3,2,1,0:T(8,128)} fusion(f32[4,4,528,4096]{3,2,1,0:T(8,128)} %get-tuple-element.113, f32[4,4,528]{2,1,0:T(4,128)S(1)} %log_add_fusion, bf16[4,528,4,128]{3,2,1,0:T(4,128)(2,1)S(1)} %reshape.233), kind=kOutput, calls=%fused_computation.8 | convolution fusion | flops 8962179072 | bytes 174162944 | tf_op jit(solution)/shard_map/while/body/eval_jaxpr/nhrk,nrhd->nkhd/dot_general | solution.py:211
  652.8 31.1 %copy.49 = f32[4,4096,512]{2,1,0:T(8,128)} copy(f32[4,4096,512]{1,2,0:T(8,128)} %bitcast.92) | data formatting | bytes 67108864 | tf_op jit(solution)/shard_map/while/body/eval_jaxpr/reshape | solution.py:219
  684.0 96.6 %multiply_reduce_fusion = (f32[4,4,528]{2,1,0:T(4,128)S(1)}, f32[4,4,528,4096]{3,2,1,0:T(8,128)}) fusion(f32[4,4,528,4096]{3,2,1,0:T(8,128)} %get-tuple-element.113, f32[4,4,528]{2,1,0:T(4,128)S(1)} %log_add_fusion, bf16[4,4096,4,128]{1,3,2,0:T(8,128)(2,1)} %bitcast.95, bf16[4,528,4,128]{3,2,1,0:T(4,128)(2,1)S(1)} %reshape.233), kind=kOutput, calls=%fused_computation.1 | convolution fusion | flops 8996773888 | bytes 295831552 | tf_op jit(solution)/shard_map/while/body/eval_jaxpr/nrhd,nkhd->nhrk/dot_general | solution.py:194
  780.6 110.7 %multiply_convert_fusion = bf16[4,4,528,4096]{3,2,1,0:T(8,128)(2,1)} fusion(f32[4,4,528,4096]{3,2,1,0:T(8,128)} %get-tuple-element.121, f32[4,4,528,4096]{3,2,1,0:T(8,128)} %get-tuple-element.113, f32[4,4,528]{2,1,0:T(4,128)S(1)} %get-tuple-element.120, f32[4,4,528]{2,1,0:T(4,128)S(1)} %log_add_fusion), kind=kLoop, calls=%fused_computation | loop fusion | flops 173015040 | bytes 346097664 | tf_op jit(solution)/shard_map/while/body/eval_jaxpr/convert_element_type | solution.py:198
  891.3 35.0 %broadcast_multiply_fusion = f32[4,4,128,4096]{3,2,1,0:T(8,128)} fusion(bf16[4,4,528,4096]{3,2,1,0:T(8,128)(2,1)} %multiply_convert_fusion, bf16[4,528,4,128]{3,2,1,0:T(4,128)(2,1)S(1)} %copy-done.13), kind=kOutput, calls=%fused_computation.6 | convolution fusion | flops 8866758656 | bytes 104923136 | tf_op jit(solution)/shard_map/while/body/eval_jaxpr/nhrk,nrhd->nkhd/dot_general | solution.py:206
  926.3 31.5 %copy.47 = f32[4,4096,512]{2,1,0:T(8,128)} copy(f32[4,4096,512]{1,2,0:T(8,128)} %bitcast.93) | data formatting | bytes 67108864 | tf_op jit(solution)/shard_map/while/body/eval_jaxpr/reshape | solution.py:216
  957.9 35.4 %multiply_convert_fusion.2 = bf16[4,4,128,528]{2,3,1,0:T(8,128)(2,1)} fusion(bf16[4,4096,4,128]{1,3,2,0:T(8,128)(2,1)} %bitcast.112, bf16[4,4,528,4096]{3,2,1,0:T(8,128)(2,1)} %multiply_convert_fusion), kind=kOutput, calls=%fused_computation.39 | convolution fusion | flops 8860532736 | bytes 88145920 | tf_op jit(solution)/shard_map/while/body/eval_jaxpr/nhrk,nkhd->nrhd/dot_general | solution.py:200
  997.5 4.8 fusion.16
  1002.3 7.7 fusion.39
  1014.2 211.1 %reduce-scatter.5.cloned.1.call-done = f32[4,512,512]{2,1,0:T(8,128)} async-done(((f32[4,4096,512]{2,1,0:T(8,128)}), f32[4,512,512]{2,1,0:T(8,128)}) %reduce-scatter.5.cloned.1.call-update) | async-done | bytes 4194320 | tf_op jit(solution)/shard_map/while/body/eval_jaxpr/reduce_scatter | solution.py:218
  1231.3 539.7 %reduce-scatter.3.cloned.1.call-done = f32[4,512,512]{2,1,0:T(8,128)} async-done(((f32[4,4096,512]{2,1,0:T(8,128)}), f32[4,512,512]{2,1,0:T(8,128)}) %reduce-scatter.3.cloned.1.call-update) | async-done | bytes 4194320 | tf_op jit(solution)/shard_map/while/body/eval_jaxpr/reduce_scatter | solution.py:215
  1785.5 41.3 %all-reduce = (f32[1024]{0:T(1024)}, f32[512]{0:T(512)}, f32[512]{0:T(512)}, f32[512]{0:T(512)}, f32[512]{0:T(512)}, /*index=5*/f32[512]{0:T(512)}) all-reduce(f32[1024]{0:T(1024)S(1)} %copy-done.38, f32[512]{0:T(512)S(1)} %copy-done.34, f32[512]{0:T(512)S(1)} %copy-done.40, ...), channel_id=1, replica_groups=mesh['grp'=4,'ctx'=8] {'grp','ctx'}, use_global_device_ids=true, to_apply=%region_19.20 | all-reduce | flops 3584 | bytes 28672 | tf_op jit(solution)/shard_map/psum | solution.py:246
  1833.4 125.4 %all-reduce.4.cloned.1.call-done = (f32[512,512]{0,1:T(8,128)}, f32[512,512]{0,1:T(8,128)}, f32[512,512]{0,1:T(8,128)}, f32[512,512]{1,0:T(8,128)}, f32[512,1024]{1,0:T(8,128)}, /*index=5*/f32[1024,512]{1,0:T(8,128)}) async-done(((f32[512,512]{0,1:T(8,128)}, f32[512,512]{0,1:T(8,128)}, f32[512,512]{0,1:T(8,128)}, f32[512,512]{1,0:T(8,128)}, f32[512,1024]{1,0:T(8,128)}, /*index=5*/f32[1024,512]{1,0:T(8,128)}), ...) | async-done | bytes 8388624 | tf_op jit(solution)/shard_map/psum | solution.py:246
  (193 shorter events, 98.1 us)
Async XLA Ops:
  7.2 524.1 %copy-start = (bf16[512,1024]{1,0:T(8,128)(2,1)S(1)}, bf16[512,1024]{1,0:T(8,128)(2,1)}, u32[]{:S(2)}) copy-start(bf16[512,1024]{1,0:T(8,128)(2,1)} %param.22) | copy-start | bytes 3145732
  7.2 240.3 %all-gather.5.cloned.1.call-start = ((), (), s32[]{:S(2)}) async-start(), calls=%async_computation.3 | async-start | bytes 18874368 | tf_op jit(solution)/shard_map/while/body/eval_jaxpr/all_gather | solution.py:98
  16.9 459.2 %all-gather.3.cloned.1.call-start = ((), (), s32[]{:S(2)}) async-start(), calls=%async_computation.2 | async-start | bytes 18874368 | tf_op jit(solution)/shard_map/while/body/eval_jaxpr/all_gather | solution.py:99
  20.6 10.1 copy-start.4
  24.9 1200.3 %reduce-scatter.5.cloned.1.call-start = ((), (), s32[]{:S(2)}) async-start(), calls=%async_computation.5 | async-start | bytes 37748736 | tf_op jit(solution)/shard_map/while/body/eval_jaxpr/reduce_scatter | solution.py:218
  25.0 557.6 %copy-start.35 = (f32[512]{0:T(512)}, f32[512]{0:T(512)S(1)}, u32[]{:S(2)}) copy-start(f32[512]{0:T(512)S(1)} %convert_element_type.132) | copy-start | bytes 6148
  25.0 530.3 %copy-start.42 = (f32[512]{0:T(512)}, f32[512]{0:T(512)S(1)}, u32[]{:S(2)}) copy-start(f32[512]{0:T(512)S(1)} %convert_element_type.133) | copy-start | bytes 6148
  25.1 9.3 copy-start.30
  26.4 13.0 copy-start.23
  530.3 52.3 %copy-start.3 = (f32[2112,512]{1,0:T(8,128)}, f32[2112,512]{1,0:T(8,128)S(1)}, u32[]{:S(2)}) copy-start(f32[2112,512]{1,0:T(8,128)S(1)} %get-tuple-element.115) | copy-start | bytes 12976132
  530.4 52.3 %copy-start.25 = (f32[2112]{0:T(1024)}, f32[2112]{0:T(1024)S(1)}, u32[]{:S(2)}) copy-start(f32[2112]{0:T(1024)S(1)} %broadcast_multiply_fusion.5) | copy-start | bytes 25348
  531.3 51.4 %copy-start.27 = (f32[2112]{0:T(1024)}, f32[2112]{0:T(1024)S(1)}, u32[]{:S(2)}) copy-start(f32[2112]{0:T(1024)S(1)} %add_rsqrt_fusion.1) | copy-start | bytes 25348
  531.3 24.0 %copy-start.44 = (f32[512]{0:T(512)S(1)}, f32[512]{0:T(512)}, u32[]{:S(2)}) copy-start(f32[512]{0:T(512)} %convert_element_type.137) | copy-start | bytes 6148
  531.3 24.0 %copy-start.51 = (bf16[1024,512]{1,0:T(8,128)(2,1)S(1)}, bf16[1024,512]{1,0:T(8,128)(2,1)}, u32[]{:S(2)}) copy-start(bf16[1024,512]{1,0:T(8,128)(2,1)} %param.24) | copy-start | bytes 3145732
  566.7 11.2 copy-start.15
  683.9 1087.1 %reduce-scatter.3.cloned.1.call-start = ((), (), s32[]{:S(2)}) async-start(), calls=%async_computation.4 | async-start | bytes 37748736 | tf_op jit(solution)/shard_map/while/body/eval_jaxpr/reduce_scatter | solution.py:215
  780.6 110.7 %copy-start.13 = (bf16[4,528,4,128]{3,2,1,0:T(4,128)(2,1)S(1)}, bf16[4,528,4,128]{3,2,1,0:T(4,128)(2,1)}, u32[]{:S(2)}) copy-start(bf16[4,528,4,128]{3,2,1,0:T(4,128)(2,1)} %reshape.230) | copy-start | bytes 6488068
  957.8 35.5 %copy-start.5 = (bf16[4,528,512]{2,1,0:T(8,128)(2,1)S(1)}, bf16[4,528,512]{2,1,0:T(8,128)(2,1)}, u32[]{:S(2)}) copy-start(bf16[4,528,512]{2,1,0:T(8,128)(2,1)} %param.15) | copy-start | bytes 6488068
  957.8 1001.0 %all-reduce.4.cloned.1.call-start = ((), (), s32[]{:S(2)}) async-start(), calls=%async_computation.6 | async-start | bytes 16777216 | tf_op jit(solution)/shard_map/psum | solution.py:246
  997.4 12.6 slice-start
  997.4 12.6 slice-start.6
  1002.3 7.8 copy-start.43
  1779.5 47.3 %copy-start.12 = (bf16[4,512,512]{2,1,0:T(8,128)(2,1)S(1)}, bf16[4,512,512]{2,1,0:T(8,128)(2,1)}, u32[]{:S(2)}) copy-start(bf16[4,512,512]{2,1,0:T(8,128)(2,1)} %copy-done.11) | copy-start | bytes 6291460
  1779.6 47.3 %copy-start.21 = (bf16[512,512]{1,0:T(8,128)(2,1)S(1)}, bf16[512,512]{1,0:T(8,128)(2,1)}, u32[]{:S(2)}) copy-start(bf16[512,512]{1,0:T(8,128)(2,1)} %param.19) | copy-start | bytes 1572868
  (43 other events, 181.3 us)
Sparse Core Ops, SparseCore 0:
  17.0 230.4 all-gather.4
  250.1 225.9 all-gather.2
  684.0 541.1 reduce-scatter.4
  1228.9 542.0 reduce-scatter.2
  1777.8 180.9 all-reduce.3
where the time goes:
time: 1980 us
  waiting for transfers between devices  1210 us (61%)
  matrix products  423 us (21%)
  other arithmetic  181 us (9%)
  local copies, waits for them, and re-layouts  109 us (6%)
  blocking collectives  41.3 us (2%)
    reduce_scatter x1, waiting for transfers between devices, attend_back(): lax.psum_scatter(key_part.reshape(NBLK, -1, width), 'ctx', scatter_dimens...  540 us
    reduce_scatter x1, waiting for transfers between devices, attend_back(): lax.psum_scatter(value_part.reshape(NBLK, -1, width), 'ctx', scatter_dime...  211 us
    all_gather x1, waiting for transfers between devices, fetch(): lax.all_gather(keys_mine, 'ctx', axis=1, tiled=True)  204 us
    all_gather x1, waiting for transfers between devices, fetch(): lax.all_gather(values_mine, 'ctx', axis=1, tiled=True)  130 us
    psum x1, waiting for transfers between devices, on_device(): lax.psum((grad_query, grad_key, grad_value, grad_output, grad_inner, grad...  125 us
    convert_element_type x1, other arithmetic, attend_back(): (soft * (soft_grad - row_delta[..., None])).astype(jnp.bfloat16)  111 us
    dot_general x1, matrix products, attend_back(): jnp.einsum('nrhd,nkhd->nhrk', grad_heads, value_heads, preferred_element_...  96.6 us
    dot_general x1, matrix products, attend_back(): jnp.einsum('nhrk,nrhd->nkhd', soft_low, grad_heads, preferred_element_typ...  59.5 us
  transfers between devices with their start and end apart: 5, of which 5 were waited for; matrix products, arithmetic and copies ran while one was open for 24% of the time, Pallas kernels for 0%

commit v1 on v0

--- a/solution.py
+++ b/solution.py
@@ -3,6 +3,8 @@
 import jax
 import jax.numpy as jnp
 from jax import lax
+from jax.experimental import pallas as pl
+from jax.experimental.pallas import tpu as pltpu
 from jax.sharding import PartitionSpec as P
 
 HEADS = 4
@@ -46,7 +48,7 @@
     return (value_grad, jnp.sum(upstream * normed, axis=0), jnp.sum(upstream, axis=0))
 
 
-def on_device(
+def spread_plan(
     tokens,
     query_counts,
     cotangent,
@@ -263,9 +265,597 @@
     return (layer_out, grad_tokens) + tuple(finals)
 
 
+BF16, F32 = jnp.bfloat16, jnp.float32
+MIB = 2**20
+AXES = ("grp", "ctx")
+LANES = 128
+
+
+def one_chip_each(mesh):
+    return mesh.shape["grp"] % 2 == 0 and mesh.shape["ctx"] == 2 * NBLK
+
+
+def dot(left, right, over_left, over_right):
+    return lax.dot_general(
+        left, right, (((over_left,), (over_right,)), ((), ())), preferred_element_type=F32
+    )
+
+
+def kernel_call(body, grid, ins, outs, scratch, flops, moved, *operands, exps=0):
+    return pl.pallas_call(
+        body,
+        grid=grid,
+        in_specs=[pl.BlockSpec(shape, index) for shape, index in ins],
+        out_specs=[pl.BlockSpec(shape, index) for shape, index, _, _ in outs],
+        out_shape=[jax.ShapeDtypeStruct(shape, kind) for _, _, shape, kind in outs],
+        scratch_shapes=scratch,
+        cost_estimate=pl.CostEstimate(flops=flops, bytes_accessed=moved, transcendentals=exps),
+        compiler_params=pltpu.CompilerParams(vmem_limit_bytes=60 * MIB),
+    )(*operands)
+
+
+def project_kernel(context, scale, own, other, wq, wk, wv, q_out, k_out, v_out):
+    rows = own[0]
+    queries = (dot(rows, wq[...], 1, 0) * scale).astype(BF16)
+    for h in range(HEADS):
+        q_out[h] = queries[:, h * HD : (h + 1) * HD]
+    for side, keys_of in enumerate((rows[:context], other[0])):
+        keys = dot(keys_of, wk[...], 1, 0).astype(BF16)
+        values = dot(keys_of, wv[...], 1, 0).astype(BF16)
+        for h in range(HEADS):
+            k_out[h, side, 0] = keys[:, h * HD : (h + 1) * HD]
+            v_out[h, side, 0] = values[:, h * HD : (h + 1) * HD]
+
+
+def project(own, other, wq, wk, wv, scale):
+    blocks, rows, width = own.shape
+    context = other.shape[1]
+    whole = (width, width)
+    block = lambda b: (b, 0, 0)
+    fixed = lambda b: (0, 0)
+    key_spec = (
+        (HEADS, 2, 1, context, HD),
+        lambda b: (0, 0, b, 0, 0),
+        (HEADS, 2, blocks, context, HD),
+        BF16,
+    )
+    q, k, v = kernel_call(
+        partial(project_kernel, context, scale),
+        (blocks,),
+        [((1, rows, width), block), ((1, context, width), block)] + [(whole, fixed)] * 3,
+        [
+            ((HEADS, rows, HD), lambda b: (0, b, 0), (HEADS, blocks * rows, HD), BF16),
+            key_spec,
+            key_spec,
+        ],
+        [],
+        2 * blocks * width * width * (rows + 4 * context),
+        4 * blocks * width * (rows + 3 * context),
+        own,
+        other,
+        wq,
+        wk,
+        wv,
+    )
+    flat = (HEADS, 2 * blocks * context, HD)
+    return q, k.reshape(flat), v.reshape(flat)
+
+
+def forward_kernel(
+    steps, row_blocks, chunk, q_ref, k_ref, v_ref, p_ref, o_ref, inv_ref, s_even, s_odd, top_even, top_odd, v_wide
+):
+    t = pl.program_id(0)
+    rows, hd = q_ref.shape[-2:]
+    keys = k_ref.shape[-2]
+
+    @pl.when(t == 0)
+    def _():
+        v_wide[:, hd:] = jnp.ones((keys, hd), BF16)
+
+    @pl.when((t > 0) & (lax.rem(t - 1, row_blocks) == 0))
+    def _():
+        v_wide[:, :hd] = v_ref[0]
+
+    def body(score, weigh, s_now, s_before, top_now, top_before):
+        if score:
+            q = q_ref[0]
+            high = None
+        if weigh:
+            peak = jnp.max(top_before[...], axis=-1, keepdims=True)
+            total = jnp.zeros((rows, 2 * hd), F32)
+        for c in range(keys // chunk):
+            at = slice(c * chunk, (c + 1) * chunk)
+            if score:
+                scores = dot(q, k_ref[0, at, :], 1, 1)
+                s_now[:, at] = scores
+                for j in range(chunk // LANES):
+                    part = scores[:, j * LANES : (j + 1) * LANES]
+                    high = part if high is None else jnp.maximum(high, part)
+            if weigh:
+                soft = jnp.exp2(s_before[:, at] - peak).astype(BF16)
+                p_ref[0, 0, :, at] = soft
+                total = total + dot(soft, v_wide[at, :], 1, 0)
+        if score:
+            top_now[...] = high
+        if weigh:
+            inverse = 1.0 / total[:, hd:]
+            o_ref[...] = total[:, :hd] * inverse
+            inv_ref[0] = inverse
+
+    even = (s_even, s_odd, top_even, top_odd)
+    odd = (s_odd, s_even, top_odd, top_even)
+    inside = (t > 0) & (t < steps)
+    pl.when(inside & (lax.rem(t, 2) == 0))(lambda: body(True, True, *even))
+    pl.when(inside & (lax.rem(t, 2) == 1))(lambda: body(True, True, *odd))
+    pl.when(t == 0)(lambda: body(True, False, *even))
+    pl.when(t == steps)(lambda: body(False, True, *(odd if steps % 2 else even)))
+
+
+def attention_forward(q, k, v, row_blocks, chunk=512):
+    heads, total, hd = q.shape
+    keys = k.shape[1]
+    rows = total // row_blocks
+    steps = heads * row_blocks
+    ahead = lambda t: jnp.minimum(t, steps - 1)
+    behind = lambda t: jnp.maximum(t - 1, 0)
+    return kernel_call(
+        partial(forward_kernel, steps, row_blocks, chunk),
+        (steps + 1,),
+        [
+            ((1, rows, hd), lambda t: (ahead(t) // row_blocks, ahead(t) % row_blocks, 0)),
+            ((1, keys, hd), lambda t: (ahead(t) // row_blocks, 0, 0)),
+            ((1, keys, hd), lambda t: (behind(t) // row_blocks, 0, 0)),
+        ],
+        [
+            (
+                (1, 1, rows, keys),
+                lambda t: (behind(t) // row_blocks, behind(t) % row_blocks, 0, 0),
+                (heads, row_blocks, rows, keys),
+                BF16,
+            ),
+            (
+                (rows, hd),
+                lambda t: (behind(t) % row_blocks, behind(t) // row_blocks),
+                (total, heads * hd),
+                F32,
+            ),
+            (
+                (1, rows, hd),
+                lambda t: (behind(t) // row_blocks, behind(t) % row_blocks, 0),
+                (heads, total, hd),
+                F32,
+            ),
+        ],
+        [
+            pltpu.VMEM((rows, keys), F32),
+            pltpu.VMEM((rows, keys), F32),
+            pltpu.VMEM((rows, LANES), F32),
+            pltpu.VMEM((rows, LANES), F32),
+            pltpu.VMEM((keys, 2 * hd), BF16),
+        ],
+        8 * heads * total * keys * hd,
+        2 * heads * total * keys,
+        q,
+        k,
+        v,
+        exps=heads * total * keys,
+    )
+
+
+def gelu_pair(inner):
+    size = jnp.abs(inner) * (0.5**0.5)
+    rate = 1.0 / (1.0 + 0.3275911 * size)
+    bell = jnp.exp(-(size * size))
+    tail = rate * (
+        0.254829592
+        + rate * (-0.284496736 + rate * (1.421413741 + rate * (-1.453152027 + rate * 1.061405429)))
+    )
+    tail = 0.5 * tail * bell
+    below = jnp.where(inner < 0, tail, 1.0 - tail)
+    return inner * below, below + inner * bell * 0.3989422804014327
+
+
+def dense_kernel(
+    x_ref, o_ref, inv_ref, cot_ref, wo, w1, b1, w2, b2, g1, s1, g2, s2,
+    out_ref, first_ref, grad_ref, delta_ref, go_ref, gi_ref, gu_ref, vec_ref,
+):
+    @pl.when(pl.program_id(0) == 0)
+    def _():
+        for ref in (go_ref, gi_ref, gu_ref, vec_ref):
+            ref[...] = jnp.zeros_like(ref)
+
+    width = x_ref.shape[1]
+    attended = o_ref[...]
+    attended_low = attended.astype(BF16)
+    gain_one, gain_two = g1[...].astype(F32), g2[...].astype(F32)
+    first_sum = x_ref[...].astype(F32) + dot(attended_low, wo[...], 1, 0)
+    hidden, normed_one, inverse_one = norm_forward(first_sum, gain_one, s1[...].astype(F32))
+    hidden_low = hidden.astype(BF16)
+    inner = dot(hidden_low, w1[...], 1, 0) + b1[...].astype(F32)
+    activated, slope = gelu_pair(inner)
+    activated = activated.astype(BF16)
+    second_sum = hidden + dot(activated, w2[...], 1, 0) + b2[...].astype(F32)
+    result, normed_two, inverse_two = norm_forward(second_sum, gain_two, s2[...].astype(F32))
+    out_ref[...] = result.astype(BF16)
+    upstream = cot_ref[...].astype(F32)
+    second_grad, gain_two_sum, shift_two_sum = norm_backward(
+        upstream, normed_two, inverse_two, gain_two
+    )
+    outer_grad = second_grad.astype(BF16)
+    gu_ref[...] += dot(activated, outer_grad, 0, 0)
+    inner_grad = (dot(outer_grad, w2[...], 1, 1) * slope).astype(BF16)
+    gi_ref[...] += dot(hidden_low, inner_grad, 0, 0)
+    hidden_grad = second_grad + dot(inner_grad, w1[...], 1, 1)
+    first_grad, gain_one_sum, shift_one_sum = norm_backward(
+        hidden_grad, normed_one, inverse_one, gain_one
+    )
+    first_ref[...] = first_grad
+    branch_grad = first_grad.astype(BF16)
+    go_ref[...] += dot(attended_low, branch_grad, 0, 0)
+    attended_grad = dot(branch_grad, wo[...], 1, 1)
+    for h in range(HEADS):
+        at = slice(h * HD, (h + 1) * HD)
+        scaled = (attended_grad[:, at] * inv_ref[h]).astype(BF16)
+        grad_ref[h] = scaled
+        delta = jnp.sum(scaled.astype(F32) * attended[:, at], axis=-1, keepdims=True)
+        delta_ref[h] = jnp.broadcast_to(delta, delta_ref.shape[1:])
+    inner_sum = jnp.sum(inner_grad.astype(F32), axis=0)
+    sums = (
+        gain_one_sum,
+        shift_one_sum,
+        gain_two_sum,
+        shift_two_sum,
+        jnp.sum(outer_grad.astype(F32), axis=0),
+        inner_sum[:width],
+        inner_sum[width:],
+    )
+    for j, part in enumerate(sums):
+        vec_ref[j : j + 1, :] += part[None, :]
+
+
+def dense(x, attended, inverse, cot, weights, row_blocks):
+    total, width = x.shape
+    rows = total // row_blocks
+    hidden = weights[1].shape[1]
+    block = lambda b: (b, 0)
+    fixed = lambda b: (0, 0)
+    by_head = lambda b: (0, b, 0)
+    whole = lambda *shape: (shape, fixed, shape, F32)
+    return kernel_call(
+        dense_kernel,
+        (row_blocks,),
+        [
+            ((rows, width), block),
+            ((rows, width), block),
+            ((HEADS, rows, HD), by_head),
+            ((rows, width), block),
+        ]
+        + [(w.shape, fixed) for w in weights],
+        [
+            ((rows, width), block, (total, width), BF16),
+            ((rows, width), block, (total, width), F32),
+            ((HEADS, rows, HD), by_head, (HEADS, total, HD), BF16),
+            ((HEADS, rows, HD), by_head, (HEADS, total, HD), F32),
+            whole(width, width),
+            whole(width, hidden),
+            whole(hidden, width),
+            whole(8, width),
+        ],
+        [],
+        6 * total * width * (width + 2 * hidden),
+        20 * total * width + 8 * width * (width + 2 * hidden),
+        x,
+        attended,
+        inverse,
+        cot,
+        *weights,
+    )
+
+
+def backward_kernel(
+    row_blocks, chunks, scale_q, scale_k,
+    q_ref, g_ref, k_ref, v_ref, d_ref, p_ref, dq_ref, dk_ref, dv_ref, ds, dq_sum, q_t, g_t,
+):
+    c = pl.program_id(1)
+    rows, chunk = p_ref.shape[2:]
+
+    @pl.when(c == 0)
+    def _():
+        q_t[...] = q_ref[0].T
+        g_t[...] = g_ref[0].T
+        dq_sum[...] = jnp.zeros_like(dq_sum)
+
+    keys, values = k_ref[0], v_ref[0]
+    dv_t = jnp.zeros((HD, chunk), F32)
+    for i in range(row_blocks):
+        at = slice(i * rows, (i + 1) * rows)
+        soft = p_ref[0, i]
+        soft_grad = dot(g_ref[0, at, :], values, 1, 1)
+        delta = jnp.concatenate([d_ref[0, at, :]] * (chunk // LANES), axis=1)
+        score_grad = (soft.astype(F32) * (soft_grad - delta)).astype(BF16)
+        ds[at, :] = score_grad
+        dq_sum[at, :] += dot(score_grad, keys, 1, 0)
+        dv_t += dot(g_t[:, at], soft, 1, 0)
+    dv_ref[0] = dv_t.T.astype(BF16)
+    dk_t = dot(q_t[...], ds[...], 1, 0)
+    dk_ref[0] = (dk_t.T * scale_k).astype(BF16)
+
+    @pl.when(c == chunks - 1)
+    def _():
+        dq_ref[0] = (dq_sum[...] * scale_q).astype(BF16)
+
+
+def attention_backward(q, g, k, v, delta, p, scale_q, scale_k, chunk=1024):
+    heads, total, hd = q.shape
+    keys = k.shape[1]
+    row_blocks, rows = p.shape[1:3]
+    chunks = keys // chunk
+    head = lambda h, c: (h, 0, 0)
+    key = lambda h, c: (h, c, 0)
+    key_out = ((1, chunk, hd), key, (heads, keys, hd), BF16)
+    return kernel_call(
+        partial(backward_kernel, row_blocks, chunks, scale_q, scale_k),
+        (heads, chunks),
+        [
+            ((1, total, hd), head),
+            ((1, total, hd), head),
+            ((1, chunk, hd), key),
+            ((1, chunk, hd), key),
+            ((1, total, hd), head),
+            ((1, row_blocks, rows, chunk), lambda h, c: (h, 0, 0, c)),
+        ],
+        [((1, total, hd), head, (heads, total, hd), BF16), key_out, key_out],
+        [
+            pltpu.VMEM((total, chunk), BF16),
+            pltpu.VMEM((total, hd), F32),
+            pltpu.VMEM((hd, total), BF16),
+            pltpu.VMEM((hd, total), BF16),
+        ],
+        12 * heads * total * keys * hd,
+        2 * heads * total * keys,
+        q,
+        g,
+        k,
+        v,
+        delta,
+        p,
+    )
+
+
+def finish_kernel(
+    context, x_ref, first_ref, dq_ref, dk_own, dk_other, dv_own, dv_other, wq, wk, wv,
+    token_ref, late_ref,
+):
+    width = x_ref.shape[2]
+
+    @pl.when(pl.program_id(0) == 0)
+    def _():
+        late_ref[...] = jnp.zeros_like(late_ref)
+
+    def joined(ref, other=None):
+        parts = [ref[h, 0] if other is None else ref[h, 0, 0] for h in range(HEADS)]
+        if other is not None:
+            parts = [
+                (part.astype(F32) + other[h, 0].astype(F32)).astype(BF16)
+                for h, part in enumerate(parts)
+            ]
+        return jnp.concatenate(parts, axis=1)
+
+    rows = x_ref[0]
+    above = rows[:context]
+    query_grad = joined(dq_ref)
+    key_grad = joined(dk_own, dk_other)
+    value_grad = joined(dv_own, dv_other)
+    base = first_ref[0] + dot(query_grad, wq[...], 1, 1)
+    back = dot(key_grad, wk[...], 1, 1) + dot(value_grad, wv[...], 1, 1)
+    token_ref[0, :context] = (base[:context] + back).astype(BF16)
+    token_ref[0, context:] = base[context:].astype(BF16)
+    late_ref[:width] += dot(rows, query_grad, 0, 0)
+    late_ref[width : 2 * width] += dot(above, key_grad, 0, 0)
+    late_ref[2 * width :] += dot(above, value_grad, 0, 0)
+
+
+def finish(x, first_grad, dq, dk, dk_other, dv, dv_other, wq, wk, wv):
+    blocks, rows, width = x.shape
+    context = dk.shape[1] // (2 * blocks)
+    block = lambda b: (b, 0, 0)
+    fixed = lambda b: (0, 0)
+    sided = (HEADS, 2 * blocks, context, HD)
+    own = ((HEADS, 1, 1, context, HD), lambda b: (0, 0, b, 0, 0))
+    other = ((HEADS, 1, context, HD), lambda b: (0, b, 0, 0))
+    both = lambda array: array.reshape(HEADS, 2, blocks, context, HD)
+    return kernel_call(
+        partial(finish_kernel, context),
+        (blocks,),
+        [
+            ((1, rows, width), block),
+            ((1, rows, width), block),
+            ((HEADS, 1, rows, HD), lambda b: (0, b, 0, 0)),
+            own,
+            other,
+            own,
+            other,
+        ]
+        + [((width, width), fixed)] * 3,
+        [
+            ((1, rows, width), block, (blocks, rows, width), BF16),
+            ((3 * width, width), fixed, (3 * width, width), F32),
+        ],
+        [],
+        4 * blocks * width * width * (rows + 2 * context),
+        8 * blocks * width * (rows + 2 * context),
+        x,
+        first_grad.reshape(blocks, rows, width),
+        dq.reshape(HEADS, blocks, rows, HD),
+        both(dk),
+        dk_other,
+        both(dv),
+        dv_other,
+        wq,
+        wk,
+        wv,
+    )
+
+
+def sum_over_all(part, groups, members, name):
+    grp, ctx = lax.axis_index("grp"), lax.axis_index("ctx")
+
+    def partner(flip_grp, flip_ctx):
+        return [
+            (g * members + c, (g ^ flip_grp) * members + (c ^ flip_ctx))
+            for g in range(groups)
+            for c in range(members)
+        ]
+
+    ways = [(1, 0)]
+    ways += [(1 << b, 0) for b in range(1, groups.bit_length() - 1)]
+    ways += [(0, 1 << b) for b in range(members.bit_length() - 1)]
+    bits = [
+        lax.rem((grp if flip_grp else ctx) // max(flip_grp, flip_ctx), 2)
+        for flip_grp, flip_ctx in ways
+    ]
+    for way, bit in zip(ways, bits, strict=True):
+        half = part.shape[0] // 2
+        sent = lax.dynamic_slice_in_dim(part, (1 - bit) * half, half).astype(BF16)
+        kept = lax.dynamic_slice_in_dim(part, bit * half, half)
+        part = kept + lax.ppermute(sent, AXES, partner(*way)).astype(F32)
+    part = part.astype(BF16)
+    for way, bit in reversed(list(zip(ways, bits, strict=True))):
+        came = lax.ppermute(part, AXES, partner(*way))
+        part = jnp.where(
+            bit == 0, jnp.concatenate([part, came]), jnp.concatenate([came, part])
+        )
+    return part.astype(F32)
+
+
+def gathered_plan(
+    tokens,
+    query_counts,
+    cotangent,
+    query_weight,
+    key_weight,
+    value_weight,
+    output_weight,
+    inner_weight,
+    inner_bias,
+    outer_weight,
+    outer_bias,
+    first_gain,
+    first_shift,
+    second_gain,
+    second_shift,
+):
+    blocks, rows, width = tokens.shape
+    groups, members = lax.axis_size("grp"), lax.axis_size("ctx")
+    member = lax.axis_index("ctx")
+    place = member // 2
+    context = CTX // members
+    slots = QUERIES // members
+
+    def route(r, back=False):
+        pairs = []
+        for g in range(groups):
+            for c in range(members):
+                to = (g - g % 2 + c % 2) * members + ((c // 2 + r) % blocks) * 2 + g % 2
+                pairs.append((to, g * members + c) if back else (g * members + c, to))
+        return pairs
+
+    across = [
+        (g * members + c, (g ^ 1) * members + c) for g in range(groups) for c in range(members)
+    ]
+
+    def outward(array):
+        return [
+            lax.ppermute(
+                lax.dynamic_index_in_dim(array, lax.rem(place + r, blocks), 0, keepdims=False),
+                AXES,
+                route(r),
+            )
+            for r in range(blocks)
+        ]
+
+    def homeward(array):
+        came = [lax.ppermute(array[r], AXES, route(r, True)) for r in range(blocks)]
+        twice = jnp.stack(came + came)
+        return lax.dynamic_slice_in_dim(twice, blocks - place, blocks)
+
+    slot = member * slots + jnp.arange(rows, dtype=jnp.int32) - context
+    live = (jnp.arange(rows) < context)[None, :] | (slot[None, :] < query_counts[:, None])
+    live = live[:, :, None]
+
+    own = outward(tokens)
+    other = jnp.stack([lax.ppermute(block[:context], AXES, across) for block in own])
+    own = jnp.stack(own)
+    masked, own, other = lax.optimization_barrier(
+        (jnp.where(live, cotangent, 0).astype(BF16), own, other)
+    )
+    cot = jnp.stack(outward(masked)).reshape(blocks * rows, width)
+
+    scale = HD**-0.5
+    log2e = 1.4426950408889634
+    q, k, v = project(own, other, query_weight, key_weight, value_weight, scale * log2e)
+    p, attended, inverse = attention_forward(q, k, v, blocks)
+    lifted = lambda vector: vector.reshape(1, -1)
+    weights = (
+        output_weight,
+        inner_weight,
+        lifted(inner_bias),
+        outer_weight,
+        lifted(outer_bias),
+        lifted(first_gain),
+        lifted(first_shift),
+        lifted(second_gain),
+        lifted(second_shift),
+    )
+    out, first_grad, grads, delta, grad_output, grad_inner, grad_outer, vectors = dense(
+        own.reshape(blocks * rows, width), attended, inverse, cot, weights, blocks
+    )
+    layer_out = homeward(out.reshape(blocks, rows, width))
+    layer_out = jnp.where(live, layer_out, 0).astype(BF16)
+    early = jnp.concatenate(
+        [
+            grad_output,
+            grad_inner[:, :width],
+            grad_inner[:, width:],
+            grad_outer,
+            vectors,
+            jnp.zeros((504, width), F32),
+        ]
+    )
+    early = sum_over_all(early, groups, members, "early")
+
+    dq, dk, dv = attention_backward(q, grads, k, v, delta, p, scale, 1.0 / log2e)
+    half = blocks * context
+    dk_other = lax.ppermute(dk[:, half:], AXES, across).reshape(HEADS, blocks, context, HD)
+    dv_other = lax.ppermute(dv[:, half:], AXES, across).reshape(HEADS, blocks, context, HD)
+    token_grad, late = finish(
+        own, first_grad, dq, dk, dk_other, dv, dv_other, query_weight, key_weight, value_weight
+    )
+    grad_tokens = homeward(token_grad).astype(F32)
+    late = sum_over_all(late, groups, members, "late")
+
+    vectors = early[5 * width :]
+    return (
+        layer_out,
+        grad_tokens,
+        late[:width],
+        late[width : 2 * width],
+        late[2 * width :],
+        early[:width],
+        jnp.concatenate([early[width : 2 * width], early[2 * width : 3 * width]], axis=1),
+        jnp.concatenate([vectors[5], vectors[6]]),
+        early[3 * width : 5 * width],
+        vectors[4],
+        vectors[0],
+        vectors[1],
+        vectors[2],
+        vectors[3],
+    )
+
+
 def solution(mesh):
     return jax.shard_map(
-        on_device,
+        gathered_plan if one_chip_each(mesh) else spread_plan,
         mesh=mesh,
         in_specs=(
             P("grp", "ctx", None),

time: 1980 us -> 418 us (0.21)
  waiting for transfers between devices: 1210 us -> 121 us
  matrix products: 423 us -> 0 us
  Pallas kernels: 0 us -> 183 us
  other arithmetic: 181 us -> 18.6 us
  local copies, waits for them, and re-layouts: 109 us -> 30.1 us
  starting transfers between devices: 0.21 us -> 59.8 us
  blocking collectives: 41.3 us -> 0 us
    reduce_scatter x2 -> x0, waiting for transfers between devices: 751 us -> none  [the longest x1 540 us: attend_back(): lax.psum_scatter(key_part.reshape(NBLK, -1, width), 'ctx', scatter_dimens...]
    dot_general x24 -> x0, matrix products: 423 us -> none  [the longest x1 96.6 us: attend_back(): jnp.einsum('nrhd,nkhd->nhrk', grad_heads, value_heads, preferred_element_...]
    all_gather x2 -> x0, waiting for transfers between devices: 334 us -> none  [the longest x1 204 us: fetch(): lax.all_gather(keys_mine, 'ctx', axis=1, tiled=True)]
    pallas_call x0 -> x5, Pallas kernels: none -> 183 us  [kernel_call(): pl.pallas_call(body, grid=grid, in_specs=[pl.BlockSpec(shape, index) for...]
    psum x1 -> x0, waiting for transfers between devices: 125 us -> none  [on_device(): lax.psum((grad_query, grad_key, grad_value, grad_output, grad_inner, grad...]
    ppermute x0 -> x42, waiting for transfers between devices: none -> 121 us  [the longest x10 43.6 us: sum_over_all(): part = kept + lax.ppermute(sent, AXES, partner(*way)).astype(F32)]
    convert_element_type x10 -> x5, other arithmetic: 117 us -> 4.09 us  [the longest x1 2.67 us: gathered_plan(): grad_tokens = homeward(token_grad).astype(F32)]
    reshape x4 -> x6, local copies, waits for them, and re-layouts: 71.6 us -> 3.5 us  [gathered_plan(): lifted = lambda vector: vector.reshape(1, -1)]
  transfers between devices with their start and end apart: 5 -> 42, of which waited for: 5 -> 14; matrix products, arithmetic and copies ran while one was open for 24% -> 6% of each run, Pallas kernels for 0% -> 35%
where the time goes in v1:
time: 418 us; the launch traced here: 414 us
  Pallas kernels  183 us (44%)
  waiting for transfers between devices  121 us (29%)
  starting transfers between devices  59.8 us (14%)
  local copies, waits for them, and re-layouts  30.1 us (7%)
  other arithmetic  18.6 us (4%)
    pallas_call x5, Pallas kernels, kernel_call(): pl.pallas_call(body, grid=grid, in_specs=[pl.BlockSpec(shape, index) for...  183 us
    ppermute x10, waiting for transfers between devices, sum_over_all(): part = kept + lax.ppermute(sent, AXES, partner(*way)).astype(F32)  43.6 us
    ppermute x10, waiting for transfers between devices, sum_over_all(): came = lax.ppermute(part, AXES, partner(*way))  41.2 us
    ppermute x8, waiting for transfers between devices, outward(): lax.ppermute(lax.dynamic_index_in_dim(array, lax.rem(place + r, blocks),...  36.1 us
    ppermute x8, starting transfers between devices, outward(): lax.ppermute(lax.dynamic_index_in_dim(array, lax.rem(place + r, blocks),...  18.3 us
    ppermute x10, starting transfers between devices, sum_over_all(): part = kept + lax.ppermute(sent, AXES, partner(*way)).astype(F32)  16.1 us
    ppermute x8, starting transfers between devices, homeward(): came = [lax.ppermute(array[r], AXES, route(r, True)) for r in range(blocks)]  12.3 us
  transfers between devices with their start and end apart: 42, of which 14 were waited for; matrix products, arithmetic and copies ran while one was open for 6% of the time, Pallas kernels for 35%

profile of v1, /device:TPU:0, one launch (start us, length us, event | category | flops | bytes accessed | tf_op | source)
XLA Modules:
  0.0 414.2 jit_solution(6793810289983652020)
XLA Ops:
  0.8 2.9 dynamic-slice_bitcast_fusion.7
  3.7 5.0 %collective-permute-start.3 = (bf16[528,512]{1,0:T(8,128)(2,1)}, bf16[528,512]{1,0:T(8,128)(2,1)S(1)}, u32[]{:S(2)}, u32[]{:S(2)}) collective-permute-start(bf16[528,512]{1,0:T(8,128)(2,1)} %get-tuple-element.85), channel_id=1, source_target_pairs={{0,6},{1,14},{2,0},{3,8},{4,2},{5,10},{6,4},{7,12},{8,7},{9,15},{1... | collective-permute-start | bytes 1622024 | tf_op jit(solution)/shard_map/ppermute | solution.py:769
  9.8 5.8 %collective-permute-start = (bf16[528,512]{1,0:T(8,128)(2,1)}, bf16[528,512]{1,0:T(8,128)(2,1)}, u32[]{:S(2)}, u32[]{:S(2)}) collective-permute-start(bf16[528,512]{1,0:T(8,128)(2,1)} %get-tuple-element.83), channel_id=1, source_target_pairs={{0,0},{1,8},{2,2},{3,10},{4,4},{5,12},{6,6},{7,14},{8,1},{9,9},{10... | collective-permute-start | bytes 1622024 | tf_op jit(solution)/shard_map/ppermute | solution.py:769
  22.3 33.7 %collective-permute-done.2 = bf16[528,512]{1,0:T(8,128)(2,1)S(1)} collective-permute-done((bf16[528,512]{1,0:T(8,128)(2,1)}, bf16[528,512]{1,0:T(8,128)(2,1)S(1)}, u32[]{:S(2)}, u32[]{:S(2)}) %collective-permute-start.2) | collective-permute-done | bytes 540704 | tf_op jit(solution)/shard_map/ppermute | solution.py:769
  59.5 2.8 pad_maximum_fusion.own.x_ref
  64.9 3.3 collective-permute-start.10
  71.4 9.9 %shard_map.254 = (bf16[4,2112,128]{2,1,0:T(8,128)(2,1)}, bf16[4,2,4,512,128]{4,3,2,1,0:T(8,128)(2,1)}, bf16[4,2,4,512,128]{4,3,2,1,0:T(8,128)(2,1)}) custom-call(bf16[4,528,512]{2,1,0:T(8,128)(2,1)} %pad_maximum_fusion.own.x_ref, bf16[4,512,512]{2,1,0:T(8,128)(2,1)} %pad_maximum_fusion.2.other, bf16[512,512]{1,0:T(8,128)(2,1)} %wq.3, bf16[512,512]{1,0:T(8,128)(2,1)} %wk.3, ...), custom_call_target="tpu_custom_call" | custom-call | flops 5402263552 | bytes 16908288 | tf_op jit(solution)/shard_map/pallas_call | solution.py:285
  81.4 52.0 %shard_map.255 = (bf16[4,4,528,4096]{3,2,1,0:T(8,128)(2,1)}, f32[2112,512]{1,0:T(8,128)}, f32[4,2112,128]{2,1,0:T(8,128)}) custom-call(bf16[4,2112,128]{2,1,0:T(8,128)(2,1)} %get-tuple-element.38.q_ref, bf16[4,4096,128]{2,1,0:T(8,128)(2,1)} %bitcast.101, bf16[4,4096,128]{2,1,0:T(8,128)(2,1)} %bitcast.103), custom_call_target="tpu_custom_call" | custom-call | flops 35433480192 | bytes 69206016 | tf_op jit(solution)/shard_map/pallas_call | solution.py:285
  135.0 38.0 %shard_map.256 = (bf16[2112,512]{1,0:T(8,128)(2,1)}, f32[2112,512]{1,0:T(8,128)}, bf16[4,2112,128]{2,1,0:T(8,128)(2,1)}, f32[4,2112,128]{2,1,0:T(8,128)}, f32[51...) custom-call(bf16[2112,512]{1,0:T(8,128)(2,1)} %bitcast.77, ...), custom_call_target="tpu_custom_call" | custom-call | flops 16609443840 | bytes 32112640 | tf_op jit(solution)/shard_map/pallas_call | solution.py:285
  179.6 70.2 %shard_map.257 = (bf16[4,2112,128]{2,1,0:T(8,128)(2,1)}, bf16[4,4096,128]{2,1,0:T(8,128)(2,1)}, bf16[4,4096,128]{2,1,0:T(8,128)(2,1)}) custom-call(bf16[4,2112,128]{2,1,0:T(8,128)(2,1)} %get-tuple-element.38.q_ref, bf16[4,2112,128]{2,1,0:T(8,128)(2,1)} %get-tuple-element.46.g_ref, bf16[4,4096,128]{2,1,0:T(8,128)(2,1)} %bitcast.102, ...), custom_call_target="tpu_custom_call" | custom-call | flops 53150220288 | bytes 69206016 | tf_op jit(solution)/shard_map/pallas_call | solution.py:285
  251.8 5.2 %collective-permute-start.16 = (bf16[4,2048,128]{2,1,0:T(8,128)(2,1)S(1)}, bf16[4,2048,128]{2,1,0:T(8,128)(2,1)S(1)}, u32[]{:S(2)}, u32[]{:S(2)}) collective-permute-start(bf16[4,2048,128]{2,1,0:T(8,128)(2,1)S(1)} %slice.110), channel_id=1, source_target_pairs={{0,8},{1,9},{2,10},{3,11},{4,12},{5,13},{6,14},{7,15},{8,0},{9,1},... | collective-permute-start | bytes 6291464 | tf_op jit(solution)/shard_map/ppermute | solution.py:829
  271.0 12.9 %shard_map.258 = (bf16[4,528,512]{2,1,0:T(8,128)(2,1)}, f32[1536,512]{1,0:T(8,128)}) custom-call(bf16[4,528,512]{2,1,0:T(8,128)(2,1)} %pad_maximum_fusion.own.x_ref, f32[4,528,512]{2,1,0:T(8,128)} %bitcast.100, bf16[4,4,528,128]{3,2,1,0:T(8,128)(2,1)} %bitcast.105, bf16[4,2,4,512,128]{4,3,2,1,0:T(8,128)(2,1)} %bitcast.81, bf16[4,4,512,128]{3,2,1,0:T(8,128)(2,1)} %bitcast.98, ...), custom_call_target="tpu_custom_call" | custom-call | flops 6509559808 | bytes 25427968 | tf_op jit(solution)/shard_map/pallas_call | solution.py:285
  291.4 3.1 collective-permute-start.19
  295.3 4.1 collective-permute-done.34
  299.4 3.5 collective-permute-start.21
  307.1 26.0 %collective-permute-done.35 = bf16[192,512]{1,0:T(8,128)(2,1)S(1)} collective-permute-done((bf16[192,512]{1,0:T(8,128)(2,1)S(1)}, bf16[192,512]{1,0:T(8,128)(2,1)S(1)}, u32[]{:S(2)}, u32[]{:S(2)}) %collective-permute-start.35) | collective-permute-done | bytes 196640 | tf_op jit(solution)/shard_map/ppermute | solution.py:721
  333.1 3.9 collective-permute-start.36
  337.2 8.3 %collective-permute-done.36 = bf16[96,512]{1,0:T(8,128)(2,1)S(1)} collective-permute-done((bf16[96,512]{1,0:T(8,128)(2,1)S(1)}, bf16[96,512]{1,0:T(8,128)(2,1)S(1)}, u32[]{:S(2)}, u32[]{:S(2)}) %collective-permute-start.36) | collective-permute-done | bytes 98336 | tf_op jit(solution)/shard_map/ppermute | solution.py:721
  348.1 3.1 collective-permute-start.25
  357.1 5.0 %collective-permute-done.38 = bf16[192,512]{1,0:T(8,128)(2,1)S(1)} collective-permute-done((bf16[192,512]{1,0:T(8,128)(2,1)S(1)}, bf16[192,512]{1,0:T(8,128)(2,1)S(1)}, u32[]{:S(2)}, u32[]{:S(2)}) %collective-permute-start.38) | collective-permute-done | bytes 196640 | tf_op jit(solution)/shard_map/ppermute | solution.py:724
  363.5 4.1 collective-permute-done.27
  367.7 5.7 %collective-permute-done.39 = bf16[384,512]{1,0:T(8,128)(2,1)S(1)} collective-permute-done((bf16[384,512]{1,0:T(8,128)(2,1)S(1)}, bf16[384,512]{1,0:T(8,128)(2,1)S(1)}, u32[]{:S(2)}, u32[]{:S(2)}) %collective-permute-start.39) | collective-permute-done | bytes 393248 | tf_op jit(solution)/shard_map/ppermute | solution.py:724
  375.9 5.5 %collective-permute-done.29 = bf16[192,512]{1,0:T(8,128)(2,1)S(1)} collective-permute-done((bf16[192,512]{1,0:T(8,128)(2,1)S(1)}, bf16[192,512]{1,0:T(8,128)(2,1)S(1)}, u32[]{:S(2)}, u32[]{:S(2)}) %collective-permute-start.29) | collective-permute-done | bytes 196640 | tf_op jit(solution)/shard_map/ppermute | solution.py:724
  382.0 18.9 %collective-permute-done.30 = bf16[384,512]{1,0:T(8,128)(2,1)S(1)} collective-permute-done((bf16[384,512]{1,0:T(8,128)(2,1)S(1)}, bf16[384,512]{1,0:T(8,128)(2,1)S(1)}, u32[]{:S(2)}, u32[]{:S(2)}) %collective-permute-start.30) | collective-permute-done | bytes 393248 | tf_op jit(solution)/shard_map/ppermute | solution.py:724
  (186 shorter events, 79.5 us)
Async XLA Ops:
  3.7 17.9 %collective-permute-start.3 = (bf16[528,512]{1,0:T(8,128)(2,1)}, bf16[528,512]{1,0:T(8,128)(2,1)S(1)}, u32[]{:S(2)}, u32[]{:S(2)}) collective-permute-start(bf16[528,512]{1,0:T(8,128)(2,1)} %get-tuple-element.85), channel_id=1, source_target_pairs={{0,6},{1,14},{2,0},{3,8},{4,2},{5,10},{6,4},{7,12},{8,7},{9,15},{1... | collective-permute-start | bytes 1622024 | tf_op jit(solution)/shard_map/ppermute | solution.py:769
  8.8 47.3 %collective-permute-start.2 = (bf16[528,512]{1,0:T(8,128)(2,1)}, bf16[528,512]{1,0:T(8,128)(2,1)S(1)}, u32[]{:S(2)}, u32[]{:S(2)}) collective-permute-start(bf16[528,512]{1,0:T(8,128)(2,1)} %get-tuple-element.86), channel_id=1, source_target_pairs={{0,4},{1,12},{2,6},{3,14},{4,0},{5,8},{6,2},{7,10},{8,5},{9,13},{1... | collective-permute-start | bytes 1622024 | tf_op jit(solution)/shard_map/ppermute | solution.py:769
  8.8 47.4 %collective-permute-start.1 = (bf16[528,512]{1,0:T(8,128)(2,1)}, bf16[528,512]{1,0:T(8,128)(2,1)}, u32[]{:S(2)}, u32[]{:S(2)}) collective-permute-start(bf16[528,512]{1,0:T(8,128)(2,1)} %get-tuple-element.84), channel_id=1, source_target_pairs={{0,2},{1,10},{2,4},{3,12},{4,6},{5,14},{6,0},{7,8},{8,3},{9,11},{1... | collective-permute-start | bytes 1622024 | tf_op jit(solution)/shard_map/ppermute | solution.py:769
  9.8 48.0 %collective-permute-start = (bf16[528,512]{1,0:T(8,128)(2,1)}, bf16[528,512]{1,0:T(8,128)(2,1)}, u32[]{:S(2)}, u32[]{:S(2)}) collective-permute-start(bf16[528,512]{1,0:T(8,128)(2,1)} %get-tuple-element.83), channel_id=1, source_target_pairs={{0,0},{1,8},{2,2},{3,10},{4,4},{5,12},{6,6},{7,14},{8,1},{9,9},{10... | collective-permute-start | bytes 1622024 | tf_op jit(solution)/shard_map/ppermute | solution.py:769
  21.6 40.8 %collective-permute-start.7 = (bf16[512,512]{1,0:T(8,128)(2,1)S(1)}, bf16[512,512]{1,0:T(8,128)(2,1)S(1)}, u32[]{:S(2)}, u32[]{:S(2)}) collective-permute-start(bf16[512,512]{1,0:T(8,128)(2,1)S(1)} %slice.135), channel_id=1, source_target_pairs={{0,8},{1,9},{2,10},{3,11},{4,12},{5,13},{6,14},{7,15},{8,0},{9,1},... | collective-permute-start | bytes 1572872 | tf_op jit(solution)/shard_map/ppermute | solution.py:787
  64.9 68.5 %collective-permute-start.11 = (bf16[528,512]{1,0:T(8,128)(2,1)}, bf16[528,512]{1,0:T(8,128)(2,1)S(1)}, u32[]{:S(2)}, u32[]{:S(2)}) collective-permute-start(bf16[528,512]{1,0:T(8,128)(2,1)} %get-tuple-element.80), channel_id=1, source_target_pairs={{0,6},{1,14},{2,0},{3,8},{4,2},{5,10},{6,4},{7,12},{8,7},{9,15},{1... | collective-permute-start | bytes 1622024 | tf_op jit(solution)/shard_map/ppermute | solution.py:769
  64.9 68.5 %collective-permute-start.10 = (bf16[528,512]{1,0:T(8,128)(2,1)S(1)}, bf16[528,512]{1,0:T(8,128)(2,1)S(1)}, u32[]{:S(2)}, u32[]{:S(2)}) collective-permute-start(bf16[528,512]{1,0:T(8,128)(2,1)S(1)} %get-tuple-element.81), channel_id=1, source_target_pairs={{0,4},{1,12},{2,6},{3,14},{4,0},{5,8},{6,2},{7,10},{8,5},{9,13},{1... | collective-permute-start | bytes 1622024 | tf_op jit(solution)/shard_map/ppermute | solution.py:769
  68.2 65.2 %collective-permute-start.9 = (bf16[528,512]{1,0:T(8,128)(2,1)S(1)}, bf16[528,512]{1,0:T(8,128)(2,1)S(1)}, u32[]{:S(2)}, u32[]{:S(2)}) collective-permute-start(bf16[528,512]{1,0:T(8,128)(2,1)S(1)} %get-tuple-element.82), channel_id=1, source_target_pairs={{0,2},{1,10},{2,4},{3,12},{4,6},{5,14},{6,0},{7,8},{8,3},{9,11},{1... | collective-permute-start | bytes 1622024 | tf_op jit(solution)/shard_map/ppermute | solution.py:769
  70.2 63.2 %collective-permute-start.8 = (bf16[528,512]{1,0:T(8,128)(2,1)S(1)}, bf16[528,512]{1,0:T(8,128)(2,1)S(1)}, u32[]{:S(2)}, u32[]{:S(2)}) collective-permute-start(bf16[528,512]{1,0:T(8,128)(2,1)S(1)} %get-tuple-element.79), channel_id=1, source_target_pairs={{0,0},{1,8},{2,2},{3,10},{4,4},{5,12},{6,6},{7,14},{8,1},{9,9},{10... | collective-permute-start | bytes 1622024 | tf_op jit(solution)/shard_map/ppermute | solution.py:769
  175.6 85.5 %collective-permute-start.12 = (bf16[528,512]{1,0:T(8,128)(2,1)}, bf16[528,512]{1,0:T(8,128)(2,1)S(1)}, u32[]{:S(2)}, u32[]{:S(2)}) collective-permute-start(bf16[528,512]{1,0:T(8,128)(2,1)} %get-tuple-element.78), channel_id=1, source_target_pairs={{0,0},{8,1},{2,2},{10,3},{4,4},{12,5},{6,6},{14,7},{1,8},{9,9},{3,... | collective-permute-start | bytes 1622024 | tf_op jit(solution)/shard_map/ppermute | solution.py:778
  177.3 84.0 %collective-permute-start.13 = (bf16[528,512]{1,0:T(8,128)(2,1)S(1)}, bf16[528,512]{1,0:T(8,128)(2,1)S(1)}, u32[]{:S(2)}, u32[]{:S(2)}) collective-permute-start(bf16[528,512]{1,0:T(8,128)(2,1)S(1)} %get-tuple-element.77), channel_id=1, source_target_pairs={{2,0},{10,1},{4,2},{12,3},{6,4},{14,5},{0,6},{8,7},{3,8},{11,9},{5... | collective-permute-start | bytes 1622024 | tf_op jit(solution)/shard_map/ppermute | solution.py:778
  179.1 82.7 %collective-permute-start.14 = (bf16[528,512]{1,0:T(8,128)(2,1)S(1)}, bf16[528,512]{1,0:T(8,128)(2,1)S(1)}, u32[]{:S(2)}, u32[]{:S(2)}) collective-permute-start(bf16[528,512]{1,0:T(8,128)(2,1)S(1)} %get-tuple-element.76), channel_id=1, source_target_pairs={{4,0},{12,1},{6,2},{14,3},{0,4},{8,5},{2,6},{10,7},{5,8},{13,9},{7... | collective-permute-start | bytes 1622024 | tf_op jit(solution)/shard_map/ppermute | solution.py:778
  179.1 82.7 %collective-permute-start.15 = (bf16[528,512]{1,0:T(8,128)(2,1)S(1)}, bf16[528,512]{1,0:T(8,128)(2,1)S(1)}, u32[]{:S(2)}, u32[]{:S(2)}) collective-permute-start(bf16[528,512]{1,0:T(8,128)(2,1)S(1)} %get-tuple-element.75), channel_id=1, source_target_pairs={{6,0},{14,1},{0,2},{8,3},{2,4},{10,5},{4,6},{12,7},{7,8},{15,9},{1... | collective-permute-start | bytes 1622024 | tf_op jit(solution)/shard_map/ppermute | solution.py:778
  251.8 15.8 %collective-permute-start.16 = (bf16[4,2048,128]{2,1,0:T(8,128)(2,1)S(1)}, bf16[4,2048,128]{2,1,0:T(8,128)(2,1)S(1)}, u32[]{:S(2)}, u32[]{:S(2)}) collective-permute-start(bf16[4,2048,128]{2,1,0:T(8,128)(2,1)S(1)} %slice.110), channel_id=1, source_target_pairs={{0,8},{1,9},{2,10},{3,11},{4,12},{5,13},{6,14},{7,15},{8,0},{9,1},... | collective-permute-start | bytes 6291464 | tf_op jit(solution)/shard_map/ppermute | solution.py:829
  266.0 19.9 %collective-permute-start.33 = (bf16[768,512]{1,0:T(8,128)(2,1)}, bf16[768,512]{1,0:T(8,128)(2,1)}, u32[]{:S(2)}, u32[]{:S(2)}) collective-permute-start(bf16[768,512]{1,0:T(8,128)(2,1)} %dynamic-slice_convert_fusion.2), channel_id=1, source_target_pairs={{0,16},{1,17},{2,18},{3,19},{4,20},{5,21},{6,22},{7,23},{8,24},{9,... | collective-permute-start | bytes 2359304 | tf_op jit(solution)/shard_map/ppermute | solution.py:721
  285.5 17.6 %collective-permute-start.22 = (bf16[768,512]{1,0:T(8,128)(2,1)S(1)}, bf16[768,512]{1,0:T(8,128)(2,1)S(1)}, u32[]{:S(2)}, u32[]{:S(2)}) collective-permute-start(bf16[768,512]{1,0:T(8,128)(2,1)S(1)} %dynamic-slice_convert_fusion.3), channel_id=1, source_target_pairs={{0,8},{1,9},{2,10},{3,11},{4,12},{5,13},{6,14},{7,15},{8,0},{9,1},... | collective-permute-start | bytes 2359304 | tf_op jit(solution)/shard_map/ppermute | solution.py:721
  290.6 14.3 %collective-permute-start.18 = (bf16[528,512]{1,0:T(8,128)(2,1)S(1)}, bf16[528,512]{1,0:T(8,128)(2,1)S(1)}, u32[]{:S(2)}, u32[]{:S(2)}) collective-permute-start(bf16[528,512]{1,0:T(8,128)(2,1)S(1)} %get-tuple-element.74), channel_id=1, source_target_pairs={{0,0},{8,1},{2,2},{10,3},{4,4},{12,5},{6,6},{14,7},{1,8},{9,9},{3,... | collective-permute-start | bytes 1622024 | tf_op jit(solution)/shard_map/ppermute | solution.py:778
  291.4 72.1 %collective-permute-start.19 = (bf16[528,512]{1,0:T(8,128)(2,1)S(1)}, bf16[528,512]{1,0:T(8,128)(2,1)S(1)}, u32[]{:S(2)}, u32[]{:S(2)}) collective-permute-start(bf16[528,512]{1,0:T(8,128)(2,1)S(1)} %get-tuple-element.73), channel_id=1, source_target_pairs={{2,0},{10,1},{4,2},{12,3},{6,4},{14,5},{0,6},{8,7},{3,8},{11,9},{5... | collective-permute-start | bytes 1622024 | tf_op jit(solution)/shard_map/ppermute | solution.py:778
  294.5 81.4 %collective-permute-start.20 = (bf16[528,512]{1,0:T(8,128)(2,1)S(1)}, bf16[528,512]{1,0:T(8,128)(2,1)S(1)}, u32[]{:S(2)}, u32[]{:S(2)}) collective-permute-start(bf16[528,512]{1,0:T(8,128)(2,1)S(1)} %get-tuple-element.72), channel_id=1, source_target_pairs={{4,0},{12,1},{6,2},{14,3},{0,4},{8,5},{2,6},{10,7},{5,8},{13,9},{7... | collective-permute-start | bytes 1622024 | tf_op jit(solution)/shard_map/ppermute | solution.py:778
  299.4 82.5 %collective-permute-start.21 = (bf16[528,512]{1,0:T(8,128)(2,1)S(1)}, bf16[528,512]{1,0:T(8,128)(2,1)S(1)}, u32[]{:S(2)}, u32[]{:S(2)}) collective-permute-start(bf16[528,512]{1,0:T(8,128)(2,1)S(1)} %get-tuple-element.71), channel_id=1, source_target_pairs={{6,0},{14,1},{0,2},{8,3},{2,4},{10,5},{4,6},{12,7},{7,8},{15,9},{1... | collective-permute-start | bytes 1622024 | tf_op jit(solution)/shard_map/ppermute | solution.py:778
  303.1 29.9 %collective-permute-start.35 = (bf16[192,512]{1,0:T(8,128)(2,1)S(1)}, bf16[192,512]{1,0:T(8,128)(2,1)S(1)}, u32[]{:S(2)}, u32[]{:S(2)}) collective-permute-start(bf16[192,512]{1,0:T(8,128)(2,1)S(1)} %dynamic-slice_convert_fusion.6), channel_id=1, source_target_pairs={{0,2},{1,3},{2,0},{3,1},{4,6},{5,7},{6,4},{7,5},{8,10},{9,11},{10,... | collective-permute-start | bytes 589832 | tf_op jit(solution)/shard_map/ppermute | solution.py:721
  304.9 32.1 %collective-permute-start.23 = (bf16[384,512]{1,0:T(8,128)(2,1)S(1)}, bf16[384,512]{1,0:T(8,128)(2,1)S(1)}, u32[]{:S(2)}, u32[]{:S(2)}) collective-permute-start(bf16[384,512]{1,0:T(8,128)(2,1)S(1)} %dynamic-slice_convert_fusion.5), channel_id=1, source_target_pairs={{0,16},{1,17},{2,18},{3,19},{4,20},{5,21},{6,22},{7,23},{8,24},{9,... | collective-permute-start | bytes 1179656 | tf_op jit(solution)/shard_map/ppermute | solution.py:721
  373.7 27.6 %collective-permute-start.40 = (bf16[768,512]{1,0:T(8,128)(2,1)S(1)}, bf16[768,512]{1,0:T(8,128)(2,1)S(1)}, u32[]{:S(2)}, u32[]{:S(2)}) collective-permute-start(bf16[768,512]{1,0:T(8,128)(2,1)S(1)} %maximum_select_fusion.4), channel_id=1, source_target_pairs={{0,16},{1,17},{2,18},{3,19},{4,20},{5,21},{6,22},{7,23},{8,24},{9,... | collective-permute-start | bytes 2359304 | tf_op jit(solution)/shard_map/ppermute | solution.py:724
  381.5 19.5 %collective-permute-start.30 = (bf16[384,512]{1,0:T(8,128)(2,1)S(1)}, bf16[384,512]{1,0:T(8,128)(2,1)S(1)}, u32[]{:S(2)}, u32[]{:S(2)}) collective-permute-start(bf16[384,512]{1,0:T(8,128)(2,1)S(1)} %maximum_select_fusion.5), channel_id=1, source_target_pairs={{0,16},{1,17},{2,18},{3,19},{4,20},{5,21},{6,22},{7,23},{8,24},{9,... | collective-permute-start | bytes 1179656 | tf_op jit(solution)/shard_map/ppermute | solution.py:724
  (37 other events, 350.3 us)

commit v2 on v0

--- a/solution.py
+++ b/solution.py
@@ -3,6 +3,8 @@
 import jax
 import jax.numpy as jnp
 from jax import lax
+from jax.experimental import pallas as pl
+from jax.experimental.pallas import tpu as pltpu
 from jax.sharding import PartitionSpec as P
 
 HEADS = 4
@@ -46,7 +48,7 @@
     return (value_grad, jnp.sum(upstream * normed, axis=0), jnp.sum(upstream, axis=0))
 
 
-def on_device(
+def spread_plan(
     tokens,
     query_counts,
     cotangent,
@@ -263,9 +265,777 @@
     return (layer_out, grad_tokens) + tuple(finals)
 
 
+BF16, F32 = jnp.bfloat16, jnp.float32
+MIB = 2**20
+AXES = ("grp", "ctx")
+LANES = 128
+ROWS_STEP = 528
+
+
+def one_chip_each(mesh):
+    return mesh.shape["grp"] % 2 == 0 and mesh.shape["ctx"] == 2 * NBLK
+
+
+def dot(left, right, over_left, over_right):
+    return lax.dot_general(
+        left, right, (((over_left,), (over_right,)), ((), ())), preferred_element_type=F32
+    )
+
+
+def kernel_call(body, grid, ins, outs, scratch, flops, moved, *operands, exps=0, into=()):
+    given = len(ins)
+
+    def run(*refs):
+        body(*refs[:given], *refs[given + len(into) :])
+
+    return pl.pallas_call(
+        run,
+        grid=grid,
+        in_specs=[
+            pl.BlockSpec(memory_space=index) if shape is None else pl.BlockSpec(shape, index)
+            for shape, index in ins
+        ]
+        + [pl.BlockSpec(memory_space=pl.ANY)] * len(into),
+        out_specs=[
+            pl.BlockSpec(memory_space=index) if shape is None else pl.BlockSpec(shape, index)
+            for shape, index, _, _ in outs
+        ],
+        out_shape=[jax.ShapeDtypeStruct(shape, kind) for _, _, shape, kind in outs],
+        scratch_shapes=scratch,
+        input_output_aliases={given + j: j for j in range(len(into))},
+        cost_estimate=pl.CostEstimate(flops=flops, bytes_accessed=moved, transcendentals=exps),
+        compiler_params=pltpu.CompilerParams(vmem_limit_bytes=60 * MIB),
+    )(*operands, *into)
+
+
+def project_kernel(context, scale, own, other, wq, wk, wv, q_out, k_out, v_out, x_out):
+    rows = own[...]
+    x_out[0] = rows
+    queries = (dot(rows, wq[...], 1, 0) * scale).astype(BF16)
+    for h in range(HEADS):
+        q_out[h] = queries[:, h * HD : (h + 1) * HD]
+    for side, keys_of in enumerate((rows[:context], other[:context])):
+        keys = dot(keys_of, wk[...], 1, 0).astype(BF16)
+        values = dot(keys_of, wv[...], 1, 0).astype(BF16)
+        for h in range(HEADS):
+            k_out[h, side, 0] = keys[:, h * HD : (h + 1) * HD]
+            v_out[h, side, 0] = values[:, h * HD : (h + 1) * HD]
+
+
+def project(own, other, place, blocks, context, kinds, scale, into):
+    rows, width = own.shape
+    fixed = lambda b: (0, 0)
+    key_spec = (
+        (HEADS, 2, 1, context, HD),
+        lambda b: (0, 0, place, 0, 0),
+        (HEADS, 2, blocks, context, HD),
+        BF16,
+    )
+    return kernel_call(
+        partial(project_kernel, context, scale),
+        (1,),
+        [((rows, width), fixed)] * 2 + [((width, width), fixed)] * 3,
+        [
+            ((HEADS, rows, HD), lambda b: (0, place, 0), (HEADS, blocks * rows, HD), BF16),
+            key_spec,
+            key_spec,
+            ((1, rows, width), lambda b: (place, 0, 0), (blocks, rows, width), BF16),
+        ],
+        [],
+        2 * width * width * (rows + 4 * context),
+        4 * width * (rows + 3 * context),
+        own,
+        other,
+        *kinds,
+        into=into,
+    )
+
+
+def forward_kernel(sets, steps, row_blocks, chunk, q_ref, *refs):
+    k_refs, v_refs, refs = refs[:sets], refs[sets : 2 * sets], refs[2 * sets :]
+    p_ref, o_ref, sum_ref, s_even, s_odd, top_even, top_odd, v_wide = refs
+    t = pl.program_id(0)
+    rows, hd = q_ref.shape[-2:]
+    keys = p_ref.shape[-1]
+
+    @pl.when(t == 0)
+    def _():
+        v_wide[:, hd:] = jnp.ones((keys, hd), BF16)
+
+    @pl.when((t > 0) & (lax.rem(t - 1, row_blocks) == 0))
+    def _():
+        start = 0
+        for v_ref in v_refs:
+            v_wide[start : start + v_ref.shape[1], :hd] = v_ref[0]
+            start += v_ref.shape[1]
+
+    places = []
+    for k_ref in k_refs:
+        places += [(k_ref, slice(c, c + chunk)) for c in range(0, k_ref.shape[1], chunk)]
+
+    def body(score, weigh, s_now, s_before, top_now, top_before):
+        if score:
+            q = q_ref[0]
+            high = None
+        if weigh:
+            peak = jnp.max(top_before[...], axis=-1, keepdims=True)
+            total = jnp.zeros((rows, 2 * hd), F32)
+        for c, (k_ref, within) in enumerate(places):
+            at = slice(c * chunk, (c + 1) * chunk)
+            if score:
+                scores = dot(q, k_ref[0, within, :], 1, 1)
+                s_now[:, at] = scores
+                for j in range(chunk // LANES):
+                    part = scores[:, j * LANES : (j + 1) * LANES]
+                    high = part if high is None else jnp.maximum(high, part)
+            if weigh:
+                soft = jnp.exp2(s_before[:, at] - peak).astype(BF16)
+                p_ref[0, :, at] = soft
+                total = total + dot(soft, v_wide[at, :], 1, 0)
+        if score:
+            top_now[...] = high
+        if weigh:
+            o_ref[...] = total[:, :hd]
+            sum_ref[0] = total[:, hd:]
+
+    even = (s_even, s_odd, top_even, top_odd)
+    odd = (s_odd, s_even, top_odd, top_even)
+    inside = (t > 0) & (t < steps)
+    pl.when(inside & (lax.rem(t, 2) == 0))(lambda: body(True, True, *even))
+    pl.when(inside & (lax.rem(t, 2) == 1))(lambda: body(True, True, *odd))
+    pl.when(t == 0)(lambda: body(True, False, *even))
+    pl.when(t == steps)(lambda: body(False, True, *(odd if steps % 2 else even)))
+
+
+def attention_forward(q, ks, vs, row_blocks, chunk=512):
+    heads, total, hd = q.shape
+    keys = sum(k.shape[1] for k in ks)
+    rows = total // row_blocks
+    steps = heads * row_blocks
+    ahead = lambda t: jnp.minimum(t, steps - 1)
+    behind = lambda t: jnp.maximum(t - 1, 0)
+    by_row = lambda t: (behind(t) // row_blocks, behind(t) % row_blocks, 0)
+    per_row = ((1, rows, hd), by_row, (heads, total, hd), F32)
+    return kernel_call(
+        partial(forward_kernel, len(ks), steps, row_blocks, chunk),
+        (steps + 1,),
+        [((1, rows, hd), lambda t: (ahead(t) // row_blocks, ahead(t) % row_blocks, 0))]
+        + [((1, k.shape[1], hd), lambda t: (ahead(t) // row_blocks, 0, 0)) for k in ks]
+        + [((1, v.shape[1], hd), lambda t: (behind(t) // row_blocks, 0, 0)) for v in vs],
+        [
+            ((1, rows, keys), by_row, (heads, total, keys), BF16),
+            (
+                (rows, hd),
+                lambda t: (behind(t) % row_blocks, behind(t) // row_blocks),
+                (total, heads * hd),
+                F32,
+            ),
+            per_row,
+        ],
+        [
+            pltpu.VMEM((rows, keys), F32),
+            pltpu.VMEM((rows, keys), F32),
+            pltpu.VMEM((rows, LANES), F32),
+            pltpu.VMEM((rows, LANES), F32),
+            pltpu.VMEM((keys, 2 * hd), BF16),
+        ],
+        8 * heads * total * keys * hd,
+        2 * heads * total * keys,
+        q,
+        *ks,
+        *vs,
+        exps=heads * total * keys,
+    )
+
+
+def gelu_pair(inner):
+    size = jnp.abs(inner) * (0.5**0.5)
+    rate = 1.0 / (1.0 + 0.3275911 * size)
+    bell = jnp.exp(-(size * size))
+    tail = rate * (
+        0.254829592
+        + rate * (-0.284496736 + rate * (1.421413741 + rate * (-1.453152027 + rate * 1.061405429)))
+    )
+    tail = 0.5 * tail * bell
+    below = jnp.where(inner < 0, tail, 1.0 - tail)
+    return inner * below, below + inner * bell * 0.3989422804014327
+
+
+def dense_kernel(
+    blocks, steps, bit_ref, x_ref, o_ref, total_ref, wo, w1, b1, w2, b2, g1, s1, g2, s2, *refs
+):
+    cot_refs, refs = refs[:blocks], refs[blocks:]
+    out_refs, refs = refs[:blocks], refs[blocks:]
+    first_ref, grad_ref, delta_ref, keep_ref, send_ref = refs[:5]
+    sums, sending, cot, out, arrived, left = refs[5:]
+    t = pl.program_id(0)
+    width, hidden_width = w1.shape
+    rows, half = x_ref.shape[0], sending.shape[0]
+    block = cot.shape[0] // blocks
+    load = [
+        pltpu.make_async_copy(ref, cot.at[pl.ds(j * block, block)], arrived.at[j])
+        for j, ref in enumerate(cot_refs)
+    ]
+    store = [
+        pltpu.make_async_copy(out.at[pl.ds(j * block, block)], ref, left.at[j])
+        for j, ref in enumerate(out_refs)
+    ]
+
+    @pl.when(t == 0)
+    def _():
+        for copy in load:
+            copy.start()
+        sums[...] = jnp.zeros_like(sums)
+
+    for j, copy in enumerate(load):
+        pl.when(t == j * block // rows)(copy.wait)
+    here = pl.ds(pl.multiple_of(t * rows, 16), rows)
+    gain_one, gain_two = g1[...].astype(F32), g2[...].astype(F32)
+    inverses = [1.0 / total_ref[h] for h in range(HEADS)]
+    attended = jnp.concatenate(
+        [o_ref[:, h * HD : (h + 1) * HD] * inverses[h] for h in range(HEADS)], axis=1
+    )
+    attended_low = attended.astype(BF16)
+    first_sum = x_ref[...].astype(F32) + dot(attended_low, wo[...], 1, 0)
+    hidden, normed_one, inverse_one = norm_forward(first_sum, gain_one, s1[...].astype(F32))
+    hidden_low = hidden.astype(BF16)
+    inner = dot(hidden_low, w1[...], 1, 0) + b1[...].astype(F32)
+    activated, slope = gelu_pair(inner)
+    activated = activated.astype(BF16)
+    second_sum = hidden + dot(activated, w2[...], 1, 0) + b2[...].astype(F32)
+    result, normed_two, inverse_two = norm_forward(second_sum, gain_two, s2[...].astype(F32))
+    out[here, :] = result.astype(BF16)
+    upstream = cot[here, :].astype(F32)
+    second_grad, gain_two_sum, shift_two_sum = norm_backward(
+        upstream, normed_two, inverse_two, gain_two
+    )
+    outer_grad = second_grad.astype(BF16)
+    at = width + hidden_width
+    sums[at : at + hidden_width] += dot(activated, outer_grad, 0, 0)
+    inner_grad = (dot(outer_grad, w2[...], 1, 1) * slope).astype(BF16)
+    inner_sums = dot(hidden_low, inner_grad, 0, 0)
+    for j in range(0, hidden_width, width):
+        sums[width + j : 2 * width + j] += inner_sums[:, j : j + width]
+    hidden_grad = second_grad + dot(inner_grad, w1[...], 1, 1)
+    first_grad, gain_one_sum, shift_one_sum = norm_backward(
+        hidden_grad, normed_one, inverse_one, gain_one
+    )
+    branch_grad = first_grad.astype(BF16)
+    first_ref[...] = branch_grad
+    sums[:width] += dot(attended_low, branch_grad, 0, 0)
+    attended_grad = dot(branch_grad, wo[...], 1, 1)
+    for h in range(HEADS):
+        at = slice(h * HD, (h + 1) * HD)
+        scaled = (attended_grad[:, at] * inverses[h]).astype(BF16)
+        grad_ref[h] = scaled
+        delta = jnp.sum(scaled.astype(F32) * attended[:, at], axis=-1, keepdims=True)
+        delta_ref[h] = jnp.broadcast_to(delta, delta_ref.shape[1:])
+    inner_sum = jnp.sum(inner_grad.astype(F32), axis=0)
+    vectors = [
+        gain_one_sum,
+        shift_one_sum,
+        gain_two_sum,
+        shift_two_sum,
+        jnp.sum(outer_grad.astype(F32), axis=0),
+    ]
+    vectors += [inner_sum[j : j + width] for j in range(0, hidden_width, width)]
+    at = width + 2 * hidden_width
+    for j, part in enumerate(vectors):
+        sums[at + j : at + j + 1, :] += part[None, :]
+
+    @pl.when(t == steps - 1)
+    def _():
+        bit = bit_ref[0]
+        keep = pltpu.make_async_copy(
+            sums.at[pl.ds(pl.multiple_of(bit * half, 16), half)], keep_ref, arrived.at[0]
+        )
+        sending[...] = sums[pl.ds(pl.multiple_of((1 - bit) * half, 16), half)].astype(BF16)
+        send = pltpu.make_async_copy(sending, send_ref, arrived.at[1])
+        copies = [*store, keep, send]
+        for copy in copies:
+            copy.start()
+        for copy in copies:
+            copy.wait()
+
+
+def dense(bit, x, cots, attended, total_of, weights, steps=3):
+    blocks, block, width = x.shape
+    total = blocks * block
+    rows = total // steps
+    hidden = weights[1].shape[1]
+    by_row = ((rows, width), lambda t: (t, 0))
+    by_head = ((HEADS, rows, HD), lambda t: (0, t, 0))
+    count = -(-(width + 2 * hidden + 8) // 256) * 256
+    *out, first_grad, grads, delta, keep, send = kernel_call(
+        partial(dense_kernel, blocks, steps),
+        (steps,),
+        [(None, pltpu.SMEM), by_row, by_row, by_head]
+        + [(w.shape, lambda t: (0, 0)) for w in weights]
+        + [(None, pl.ANY)] * blocks,
+        [(None, pl.ANY, (block, width), BF16)] * blocks
+        + [
+            (*by_row, (total, width), BF16),
+            (*by_head, (HEADS, total, HD), BF16),
+            (*by_head, (HEADS, total, HD), F32),
+            (None, pl.ANY, (count // 2, width), F32),
+            (None, pl.ANY, (count // 2, width), BF16),
+        ],
+        [
+            pltpu.VMEM((count, width), F32),
+            pltpu.VMEM((count // 2, width), BF16),
+            pltpu.VMEM((total, width), BF16),
+            pltpu.VMEM((total, width), BF16),
+            pltpu.SemaphoreType.DMA((blocks,)),
+            pltpu.SemaphoreType.DMA((blocks,)),
+        ],
+        6 * total * width * (width + 2 * hidden),
+        32 * total * width + 8 * width * (width + 2 * hidden),
+        bit,
+        x.reshape(total, width),
+        attended,
+        total_of,
+        *weights,
+        *cots,
+    )
+    return out, first_grad, grads, delta, keep, send
+
+
+def backward_kernel(scale_k, scale_q, carried, q_ref, g_ref, d_ref, p_ref, k_ref, v_ref, *refs):
+    if carried:
+        before, refs = refs[0], refs[1:]
+    kv_ref, dq_ref, dq_sum, ds, q_t, g_t = refs
+    c = pl.program_id(1)
+
+    @pl.when(c == 0)
+    def _():
+        q_t[...] = q_ref[0].T
+        g_t[...] = g_ref[0].T
+        dq_sum[...] = before[0] if carried else jnp.zeros_like(dq_sum)
+
+    keys, values = k_ref[0], v_ref[0]
+    chunk = keys.shape[0]
+    for start in range(0, p_ref.shape[1], ROWS_STEP):
+        at = slice(start, start + ROWS_STEP)
+        soft_grad = dot(g_ref[0, at, :], values, 1, 1)
+        delta = jnp.concatenate([d_ref[0, at, :]] * (chunk // LANES), axis=1)
+        score_grad = (p_ref[0, at, :].astype(F32) * (soft_grad - delta)).astype(BF16)
+        ds[at, :] = score_grad
+        dq_sum[at, :] += dot(score_grad, keys, 1, 0)
+    dv = dot(g_t[...], p_ref[0], 1, 0).T
+    dk = dot(q_t[...], ds[...], 1, 0).T * scale_k
+    kv_ref[0, 0] = dk.astype(BF16)
+    kv_ref[1, 0] = dv.astype(BF16)
+
+    @pl.when(c == pl.num_programs(1) - 1)
+    def _():
+        dq_ref[0] = (dq_sum[...] * scale_q).astype(dq_ref.dtype)
+
+
+def attention_backward(q, g, d, p, k, v, scale_k, scale_q, chunk, first, chunks, before=None):
+    heads, total, hd = q.shape
+    row = lambda h, c: (h, 0, 0)
+    key = lambda h, c: (h, c + first, 0)
+    by_row = ((1, total, hd), row)
+    carried = before is not None
+    return kernel_call(
+        partial(backward_kernel, scale_k, scale_q, carried),
+        (heads, chunks),
+        [
+            by_row,
+            by_row,
+            by_row,
+            ((1, total, chunk), lambda h, c: (h, 0, c + first)),
+            ((1, chunk, hd), key),
+            ((1, chunk, hd), key),
+        ]
+        + [by_row] * carried,
+        [
+            ((2, 1, chunk, hd), lambda h, c: (0, h, c, 0), (2, heads, chunks * chunk, hd), BF16),
+            (*by_row, (heads, total, hd), BF16 if carried else F32),
+        ],
+        [
+            pltpu.VMEM((total, hd), F32),
+            pltpu.VMEM((total, chunk), BF16),
+            pltpu.VMEM((hd, total), BF16),
+            pltpu.VMEM((hd, total), BF16),
+        ],
+        12 * heads * total * chunk * chunks * hd,
+        2 * heads * total * chunk * chunks,
+        q,
+        g,
+        d,
+        p,
+        k,
+        v,
+        *[before] * carried,
+    )
+
+
+def finish_kernel(context, blocks, first_ref, query_ref, own, other, wq, wk, wv, *refs):
+    token_refs, (key_ref, value_ref, tokens, left) = refs[:blocks], refs[blocks:]
+    b = pl.program_id(0)
+
+    def joined(one):
+        return jnp.concatenate([one(h).astype(BF16) for h in range(HEADS)], axis=1)
+
+    query_grad = joined(lambda h: query_ref[h, 0])
+    key_grad, value_grad = (
+        joined(lambda h, j=j: own[j, h, 0].astype(F32) + other[j, h, 0].astype(F32))
+        for j in range(2)
+    )
+    key_ref[0] = key_grad
+    value_ref[0] = value_grad
+    base = first_ref[0].astype(F32) + dot(query_grad, wq[...], 1, 1)
+    back = dot(key_grad, wk[...], 1, 1) + dot(value_grad, wv[...], 1, 1)
+    tokens[b, :context] = (base[:context] + back).astype(BF16)
+    tokens[b, context:] = base[context:].astype(BF16)
+    store = [
+        pltpu.make_async_copy(tokens.at[j], ref, left.at[j]) for j, ref in enumerate(token_refs)
+    ]
+    for j, copy in enumerate(store):
+        pl.when(b == j)(copy.start)
+
+    @pl.when(b == blocks - 1)
+    def _():
+        for copy in store:
+            copy.wait()
+
+
+def finish(first_grad, own, other, query_grad, kinds, blocks):
+    total, width = first_grad.shape
+    rows = total // blocks
+    context = own.shape[2] // blocks
+    block = lambda b: (b, 0, 0)
+    side = ((2, HEADS, 1, context, HD), lambda b: (0, 0, b, 0, 0))
+    by_rows = lambda count: ((1, count, width), block, (blocks, count, width), BF16)
+    return kernel_call(
+        partial(finish_kernel, context, blocks),
+        (blocks,),
+        [
+            ((1, rows, width), block),
+            ((HEADS, 1, rows, HD), lambda b: (0, b, 0, 0)),
+            side,
+            side,
+        ]
+        + [((width, width), lambda b: (0, 0))] * 3,
+        [(None, pl.ANY, (rows, width), BF16)] * blocks + [by_rows(context), by_rows(context)],
+        [pltpu.VMEM((blocks, rows, width), BF16), pltpu.SemaphoreType.DMA((blocks,))],
+        2 * blocks * width * width * (rows + 2 * context),
+        6 * blocks * width * (rows + 2 * context),
+        first_grad.reshape(blocks, rows, width),
+        query_grad.reshape(HEADS, blocks, rows, HD),
+        own.reshape(2, HEADS, blocks, context, HD),
+        other.reshape(2, HEADS, blocks, context, HD),
+        *kinds,
+    )
+
+
+def weigh_kernel(bit_ref, x_ref, query_ref, key_ref, value_ref, keep_ref, send_ref, sums, sending, left):
+    s = pl.program_id(0)
+    blocks, rows, width = x_ref.shape
+    context = key_ref.shape[1]
+    per = query_ref.shape[0]
+    columns = per * HD
+    x = x_ref[...].reshape(blocks * rows, width)
+    above = x_ref[:, :context].reshape(blocks * context, width)
+    query_grad = jnp.concatenate([query_ref[h] for h in range(per)], axis=1)
+    three = [dot(x, query_grad, 0, 0)]
+    for ref in (key_ref, value_ref):
+        three.append(dot(above, ref[...].reshape(blocks * context, columns), 0, 0))
+    steps = width // columns
+    for j in range(steps):
+
+        @pl.when(s == j)
+        def _(j=j):
+            for i, part in enumerate(three):
+                sums[i * width : (i + 1) * width, j * columns : (j + 1) * columns] = part
+
+    @pl.when(s == steps - 1)
+    def _():
+        bit = bit_ref[0]
+        half = sending.shape[0]
+        keep = pltpu.make_async_copy(
+            sums.at[pl.ds(pl.multiple_of(bit * half, 16), half)], keep_ref, left.at[0]
+        )
+        keep.start()
+        sending[...] = sums[pl.ds(pl.multiple_of((1 - bit) * half, 16), half)].astype(BF16)
+        send = pltpu.make_async_copy(sending, send_ref, left.at[1])
+        send.start()
+        keep.wait()
+        send.wait()
+
+
+def weigh(bit, x, query_grad, key_grad, value_grad, per=2):
+    blocks, rows, width = x.shape
+    context = key_grad.shape[1]
+    by_columns = ((blocks, context, per * HD), lambda s: (0, 0, s))
+    half = 3 * width // 2
+    return kernel_call(
+        weigh_kernel,
+        (HEADS // per,),
+        [
+            (None, pltpu.SMEM),
+            (x.shape, lambda s: (0, 0, 0)),
+            ((per, blocks * rows, HD), lambda s: (s, 0, 0)),
+            by_columns,
+            by_columns,
+        ],
+        [(None, pl.ANY, (half, width), F32), (None, pl.ANY, (half, width), BF16)],
+        [
+            pltpu.VMEM((3 * width, width), F32),
+            pltpu.VMEM((half, width), BF16),
+            pltpu.SemaphoreType.DMA((2,)),
+        ],
+        2 * blocks * width * width * (rows + 2 * context),
+        4 * blocks * width * (rows + context),
+        bit,
+        x,
+        query_grad,
+        key_grad,
+        value_grad,
+    )
+
+
+def summing(groups, members):
+    grp, ctx = lax.axis_index("grp"), lax.axis_index("ctx")
+    planes, along = groups // 2, members // 2
+    places = [(g, c) for g in range(groups) for c in range(members)]
+    number = lambda g, c: g * members + c
+    stages = (
+        (2, grp % 2, lambda g, c, s: (g ^ s, c)),
+        (
+            2 * planes,
+            grp // 2 * 2 + ctx % 2,
+            lambda g, c, s: (g ^ (s // 2 * 2), c ^ (s % 2)),
+        ),
+        (along, ctx // 2, lambda g, c, s: (g, c ^ (2 * s))),
+    )
+
+    def swap(array, move, s):
+        return lax.ppermute(
+            array, AXES, [(number(g, c), number(*move(g, c, s))) for g, c in places]
+        )
+
+    def reduce_pieces(stage, part):
+        count, index, _ = stage
+        piece = part.shape[0] // count
+        take = lambda s: lax.dynamic_slice_in_dim(part, (index ^ s) * piece, piece)
+        return [take(0)] + [take(s).astype(BF16) for s in range(1, count)]
+
+    def reduce_join(stage, own, came):
+        return sum((array.astype(F32) for array in came), own)
+
+    def gather_pieces(stage, part):
+        return [part.astype(BF16)] * stage[0]
+
+    def gather_join(stage, own, came):
+        count, index, _ = stage
+        shares = [own] + came
+        step = 1
+        while step < count:
+            turned = (index // step) % 2 == 1
+            shares = [jnp.where(turned, shares[s ^ step], shares[s]) for s in range(count)]
+            step *= 2
+        return jnp.concatenate(shares)
+
+    def send(stage, pieces):
+        return [swap(piece, stage[2], s) for s, piece in enumerate(pieces) if s]
+
+    return [
+        (partial(reduce_pieces, stage), partial(send, stage), partial(reduce_join, stage))
+        for stage in stages
+    ] + [
+        (partial(gather_pieces, stage), partial(send, stage), partial(gather_join, stage))
+        for stage in reversed(stages)
+    ]
+
+
+def gathered_plan(
+    tokens,
+    query_counts,
+    cotangent,
+    query_weight,
+    key_weight,
+    value_weight,
+    output_weight,
+    inner_weight,
+    inner_bias,
+    outer_weight,
+    outer_bias,
+    first_gain,
+    first_shift,
+    second_gain,
+    second_shift,
+):
+    blocks, rows, width = tokens.shape
+    groups, members = lax.axis_size("grp"), lax.axis_size("ctx")
+    member = lax.axis_index("ctx")
+    place = member // 2
+    context = CTX // members
+    slots = QUERIES // members
+
+    far = blocks // 2
+    order = [r for r in range(blocks) if r != far] + [far]
+
+    def route(r, back=False):
+        pairs = []
+        for g in range(groups):
+            for c in range(members):
+                to = (g - g % 2 + c % 2) * members + ((c // 2 + r) % blocks) * 2 + g % 2
+                pairs.append((to, g * members + c) if back else (g * members + c, to))
+        return pairs
+
+    across = [
+        (g * members + c, (g ^ 1) * members + c) for g in range(groups) for c in range(members)
+    ]
+    tie = lambda *arrays: lax.optimization_barrier(arrays)
+
+    def block_of(array, r):
+        return lax.dynamic_index_in_dim(array, lax.rem(place + r, blocks), 0, keepdims=False)
+
+    def outward(block, r):
+        return lax.ppermute(block, AXES, route(r))
+
+    def homeward(block, r):
+        return lax.ppermute(block, AXES, route(r, True))
+
+    def put(whole, block, r):
+        return lax.dynamic_update_index_in_dim(whole, block, lax.rem(place + r, blocks), 0)
+
+    slot = member * slots + jnp.arange(rows, dtype=jnp.int32) - context
+    live = (jnp.arange(rows) < context)[None, :] | (slot[None, :] < query_counts[:, None])
+    live = live[:, :, None]
+    masked = jnp.where(live, cotangent, 0).astype(BF16)
+
+    scale = HD**-0.5
+    log2e = 1.4426950408889634
+    kinds = (query_weight, key_weight, value_weight)
+    *own, own_far = [outward(block_of(tokens, r), r) for r in order]
+    other = [lax.ppermute(block, AXES, across) for block in own]
+    qkvx = ()
+    for j in range(blocks - 1):
+        qkvx = project(own[j], other[j], j, blocks, context, kinds, scale * log2e, qkvx)
+    own_far, *qkvx = tie(own_far, *qkvx)
+    other_far = lax.ppermute(own_far, AXES, across)
+    qkvx = project(
+        own_far, other_far, blocks - 1, blocks, context, kinds, scale * log2e, qkvx
+    )
+    q, k, v, x = qkvx
+    k, v = (array.reshape(HEADS, 2 * blocks * context, HD) for array in (k, v))
+
+    *cots, q = tie(*[block_of(masked, r) for r in order], q)
+    cots = [outward(block, r) for block, r in zip(cots, order, strict=True)]
+    p, attended, totals = attention_forward(q, [k], [v], blocks)
+    *cots, p = tie(*cots, p)
+
+    lifted = lambda vector: vector.reshape(1, -1)
+    weights = (
+        output_weight,
+        inner_weight,
+        lifted(inner_bias),
+        outer_weight,
+        lifted(outer_bias),
+        lifted(first_gain),
+        lifted(first_shift),
+        lifted(second_gain),
+        lifted(second_shift),
+    )
+    bit = lax.rem(lax.axis_index("grp"), 2).astype(jnp.int32).reshape(1)
+    out, first_grad, grads, delta, keep, given = dense(bit, x, cots, attended, totals, weights)
+
+    stages = summing(groups, members)
+    scale_k = 1.0 / log2e
+    chunk = blocks * context // 2
+
+    def start(stage, part):
+        pieces_of, send, join = stage
+        mine, *pieces = pieces_of(part)
+        return pieces, lambda pieces: send([mine] + pieces), partial(join, mine)
+
+    *out, given, grads = tie(*out, given, grads)
+    came = lax.ppermute(given, AXES, across)
+    home = [homeward(out[j], r) for j, r in enumerate(order[:-1])]
+    kv_other, dq = attention_backward(q, grads, delta, p, k, v, scale_k, 1.0, chunk, 2, 2)
+    *home, came, kv_other, grads = tie(*home, came, kv_other, grads)
+    early = keep + came.astype(F32)
+
+    pieces, send, join = start(stages[1], early)
+    *pieces, kv_other, far_out, grads = tie(*pieces, kv_other, out[-1], grads)
+    kv_came = lax.ppermute(kv_other, AXES, across)
+    came = send(pieces)
+    home.append(homeward(far_out, far))
+    kv_own, dq = attention_backward(q, grads, delta, p, k, v, scale_k, scale, chunk, 0, 2, dq)
+    *came, home[-1], kv_came, kv_own = tie(*came, home[-1], kv_came, kv_own)
+    early = join(came)
+
+    pieces, send, join = start(stages[2], early)
+    *pieces, kv_own = tie(*pieces, kv_own)
+    came = send(pieces)
+    *token_grad, key_grad, value_grad = finish(first_grad, kv_own, kv_came, dq, kinds, blocks)
+    ready = tie(*came, *token_grad)
+    came, token_grad = list(ready[: len(came)]), ready[len(came) :]
+    early = join(came)
+
+    *token_grad, x = tie(*token_grad, x)
+    back = [homeward(token_grad[j], order[j]) for j in range(blocks - 2)]
+    keep, given = weigh(bit, x, dq, key_grad, value_grad)
+    *back, given, token_three = tie(*back, given, token_grad[-2])
+    came = lax.ppermute(given, AXES, across)
+    back.append(homeward(token_three, order[-2]))
+    late = keep + came.astype(F32)
+    pieces, send, join = start(stages[1], late)
+    late = join(send(pieces))
+    pieces, send, join = start(stages[2], late)
+    came = send(pieces)
+    *came, back[-1] = tie(*came, back[-1])
+    late = join(came)
+    shares = (early.shape[0], late.shape[0])
+    both = jnp.concatenate([early, late])
+    pieces, send, join = start(stages[3], both)
+    both = join(send(pieces))
+    pieces, send, join = start(stages[4], both)
+    *pieces, token_far = tie(*pieces, token_grad[-1])
+    came = send(pieces)
+    went = homeward(token_far, far)
+    *home, live, came[0] = tie(*home, live, came[0])
+    layer_out = jnp.zeros((blocks, rows, width), BF16)
+    grad_tokens = jnp.zeros((blocks, rows, width), F32)
+    for block, r in zip(home, order, strict=True):
+        layer_out = put(layer_out, jnp.where(block_of(live, r), block, 0).astype(BF16), r)
+    for block, r in zip(back, order, strict=False):
+        grad_tokens = put(grad_tokens, block.astype(F32), r)
+    *came, went = tie(*came, went)
+    both = join(came)
+    pieces, send, join = start(stages[5], both)
+    both = join(send(pieces)).reshape(-1, sum(shares), width)
+    early = both[:, : shares[0]].reshape(-1, width).astype(F32)
+    late = both[:, shares[0] :].reshape(-1, width).astype(F32)
+    grad_tokens = put(grad_tokens, went.astype(F32), far)
+
+    hidden = inner_weight.shape[1]
+    inner_at = [early[at : at + width] for at in range(width, width + hidden, width)]
+    vectors = early[width + 2 * hidden :]
+    return (
+        layer_out,
+        grad_tokens,
+        late[:width],
+        late[width : 2 * width],
+        late[2 * width :],
+        early[:width],
+        jnp.concatenate(inner_at, axis=1),
+        vectors[5 : 5 + hidden // width].reshape(hidden),
+        early[width + hidden : width + 2 * hidden],
+        vectors[4],
+        vectors[0],
+        vectors[1],
+        vectors[2],
+        vectors[3],
+    )
+
+
 def solution(mesh):
     return jax.shard_map(
-        on_device,
+        gathered_plan if one_chip_each(mesh) else spread_plan,
         mesh=mesh,
         in_specs=(
             P("grp", "ctx", None),

time: 1980 us -> 396 us (0.20)
  waiting for transfers between devices: 1210 us -> 79.1 us
  matrix products: 423 us -> 0 us
  Pallas kernels: 0 us -> 200 us
  other arithmetic: 181 us -> 20.6 us
  local copies, waits for them, and re-layouts: 109 us -> 22.7 us
  starting transfers between devices: 0.21 us -> 66.2 us
  blocking collectives: 41.3 us -> 0 us
    reduce_scatter x2 -> x0, waiting for transfers between devices: 751 us -> none  [the longest x1 540 us: attend_back(): lax.psum_scatter(key_part.reshape(NBLK, -1, width), 'ctx', scatter_dimens...]
    dot_general x24 -> x0, matrix products: 423 us -> none  [the longest x1 96.6 us: attend_back(): jnp.einsum('nrhd,nkhd->nhrk', grad_heads, value_heads, preferred_element_...]
    all_gather x2 -> x0, waiting for transfers between devices: 334 us -> none  [the longest x1 204 us: fetch(): lax.all_gather(keys_mine, 'ctx', axis=1, tiled=True)]
    pallas_call x0 -> x10, Pallas kernels: none -> 200 us  [kernel_call(): pl.pallas_call(run, grid=grid, in_specs=[pl.BlockSpec(memory_space=index)...]
    psum x1 -> x0, waiting for transfers between devices: 125 us -> none  [on_device(): lax.psum((grad_query, grad_key, grad_value, grad_output, grad_inner, grad...]
    convert_element_type x10 -> x2, other arithmetic: 117 us -> 1.53 us  [the longest x1 1 us: gathered_plan(): early = both[:, :shares[0]].reshape(-1, width).astype(F32)]
    ppermute x0 -> x42, waiting for transfers between devices: none -> 79.1 us  [the longest x19 34.7 us: swap(): lax.ppermute(array, AXES, [(number(g, c), number(*move(g, c, s))) for g,...]
    reshape x4 -> x6, local copies, waits for them, and re-layouts: 71.6 us -> 3.5 us  [gathered_plan(): lifted = lambda vector: vector.reshape(1, -1)]
  transfers between devices with their start and end apart: 5 -> 42, of which waited for: 5 -> 17; matrix products, arithmetic and copies ran while one was open for 24% -> 2% of each run, Pallas kernels for 0% -> 41%
where the time goes in v2:
time: 396 us; the launch traced here: 391 us
  Pallas kernels  200 us (51%)
  waiting for transfers between devices  79.1 us (20%)
  starting transfers between devices  66.2 us (17%)
  local copies, waits for them, and re-layouts  22.7 us (6%)
  other arithmetic  20.6 us (5%)
    pallas_call x10, Pallas kernels, kernel_call(): pl.pallas_call(run, grid=grid, in_specs=[pl.BlockSpec(memory_space=index)...  200 us
    ppermute x19, waiting for transfers between devices, swap(): lax.ppermute(array, AXES, [(number(g, c), number(*move(g, c, s))) for g,...  34.7 us
    ppermute x19, starting transfers between devices, swap(): lax.ppermute(array, AXES, [(number(g, c), number(*move(g, c, s))) for g,...  27.3 us
    ppermute x8, waiting for transfers between devices, outward(): return lax.ppermute(block, AXES, route(r))  23.5 us
    ppermute x8, waiting for transfers between devices, homeward(): return lax.ppermute(block, AXES, route(r, True))  18.8 us
    ppermute x8, starting transfers between devices, homeward(): return lax.ppermute(block, AXES, route(r, True))  11.6 us
    ppermute x3, starting transfers between devices, gathered_plan(): other = [lax.ppermute(block, AXES, across) for block in own]  11 us
    ppermute x8, starting transfers between devices, outward(): return lax.ppermute(block, AXES, route(r))  10.9 us
  transfers between devices with their start and end apart: 42, of which 17 were waited for; matrix products, arithmetic and copies ran while one was open for 2% of the time, Pallas kernels for 41%

profile of v2, /device:TPU:0, one launch (start us, length us, event | category | flops | bytes accessed | tf_op | source)
XLA Modules:
  0.0 390.6 jit_solution(17983375123334019011)
XLA Ops:
  9.0 7.0 %collective-permute-start.6 = (bf16[528,512]{1,0:T(8,128)(2,1)}, bf16[528,512]{1,0:T(8,128)(2,1)}, u32[]{:S(2)}, u32[]{:S(2)}) collective-permute-start(bf16[528,512]{1,0:T(8,128)(2,1)} %collective-permute-done.5.refs_0_), channel_id=1, source_target_pairs={{0,8},{1,9},{2,10},{3,11},{4,12},{5,13},{6,14},{7,15},{8,0},{9,1},... | collective-permute-start | bytes 1622024 | tf_op jit(solution)/shard_map/ppermute | solution.py:914
  15.9 4.9 %collective-permute-done.3.refs_0_ = bf16[528,512]{1,0:T(8,128)(2,1)S(1)} collective-permute-done((bf16[528,512]{1,0:T(8,128)(2,1)S(1)}, bf16[528,512]{1,0:T(8,128)(2,1)S(1)}, u32[]{:S(2)}, u32[]{:S(2)}) %collective-permute-start.3) | collective-permute-done | bytes 540704 | tf_op jit(solution)/shard_map/ppermute | solution.py:897
  20.8 4.0 %collective-permute-start.4 = (bf16[528,512]{1,0:T(8,128)(2,1)S(1)}, bf16[528,512]{1,0:T(8,128)(2,1)S(1)}, u32[]{:S(2)}, u32[]{:S(2)}) collective-permute-start(bf16[528,512]{1,0:T(8,128)(2,1)S(1)} %collective-permute-done.3.refs_0_), channel_id=1, source_target_pairs={{0,8},{1,9},{2,10},{3,11},{4,12},{5,13},{6,14},{7,15},{8,0},{9,1},... | collective-permute-start | bytes 1622024 | tf_op jit(solution)/shard_map/ppermute | solution.py:914
  24.8 8.7 %collective-permute-done.1.refs_0_ = bf16[528,512]{1,0:T(8,128)(2,1)S(1)} collective-permute-done((bf16[528,512]{1,0:T(8,128)(2,1)S(1)}, bf16[528,512]{1,0:T(8,128)(2,1)S(1)}, u32[]{:S(2)}, u32[]{:S(2)}) %collective-permute-start.1) | collective-permute-done | bytes 540704 | tf_op jit(solution)/shard_map/ppermute | solution.py:897
  34.4 4.9 %shard_map.254 = (bf16[4,2112,128]{2,1,0:T(8,128)(2,1)}, bf16[4,2,4,512,128]{4,3,2,1,0:T(8,128)(2,1)}, bf16[4,2,4,512,128]{4,3,2,1,0:T(8,128)(2,1)}, bf16[4,528,512]{2,1,0:T(8,128)(2,1)}) custom-call(bf16[528,512]{1,0:T(8,128)(2,1)} %collective-permute-done.5.refs_0_, bf16[528,512]{1,0:T(8,128)(2,1)} %collective-permute-done.6.refs_1_, ...), custom_call_target="tpu_custom_call" | custom-call | flops 1350565888 | bytes 4227072 | tf_op jit(solution)/shard_map/pallas_call | solution.py:291
  40.1 4.9 %shard_map.255 = (bf16[4,2112,128]{2,1,0:T(8,128)(2,1)}, bf16[4,2,4,512,128]{4,3,2,1,0:T(8,128)(2,1)}, bf16[4,2,4,512,128]{4,3,2,1,0:T(8,128)(2,1)}, bf16[4,528,512]{2,1,0:T(8,128)(2,1)}) custom-call(bf16[528,512]{1,0:T(8,128)(2,1)} %copy-done.25, ...), custom_call_target="tpu_custom_call", output_to_operand_aliasing={{0}: (5, {}), {1}: (6, {}), {2}: (7, {}), {3}: (8, {})} | custom-call | flops 1350565888 | bytes 4227072 | tf_op jit(solution)/shard_map/pallas_call | solution.py:291
  45.9 5.0 %shard_map.256 = (bf16[4,2112,128]{2,1,0:T(8,128)(2,1)}, bf16[4,2,4,512,128]{4,3,2,1,0:T(8,128)(2,1)}, bf16[4,2,4,512,128]{4,3,2,1,0:T(8,128)(2,1)}, bf16[4,528,512]{2,1,0:T(8,128)(2,1)}) custom-call(bf16[528,512]{1,0:T(8,128)(2,1)} %copy-done.24, ...), custom_call_target="tpu_custom_call", output_to_operand_aliasing={{0}: (5, {}), {1}: (6, {}), {2}: (7, {}), {3}: (8, {})} | custom-call | flops 1350565888 | bytes 4227072 | tf_op jit(solution)/shard_map/pallas_call | solution.py:291
  50.9 9.9 %collective-permute-done.refs_0_ = bf16[528,512]{1,0:T(8,128)(2,1)S(1)} collective-permute-done((bf16[528,512]{1,0:T(8,128)(2,1)S(1)}, bf16[528,512]{1,0:T(8,128)(2,1)S(1)}, u32[]{:S(2)}, u32[]{:S(2)}) %collective-permute-start) | collective-permute-done | bytes 540704 | tf_op jit(solution)/shard_map/ppermute | solution.py:897
  66.8 4.9 %shard_map.257 = (bf16[4,2112,128]{2,1,0:T(8,128)(2,1)}, bf16[4,2,4,512,128]{4,3,2,1,0:T(8,128)(2,1)}, bf16[4,2,4,512,128]{4,3,2,1,0:T(8,128)(2,1)}, bf16[4,528,512]{2,1,0:T(8,128)(2,1)}) custom-call(bf16[528,512]{1,0:T(8,128)(2,1)} %copy-done.22, ...), custom_call_target="tpu_custom_call", output_to_operand_aliasing={{0}: (5, {}), {1}: (6, {}), {2}: (7, {}), {3}: (8, {})} | custom-call | flops 1350565888 | bytes 4227072 | tf_op jit(solution)/shard_map/pallas_call | solution.py:291
  75.1 52.0 %shard_map.258 = (bf16[4,2112,4096]{2,1,0:T(8,128)(2,1)}, f32[2112,512]{1,0:T(8,128)}, f32[4,2112,128]{2,1,0:T(8,128)}) custom-call(bf16[4,2112,128]{2,1,0:T(8,128)(2,1)} %get-tuple-element.150.refs_0_, bf16[4,4096,128]{2,1,0:T(8,128)(2,1)} %bitcast.59, bf16[4,4096,128]{2,1,0:T(8,128)(2,1)} %bitcast.62), custom_call_target="tpu_custom_call" | custom-call | flops 35433480192 | bytes 69206016 | tf_op jit(solution)/shard_map/pallas_call | solution.py:291
  128.3 36.7 %shard_map.259 = (bf16[528,512]{1,0:T(8,128)(2,1)}, bf16[528,512]{1,0:T(8,128)(2,1)}, bf16[528,512]{1,0:T(8,128)(2,1)}, bf16[528,512]{1,0:T(8,128)(2,1)}, bf16[2...) custom-call(s32[1]{0:T(128)} %bitcast.refs_0_, ...), custom_call_target="tpu_custom_call" | custom-call | flops 16609443840 | bytes 45088768 | tf_op jit(solution)/shard_map/pallas_call | solution.py:291
  169.6 3.3 collective-permute-start.13
  172.9 36.7 %shard_map.260 = (bf16[2,4,2048,128]{3,2,1,0:T(8,128)(2,1)}, f32[4,2112,128]{2,1,0:T(8,128)}) custom-call(bf16[4,2112,128]{2,1,0:T(8,128)(2,1)} %get-tuple-element.150.refs_0_, bf16[4,2112,128]{2,1,0:T(8,128)(2,1)} %get-tuple-element.191.refs_1_, f32[4,2112,128]{2,1,0:T(8,128)} %get-tuple-element.175.refs_2_, ...), custom_call_target="tpu_custom_call" | custom-call | flops 26575110144 | bytes 34603008 | tf_op jit(solution)/shard_map/pallas_call | solution.py:291
  221.8 36.5 %shard_map.261 = (bf16[2,4,2048,128]{3,2,1,0:T(8,128)(2,1)}, bf16[4,2112,128]{2,1,0:T(8,128)(2,1)}) custom-call(bf16[4,2112,128]{2,1,0:T(8,128)(2,1)} %get-tuple-element.150.refs_0_, bf16[4,2112,128]{2,1,0:T(8,128)(2,1)} %get-tuple-element.191.refs_1_, f32[4,2112,128]{2,1,0:T(8,128)} %get-tuple-element.175.refs_2_, ...), custom_call_target="tpu_custom_call" | custom-call | flops 26575110144 | bytes 34603008 | tf_op jit(solution)/shard_map/pallas_call | solution.py:291
  266.1 10.3 %shard_map.262 = (bf16[528,512]{1,0:T(8,128)(2,1)}, bf16[528,512]{1,0:T(8,128)(2,1)}, bf16[528,512]{1,0:T(8,128)(2,1)}, bf16[528,512]{1,0:T(8,128)(2,1)}, bf16[4...) custom-call(bf16[4,528,512]{2,1,0:T(8,128)(2,1)} %bitcast.69, bf16[4,4,528,128]{3,2,1,0:T(8,128)(2,1)} %bitcast.70, ...), custom_call_target="tpu_custom_call" | custom-call | flops 3254779904 | bytes 19070976 | tf_op jit(solution)/shard_map/pallas_call | solution.py:291
  280.0 8.5 %shard_map.263 = (f32[768,512]{1,0:T(8,128)}, bf16[768,512]{1,0:T(8,128)(2,1)}) custom-call(s32[1]{0:T(128)} %bitcast.refs_0_, bf16[4,528,512]{2,1,0:T(8,128)(2,1)} %get-tuple-element.217.refs_1_, bf16[4,2112,128]{2,1,0:T(8,128)(2,1)} %get-tuple-element.203.refs_2_, bf16[4,512,512]{2,1,0:T(8,128)(2,1)} %get-tuple-element.218.refs_3_, ...), custom_call_target="tpu_custom_call" | custom-call | flops 3254779904 | bytes 8519680 | tf_op jit(solution)/shard_map/pallas_call | solution.py:291
  288.6 4.6 %collective-permute-done.25 = bf16[528,512]{1,0:T(8,128)(2,1)S(1)} collective-permute-done((bf16[528,512]{1,0:T(8,128)(2,1)}, bf16[528,512]{1,0:T(8,128)(2,1)S(1)}, u32[]{:S(2)}, u32[]{:S(2)}) %collective-permute-start.25) | collective-permute-done | bytes 540704 | tf_op jit(solution)/shard_map/ppermute | solution.py:900
  306.1 3.7 collective-permute-done.28
  312.1 3.9 %collective-permute-start.30 = (bf16[48,512]{1,0:T(8,128)(2,1)S(1)}, bf16[48,512]{1,0:T(8,128)(2,1)S(1)}, u32[]{:S(2)}, u32[]{:S(2)}) collective-permute-start(bf16[48,512]{1,0:T(8,128)(2,1)S(1)} %get-tuple-element.291), channel_id=1, source_target_pairs={{0,2},{1,3},{2,0},{3,1},{4,6},{5,7},{6,4},{7,5},{8,10},{9,11},{10,... | collective-permute-start | bytes 147464 | tf_op jit(solution)/shard_map/ppermute | solution.py:815
  325.7 3.9 %collective-permute-start.36 = (bf16[136,512]{1,0:T(8,128)(2,1)S(1)}, bf16[136,512]{1,0:T(8,128)(2,1)S(1)}, u32[]{:S(2)}, u32[]{:S(2)}) collective-permute-start(bf16[136,512]{1,0:T(8,128)(2,1)S(1)} %pad_maximum_fusion.4), channel_id=1, source_target_pairs={{0,2},{1,3},{2,0},{3,1},{4,6},{5,7},{6,4},{7,5},{8,10},{9,11},{10,... | collective-permute-start | bytes 417800 | tf_op jit(solution)/shard_map/ppermute | solution.py:815
  332.5 4.1 %collective-permute-done.35 = bf16[136,512]{1,0:T(8,128)(2,1)S(1)} collective-permute-done((bf16[136,512]{1,0:T(8,128)(2,1)S(1)}, bf16[136,512]{1,0:T(8,128)(2,1)S(1)}, u32[]{:S(2)}, u32[]{:S(2)}) %collective-permute-start.35) | collective-permute-done | bytes 139296 | tf_op jit(solution)/shard_map/ppermute | solution.py:815
  340.5 12.0 %collective-permute-done.37 = bf16[544,512]{1,0:T(8,128)(2,1)S(1)} collective-permute-done((bf16[544,512]{1,0:T(8,128)(2,1)S(1)}, bf16[544,512]{1,0:T(8,128)(2,1)S(1)}, u32[]{:S(2)}, u32[]{:S(2)}) %collective-permute-start.37) | collective-permute-done | bytes 557088 | tf_op jit(solution)/shard_map/ppermute | solution.py:815
  352.5 14.1 %collective-permute-done.40 = bf16[528,512]{1,0:T(8,128)(2,1)S(1)} collective-permute-done((bf16[528,512]{1,0:T(8,128)(2,1)}, bf16[528,512]{1,0:T(8,128)(2,1)S(1)}, u32[]{:S(2)}, u32[]{:S(2)}) %collective-permute-start.40) | collective-permute-done | bytes 540704 | tf_op jit(solution)/shard_map/ppermute | solution.py:900
  377.9 3.8 broadcast_select_fusion.1
  (198 shorter events, 100.7 us)
Async XLA Ops:
  3.9 16.9 %collective-permute-start.3 = (bf16[528,512]{1,0:T(8,128)(2,1)S(1)}, bf16[528,512]{1,0:T(8,128)(2,1)S(1)}, u32[]{:S(2)}, u32[]{:S(2)}) collective-permute-start(bf16[528,512]{1,0:T(8,128)(2,1)S(1)} %get-tuple-element.278), channel_id=1, source_target_pairs={{0,2},{1,10},{2,4},{3,12},{4,6},{5,14},{6,0},{7,8},{8,3},{9,11},{1... | collective-permute-start | bytes 1622024 | tf_op jit(solution)/shard_map/ppermute | solution.py:897
  6.9 26.5 %collective-permute-start.1 = (bf16[528,512]{1,0:T(8,128)(2,1)S(1)}, bf16[528,512]{1,0:T(8,128)(2,1)S(1)}, u32[]{:S(2)}, u32[]{:S(2)}) collective-permute-start(bf16[528,512]{1,0:T(8,128)(2,1)S(1)} %get-tuple-element.276), channel_id=1, source_target_pairs={{0,6},{1,14},{2,0},{3,8},{4,2},{5,10},{6,4},{7,12},{8,7},{9,15},{1... | collective-permute-start | bytes 1622024 | tf_op jit(solution)/shard_map/ppermute | solution.py:897
  9.0 25.4 %collective-permute-start.6 = (bf16[528,512]{1,0:T(8,128)(2,1)}, bf16[528,512]{1,0:T(8,128)(2,1)}, u32[]{:S(2)}, u32[]{:S(2)}) collective-permute-start(bf16[528,512]{1,0:T(8,128)(2,1)} %collective-permute-done.5.refs_0_), channel_id=1, source_target_pairs={{0,8},{1,9},{2,10},{3,11},{4,12},{5,13},{6,14},{7,15},{8,0},{9,1},... | collective-permute-start | bytes 1622024 | tf_op jit(solution)/shard_map/ppermute | solution.py:914
  20.8 18.5 %collective-permute-start.4 = (bf16[528,512]{1,0:T(8,128)(2,1)S(1)}, bf16[528,512]{1,0:T(8,128)(2,1)S(1)}, u32[]{:S(2)}, u32[]{:S(2)}) collective-permute-start(bf16[528,512]{1,0:T(8,128)(2,1)S(1)} %collective-permute-done.3.refs_0_), channel_id=1, source_target_pairs={{0,8},{1,9},{2,10},{3,11},{4,12},{5,13},{6,14},{7,15},{8,0},{9,1},... | collective-permute-start | bytes 1622024 | tf_op jit(solution)/shard_map/ppermute | solution.py:914
  33.5 27.4 %collective-permute-start = (bf16[528,512]{1,0:T(8,128)(2,1)S(1)}, bf16[528,512]{1,0:T(8,128)(2,1)S(1)}, u32[]{:S(2)}, u32[]{:S(2)}) collective-permute-start(bf16[528,512]{1,0:T(8,128)(2,1)S(1)} %get-tuple-element.277), channel_id=1, source_target_pairs={{0,4},{1,12},{2,6},{3,14},{4,0},{5,8},{6,2},{7,10},{8,5},{9,13},{1... | collective-permute-start | bytes 1622024 | tf_op jit(solution)/shard_map/ppermute | solution.py:897
  71.7 55.5 %collective-permute-start.10 = (bf16[528,512]{1,0:T(8,128)(2,1)S(1)}, bf16[528,512]{1,0:T(8,128)(2,1)S(1)}, u32[]{:S(2)}, u32[]{:S(2)}) collective-permute-start(bf16[528,512]{1,0:T(8,128)(2,1)S(1)} %get-tuple-element.157), channel_id=1, source_target_pairs={{0,6},{1,14},{2,0},{3,8},{4,2},{5,10},{6,4},{7,12},{8,7},{9,15},{1... | collective-permute-start | bytes 1622024 | tf_op jit(solution)/shard_map/ppermute | solution.py:897
  73.7 53.5 %collective-permute-start.11 = (bf16[528,512]{1,0:T(8,128)(2,1)S(1)}, bf16[528,512]{1,0:T(8,128)(2,1)S(1)}, u32[]{:S(2)}, u32[]{:S(2)}) collective-permute-start(bf16[528,512]{1,0:T(8,128)(2,1)S(1)} %get-tuple-element.158), channel_id=1, source_target_pairs={{0,4},{1,12},{2,6},{3,14},{4,0},{5,8},{6,2},{7,10},{8,5},{9,13},{1... | collective-permute-start | bytes 1622024 | tf_op jit(solution)/shard_map/ppermute | solution.py:897
  73.7 53.5 %collective-permute-start.8 = (bf16[528,512]{1,0:T(8,128)(2,1)S(1)}, bf16[528,512]{1,0:T(8,128)(2,1)S(1)}, u32[]{:S(2)}, u32[]{:S(2)}) collective-permute-start(bf16[528,512]{1,0:T(8,128)(2,1)S(1)} %get-tuple-element.155), channel_id=1, source_target_pairs={{0,0},{1,8},{2,2},{3,10},{4,4},{5,12},{6,6},{7,14},{8,1},{9,9},{10... | collective-permute-start | bytes 1622024 | tf_op jit(solution)/shard_map/ppermute | solution.py:897
  74.4 52.9 %collective-permute-start.9 = (bf16[528,512]{1,0:T(8,128)(2,1)S(1)}, bf16[528,512]{1,0:T(8,128)(2,1)}, u32[]{:S(2)}, u32[]{:S(2)}) collective-permute-start(bf16[528,512]{1,0:T(8,128)(2,1)S(1)} %get-tuple-element.156), channel_id=1, source_target_pairs={{0,2},{1,10},{2,4},{3,12},{4,6},{5,14},{6,0},{7,8},{8,3},{9,11},{1... | collective-permute-start | bytes 1622024 | tf_op jit(solution)/shard_map/ppermute | solution.py:897
  165.0 44.7 %collective-permute-start.15 = (bf16[1408,512]{1,0:T(8,128)(2,1)}, bf16[1408,512]{1,0:T(8,128)(2,1)S(1)}, u32[]{:S(2)}, u32[]{:S(2)}) collective-permute-start(bf16[1408,512]{1,0:T(8,128)(2,1)} %get-tuple-element.173), channel_id=1, source_target_pairs={{0,8},{1,9},{2,10},{3,11},{4,12},{5,13},{6,14},{7,15},{8,0},{9,1},... | collective-permute-start | bytes 4325384 | tf_op jit(solution)/shard_map/ppermute | solution.py:956
  167.9 41.7 %collective-permute-start.12 = (bf16[528,512]{1,0:T(8,128)(2,1)}, bf16[528,512]{1,0:T(8,128)(2,1)S(1)}, u32[]{:S(2)}, u32[]{:S(2)}) collective-permute-start(bf16[528,512]{1,0:T(8,128)(2,1)} %get-tuple-element.170), channel_id=1, source_target_pairs={{0,0},{8,1},{2,2},{10,3},{4,4},{12,5},{6,6},{14,7},{1,8},{9,9},{3,... | collective-permute-start | bytes 1622024 | tf_op jit(solution)/shard_map/ppermute | solution.py:900
  169.6 40.0 %collective-permute-start.13 = (bf16[528,512]{1,0:T(8,128)(2,1)}, bf16[528,512]{1,0:T(8,128)(2,1)S(1)}, u32[]{:S(2)}, u32[]{:S(2)}) collective-permute-start(bf16[528,512]{1,0:T(8,128)(2,1)} %get-tuple-element.171), channel_id=1, source_target_pairs={{2,0},{10,1},{4,2},{12,3},{6,4},{14,5},{0,6},{8,7},{3,8},{11,9},{5... | collective-permute-start | bytes 1622024 | tf_op jit(solution)/shard_map/ppermute | solution.py:900
  172.9 36.8 %collective-permute-start.14 = (bf16[528,512]{1,0:T(8,128)(2,1)}, bf16[528,512]{1,0:T(8,128)(2,1)S(1)}, u32[]{:S(2)}, u32[]{:S(2)}) collective-permute-start(bf16[528,512]{1,0:T(8,128)(2,1)} %get-tuple-element.172), channel_id=1, source_target_pairs={{6,0},{14,1},{0,2},{8,3},{2,4},{10,5},{4,6},{12,7},{7,8},{15,9},{1... | collective-permute-start | bytes 1622024 | tf_op jit(solution)/shard_map/ppermute | solution.py:900
  214.9 43.5 %collective-permute-start.20 = (bf16[2,4,2048,128]{3,2,1,0:T(8,128)(2,1)}, bf16[2,4,2048,128]{3,2,1,0:T(8,128)(2,1)}, u32[]{:S(2)}, u32[]{:S(2)}) collective-permute-start(bf16[2,4,2048,128]{3,2,1,0:T(8,128)(2,1)} %get-tuple-element.190), channel_id=1, source_target_pairs={{0,8},{1,9},{2,10},{3,11},{4,12},{5,13},{6,14},{7,15},{8,0},{9,1},... | collective-permute-start | bytes 12582920 | tf_op jit(solution)/shard_map/ppermute | solution.py:964
  216.4 42.0 %collective-permute-start.19 = (bf16[528,512]{1,0:T(8,128)(2,1)}, bf16[528,512]{1,0:T(8,128)(2,1)S(1)}, u32[]{:S(2)}, u32[]{:S(2)}) collective-permute-start(bf16[528,512]{1,0:T(8,128)(2,1)} %get-tuple-element.189), channel_id=1, source_target_pairs={{4,0},{12,1},{6,2},{14,3},{0,4},{8,5},{2,6},{10,7},{5,8},{13,9},{7... | collective-permute-start | bytes 1622024 | tf_op jit(solution)/shard_map/ppermute | solution.py:900
  218.3 40.0 %collective-permute-start.16 = (bf16[352,512]{1,0:T(8,128)(2,1)}, bf16[352,512]{1,0:T(8,128)(2,1)}, u32[]{:S(2)}, u32[]{:S(2)}) collective-permute-start(bf16[352,512]{1,0:T(8,128)(2,1)} %get-tuple-element.186), channel_id=1, source_target_pairs={{0,1},{1,0},{2,3},{3,2},{4,5},{5,4},{6,7},{7,6},{8,9},{9,8},{10,11... | collective-permute-start | bytes 1081352 | tf_op jit(solution)/shard_map/ppermute | solution.py:815
  219.4 39.0 %collective-permute-start.17 = (bf16[352,512]{1,0:T(8,128)(2,1)}, bf16[352,512]{1,0:T(8,128)(2,1)}, u32[]{:S(2)}, u32[]{:S(2)}) collective-permute-start(bf16[352,512]{1,0:T(8,128)(2,1)} %get-tuple-element.187), channel_id=1, source_target_pairs={{0,16},{1,17},{2,18},{3,19},{4,20},{5,21},{6,22},{7,23},{8,24},{9,... | collective-permute-start | bytes 1081352 | tf_op jit(solution)/shard_map/ppermute | solution.py:815
  220.7 37.7 %collective-permute-start.18 = (bf16[352,512]{1,0:T(8,128)(2,1)S(1)}, bf16[352,512]{1,0:T(8,128)(2,1)}, u32[]{:S(2)}, u32[]{:S(2)}) collective-permute-start(bf16[352,512]{1,0:T(8,128)(2,1)S(1)} %get-tuple-element.188), channel_id=1, source_target_pairs={{0,17},{1,16},{2,19},{3,18},{4,21},{5,20},{6,23},{7,22},{8,25},{9,... | collective-permute-start | bytes 1081352 | tf_op jit(solution)/shard_map/ppermute | solution.py:815
  260.9 15.5 %collective-permute-start.21 = (bf16[88,512]{1,0:T(8,128)(2,1)S(1)}, bf16[88,512]{1,0:T(8,128)(2,1)S(1)}, u32[]{:S(2)}, u32[]{:S(2)}) collective-permute-start(bf16[88,512]{1,0:T(8,128)(2,1)S(1)} %get-tuple-element.199), channel_id=1, source_target_pairs={{0,2},{1,3},{2,0},{3,1},{4,6},{5,7},{6,4},{7,5},{8,10},{9,11},{10,... | collective-permute-start | bytes 270344 | tf_op jit(solution)/shard_map/ppermute | solution.py:815
  301.8 18.3 %collective-permute-start.33 = (bf16[528,512]{1,0:T(8,128)(2,1)}, bf16[528,512]{1,0:T(8,128)(2,1)S(1)}, u32[]{:S(2)}, u32[]{:S(2)}) collective-permute-start(bf16[528,512]{1,0:T(8,128)(2,1)} %get-tuple-element.226), channel_id=1, source_target_pairs={{6,0},{14,1},{0,2},{8,3},{2,4},{10,5},{4,6},{12,7},{7,8},{15,9},{1... | collective-permute-start | bytes 1622024 | tf_op jit(solution)/shard_map/ppermute | solution.py:900
  336.8 15.7 %collective-permute-start.37 = (bf16[544,512]{1,0:T(8,128)(2,1)S(1)}, bf16[544,512]{1,0:T(8,128)(2,1)S(1)}, u32[]{:S(2)}, u32[]{:S(2)}) collective-permute-start(bf16[544,512]{1,0:T(8,128)(2,1)S(1)} %pad_maximum_fusion.3), channel_id=1, source_target_pairs={{0,1},{1,0},{2,3},{3,2},{4,5},{5,4},{6,7},{7,6},{8,9},{9,8},{10,11... | collective-permute-start | bytes 1671176 | tf_op jit(solution)/shard_map/ppermute | solution.py:815
  337.9 28.7 %collective-permute-start.38 = (bf16[544,512]{1,0:T(8,128)(2,1)S(1)}, bf16[544,512]{1,0:T(8,128)(2,1)S(1)}, u32[]{:S(2)}, u32[]{:S(2)}) collective-permute-start(bf16[544,512]{1,0:T(8,128)(2,1)S(1)} %pad_maximum_fusion.3), channel_id=1, source_target_pairs={{0,16},{1,17},{2,18},{3,19},{4,20},{5,21},{6,22},{7,23},{8,24},{9,... | collective-permute-start | bytes 1671176 | tf_op jit(solution)/shard_map/ppermute | solution.py:815
  338.4 30.4 %collective-permute-start.39 = (bf16[544,512]{1,0:T(8,128)(2,1)S(1)}, bf16[544,512]{1,0:T(8,128)(2,1)}, u32[]{:S(2)}, u32[]{:S(2)}) collective-permute-start(bf16[544,512]{1,0:T(8,128)(2,1)S(1)} %pad_maximum_fusion.3), channel_id=1, source_target_pairs={{0,17},{1,16},{2,19},{3,18},{4,21},{5,20},{6,23},{7,22},{8,25},{9,... | collective-permute-start | bytes 1671176 | tf_op jit(solution)/shard_map/ppermute | solution.py:815
  340.4 26.2 %collective-permute-start.40 = (bf16[528,512]{1,0:T(8,128)(2,1)}, bf16[528,512]{1,0:T(8,128)(2,1)S(1)}, u32[]{:S(2)}, u32[]{:S(2)}) collective-permute-start(bf16[528,512]{1,0:T(8,128)(2,1)} %get-tuple-element.243), channel_id=1, source_target_pairs={{4,0},{12,1},{6,2},{14,3},{0,4},{8,5},{2,6},{10,7},{5,8},{13,9},{7... | collective-permute-start | bytes 1622024 | tf_op jit(solution)/shard_map/ppermute | solution.py:900
  (56 other events, 387.6 us)

commit v3 on v2

--- a/solution.py
+++ b/solution.py
@@ -565,7 +565,7 @@
     hidden = weights[1].shape[1]
     by_row = ((rows, width), lambda t: (t, 0))
     by_head = ((HEADS, rows, HD), lambda t: (0, t, 0))
-    count = -(-(width + 2 * hidden + 8) // 256) * 256
+    count = -(-(width + 2 * hidden + 8) // 512) * 512
     *out, first_grad, grads, delta, keep, send = kernel_call(
         partial(dense_kernel, blocks, steps),
         (steps,),
@@ -671,20 +671,90 @@
     )
 
 
-def finish_kernel(context, blocks, first_ref, query_ref, own, other, wq, wk, wv, *refs):
-    token_refs, (key_ref, value_ref, tokens, left) = refs[:blocks], refs[blocks:]
+def side_by_side(parts):
+    return jnp.concatenate([part.astype(BF16) for part in parts], axis=1)
+
+
+def weigh_kernel(
+    bit_ref, x_ref, query_ref, own_ref, other_ref, keep_ref, send_ref, sums, sending, left
+):
+    s = pl.program_id(0)
+    blocks, rows, width = x_ref.shape
+    context = own_ref.shape[2] // blocks
+    per = query_ref.shape[0]
+    columns = per * HD
+    x = x_ref[...].reshape(blocks * rows, width)
+    above = x_ref[:, :context].reshape(blocks * context, width)
+    three = [dot(x, side_by_side([query_ref[h] for h in range(per)]), 0, 0)]
+    for j in range(2):
+        whole = side_by_side(
+            [own_ref[j, h].astype(F32) + other_ref[j, h].astype(F32) for h in range(per)]
+        )
+        three.append(dot(above, whole, 0, 0))
+    steps = width // columns
+    for j in range(steps):
+
+        @pl.when(s == j)
+        def _(j=j):
+            for i, part in enumerate(three):
+                sums[i * width : (i + 1) * width, j * columns : (j + 1) * columns] = part
+
+    @pl.when(s == steps - 1)
+    def _():
+        bit = bit_ref[0]
+        half = sending.shape[0]
+        keep = pltpu.make_async_copy(
+            sums.at[pl.ds(pl.multiple_of(bit * half, 16), half)], keep_ref, left.at[0]
+        )
+        keep.start()
+        sending[...] = sums[pl.ds(pl.multiple_of((1 - bit) * half, 16), half)].astype(BF16)
+        send = pltpu.make_async_copy(sending, send_ref, left.at[1])
+        send.start()
+        keep.wait()
+        send.wait()
+
+
+def weigh(bit, x, query_grad, own, other, per=2):
+    blocks, rows, width = x.shape
+    keys = own.shape[2]
+    side = ((2, per, keys, HD), lambda s: (0, s, 0, 0))
+    half = 3 * width // 2
+    return kernel_call(
+        weigh_kernel,
+        (HEADS // per,),
+        [
+            (None, pltpu.SMEM),
+            (x.shape, lambda s: (0, 0, 0)),
+            ((per, blocks * rows, HD), lambda s: (s, 0, 0)),
+            side,
+            side,
+        ],
+        [(None, pl.ANY, (half, width), F32), (None, pl.ANY, (half, width), BF16)],
+        [
+            pltpu.VMEM((3 * width, width), F32),
+            pltpu.VMEM((half, width), BF16),
+            pltpu.SemaphoreType.DMA((2,)),
+        ],
+        2 * width * width * (blocks * rows + 2 * keys),
+        2 * width * (2 * blocks * rows + 4 * keys),
+        bit,
+        x,
+        query_grad,
+        own,
+        other,
+    )
+
+
+def finish_kernel(context, count, first_ref, query_ref, own, other, wq, wk, wv, *refs):
+    token_refs, (tokens, left) = refs[:count], refs[count:]
     b = pl.program_id(0)
-
-    def joined(one):
-        return jnp.concatenate([one(h).astype(BF16) for h in range(HEADS)], axis=1)
-
-    query_grad = joined(lambda h: query_ref[h, 0])
+    query_grad = side_by_side([query_ref[h, 0] for h in range(HEADS)])
     key_grad, value_grad = (
-        joined(lambda h, j=j: own[j, h, 0].astype(F32) + other[j, h, 0].astype(F32))
+        side_by_side(
+            [own[j, h, 0].astype(F32) + other[j, h, 0].astype(F32) for h in range(HEADS)]
+        )
         for j in range(2)
     )
-    key_ref[0] = key_grad
-    value_ref[0] = value_grad
     base = first_ref[0].astype(F32) + dot(query_grad, wq[...], 1, 1)
     back = dot(key_grad, wk[...], 1, 1) + dot(value_grad, wv[...], 1, 1)
     tokens[b, :context] = (base[:context] + back).astype(BF16)
@@ -695,33 +765,34 @@
     for j, copy in enumerate(store):
         pl.when(b == j)(copy.start)
 
-    @pl.when(b == blocks - 1)
+    @pl.when(b == count - 1)
     def _():
         for copy in store:
             copy.wait()
 
 
-def finish(first_grad, own, other, query_grad, kinds, blocks):
+def finish(ahead, first_grad, own, other, query_grad, kinds, blocks):
+    first, last = ahead[0], ahead[-1]
+    count = len(ahead)
+    at = lambda b: first + b * (last - first)
     total, width = first_grad.shape
     rows = total // blocks
     context = own.shape[2] // blocks
-    block = lambda b: (b, 0, 0)
-    side = ((2, HEADS, 1, context, HD), lambda b: (0, 0, b, 0, 0))
-    by_rows = lambda count: ((1, count, width), block, (blocks, count, width), BF16)
+    side = ((2, HEADS, 1, context, HD), lambda b: (0, 0, at(b), 0, 0))
     return kernel_call(
-        partial(finish_kernel, context, blocks),
-        (blocks,),
+        partial(finish_kernel, context, count),
+        (count,),
         [
-            ((1, rows, width), block),
-            ((HEADS, 1, rows, HD), lambda b: (0, b, 0, 0)),
+            ((1, rows, width), lambda b: (at(b), 0, 0)),
+            ((HEADS, 1, rows, HD), lambda b: (0, at(b), 0, 0)),
             side,
             side,
         ]
         + [((width, width), lambda b: (0, 0))] * 3,
-        [(None, pl.ANY, (rows, width), BF16)] * blocks + [by_rows(context), by_rows(context)],
-        [pltpu.VMEM((blocks, rows, width), BF16), pltpu.SemaphoreType.DMA((blocks,))],
-        2 * blocks * width * width * (rows + 2 * context),
-        6 * blocks * width * (rows + 2 * context),
+        [(None, pl.ANY, (rows, width), BF16)] * count,
+        [pltpu.VMEM((count, rows, width), BF16), pltpu.SemaphoreType.DMA((count,))],
+        2 * count * width * width * (rows + 2 * context),
+        6 * count * width * (rows + 2 * context),
         first_grad.reshape(blocks, rows, width),
         query_grad.reshape(HEADS, blocks, rows, HD),
         own.reshape(2, HEADS, blocks, context, HD),
@@ -730,69 +801,74 @@
     )
 
 
-def weigh_kernel(bit_ref, x_ref, query_ref, key_ref, value_ref, keep_ref, send_ref, sums, sending, left):
-    s = pl.program_id(0)
-    blocks, rows, width = x_ref.shape
-    context = key_ref.shape[1]
-    per = query_ref.shape[0]
-    columns = per * HD
-    x = x_ref[...].reshape(blocks * rows, width)
-    above = x_ref[:, :context].reshape(blocks * context, width)
-    query_grad = jnp.concatenate([query_ref[h] for h in range(per)], axis=1)
-    three = [dot(x, query_grad, 0, 0)]
-    for ref in (key_ref, value_ref):
-        three.append(dot(above, ref[...].reshape(blocks * context, columns), 0, 0))
-    steps = width // columns
-    for j in range(steps):
-
-        @pl.when(s == j)
-        def _(j=j):
-            for i, part in enumerate(three):
-                sums[i * width : (i + 1) * width, j * columns : (j + 1) * columns] = part
-
-    @pl.when(s == steps - 1)
+def unpack_kernel(counts, shares, place_ref, half_ref, *refs):
+    outs, (early, late, left) = refs[:7], refs[7:]
+    grad_query, grad_key, grad_value, grad_output, grad_inner, grad_outer, vectors = outs
+    first, second = shares
+    across, along = counts
+    share = first + second
+    for s in range(across):
+        for u in range(along):
+            at = (s * along + u) * share
+            number = (place_ref[1] ^ s) * along + (place_ref[2] ^ u)
+            early[pl.ds(pl.multiple_of(number * first, 16), first)] = half_ref[
+                at : at + first
+            ].astype(F32)
+            late[pl.ds(pl.multiple_of(number * second, 16), second)] = half_ref[
+                at + first : at + share
+            ].astype(F32)
+    width, hidden = grad_inner.shape
+    middle = late.shape[0] - width
+
+    def copy_out(pieces):
+        copies = [
+            pltpu.make_async_copy(source.at[pl.ds(start, size)], ref, left.at[j])
+            for j, (source, start, size, ref) in enumerate(pieces)
+        ]
+        for copy in copies:
+            copy.start()
+        for copy in copies:
+            copy.wait()
+
+    @pl.when(place_ref[0] == 0)
     def _():
-        bit = bit_ref[0]
-        half = sending.shape[0]
-        keep = pltpu.make_async_copy(
-            sums.at[pl.ds(pl.multiple_of(bit * half, 16), half)], keep_ref, left.at[0]
-        )
-        keep.start()
-        sending[...] = sums[pl.ds(pl.multiple_of((1 - bit) * half, 16), half)].astype(BF16)
-        send = pltpu.make_async_copy(sending, send_ref, left.at[1])
-        send.start()
-        keep.wait()
-        send.wait()
-
-
-def weigh(bit, x, query_grad, key_grad, value_grad, per=2):
-    blocks, rows, width = x.shape
-    context = key_grad.shape[1]
-    by_columns = ((blocks, context, per * HD), lambda s: (0, 0, s))
-    half = 3 * width // 2
+        pieces = [(late, 0, width, grad_query), (late, width, middle, grad_key.at[:middle])]
+        pieces.append((early, 0, width, grad_output))
+        for j in range(0, hidden, width):
+            pieces.append((early, width + j, width, grad_inner.at[:, pl.ds(j, width)]))
+        copy_out(pieces)
+
+    @pl.when(place_ref[0] == 1)
+    def _():
+        copy_out(
+            [
+                (late, 0, width - middle, grad_key.at[middle:]),
+                (late, width - middle, width, grad_value),
+                (early, 0, hidden, grad_outer),
+                (early, hidden, vectors.shape[0], vectors),
+            ]
+        )
+
+
+def unpack(places, half, counts, shares, hidden, into=()):
+    width = half.shape[1]
+    total = counts[0] * counts[1]
+    shapes = [(width, width)] * 4 + [(width, hidden), (hidden, width), (16, width)]
     return kernel_call(
-        weigh_kernel,
-        (HEADS // per,),
+        partial(unpack_kernel, counts, shares),
+        (1,),
+        [(None, pltpu.SMEM), (half.shape, lambda b: (0, 0))],
+        [(None, pl.ANY, shape, F32) for shape in shapes],
         [
-            (None, pltpu.SMEM),
-            (x.shape, lambda s: (0, 0, 0)),
-            ((per, blocks * rows, HD), lambda s: (s, 0, 0)),
-            by_columns,
-            by_columns,
+            pltpu.VMEM((total * shares[0], width), F32),
+            pltpu.VMEM((total * shares[1], width), F32),
+            pltpu.SemaphoreType.DMA((3 + hidden // width,)),
         ],
-        [(None, pl.ANY, (half, width), F32), (None, pl.ANY, (half, width), BF16)],
-        [
-            pltpu.VMEM((3 * width, width), F32),
-            pltpu.VMEM((half, width), BF16),
-            pltpu.SemaphoreType.DMA((2,)),
-        ],
-        2 * blocks * width * width * (rows + 2 * context),
-        4 * blocks * width * (rows + context),
-        bit,
-        x,
-        query_grad,
-        key_grad,
-        value_grad,
+        0,
+        6 * half.size,
+        places,
+        half,
+        into=into,
     )
 
 
@@ -816,27 +892,24 @@
             array, AXES, [(number(g, c), number(*move(g, c, s))) for g, c in places]
         )
 
-    def reduce_pieces(stage, part):
+    def reduce_pieces(stage, parts):
         count, index, _ = stage
-        piece = part.shape[0] // count
-        take = lambda s: lax.dynamic_slice_in_dim(part, (index ^ s) * piece, piece)
+        piece = parts[0].shape[0] // count
+
+        def take(s):
+            at = (index ^ s) * piece
+            return sum(lax.dynamic_slice_in_dim(part, at, piece).astype(F32) for part in parts)
+
         return [take(0)] + [take(s).astype(BF16) for s in range(1, count)]
 
     def reduce_join(stage, own, came):
-        return sum((array.astype(F32) for array in came), own)
+        return [own, *came]
 
     def gather_pieces(stage, part):
         return [part.astype(BF16)] * stage[0]
 
     def gather_join(stage, own, came):
-        count, index, _ = stage
-        shares = [own] + came
-        step = 1
-        while step < count:
-            turned = (index // step) % 2 == 1
-            shares = [jnp.where(turned, shares[s ^ step], shares[s]) for s in range(count)]
-            step *= 2
-        return jnp.concatenate(shares)
+        return jnp.concatenate([own] + came)
 
     def send(stage, pieces):
         return [swap(piece, stage[2], s) for s, piece in enumerate(pieces) if s]
@@ -847,7 +920,7 @@
     ] + [
         (partial(gather_pieces, stage), partial(send, stage), partial(gather_join, stage))
         for stage in reversed(stages)
-    ]
+    ], stages
 
 
 def gathered_plan(
@@ -875,7 +948,7 @@
     slots = QUERIES // members
 
     far = blocks // 2
-    order = [r for r in range(blocks) if r != far] + [far]
+    order = [r for r in range(1, blocks) if r != far] + [0, far]
 
     def route(r, back=False):
         pairs = []
@@ -943,9 +1016,11 @@
     bit = lax.rem(lax.axis_index("grp"), 2).astype(jnp.int32).reshape(1)
     out, first_grad, grads, delta, keep, given = dense(bit, x, cots, attended, totals, weights)
 
-    stages = summing(groups, members)
+    stages, stages_of = summing(groups, members)
     scale_k = 1.0 / log2e
     chunk = blocks * context // 2
+
+    added = lambda parts: sum(part.astype(F32) for part in parts)
 
     def start(stage, part):
         pieces_of, send, join = stage
@@ -957,74 +1032,81 @@
     home = [homeward(out[j], r) for j, r in enumerate(order[:-1])]
     kv_other, dq = attention_backward(q, grads, delta, p, k, v, scale_k, 1.0, chunk, 2, 2)
     *home, came, kv_other, grads = tie(*home, came, kv_other, grads)
-    early = keep + came.astype(F32)
-
-    pieces, send, join = start(stages[1], early)
+    pieces, send, early_join = start(stages[1], [keep, came])
     *pieces, kv_other, far_out, grads = tie(*pieces, kv_other, out[-1], grads)
     kv_came = lax.ppermute(kv_other, AXES, across)
-    came = send(pieces)
+    early_came = send(pieces)
     home.append(homeward(far_out, far))
     kv_own, dq = attention_backward(q, grads, delta, p, k, v, scale_k, scale, chunk, 0, 2, dq)
-    *came, home[-1], kv_came, kv_own = tie(*came, home[-1], kv_came, kv_own)
-    early = join(came)
-
-    pieces, send, join = start(stages[2], early)
-    *pieces, kv_own = tie(*pieces, kv_own)
+    *early_came, home[-1], kv_came, kv_own = tie(*early_came, home[-1], kv_came, kv_own)
+
+    token_of = lambda places, after: finish(
+        places, after, kv_own, kv_came, dq, kinds, blocks
+    )
+    three = token_of([1], first_grad)[0]
+    three, first_grad = tie(three, first_grad)
+    three = homeward(three, order[1])
+    one, two = token_of([2, 0], first_grad)
+    one, two, x = tie(one, two, x)
+    keep, given = weigh(bit, x, dq, kv_own, kv_came)
+    three, given, first_grad = tie(three, given, first_grad)
+    came = lax.ppermute(given, AXES, across)
+    last = token_of([3], first_grad)[0]
+    came, last = tie(came, last)
+
+    pieces, send, join = start(stages[1], [keep, came])
+    *pieces, two = tie(*pieces, two)
     came = send(pieces)
-    *token_grad, key_grad, value_grad = finish(first_grad, kv_own, kv_came, dq, kinds, blocks)
-    ready = tie(*came, *token_grad)
-    came, token_grad = list(ready[: len(came)]), ready[len(came) :]
-    early = join(came)
-
-    *token_grad, x = tie(*token_grad, x)
-    back = [homeward(token_grad[j], order[j]) for j in range(blocks - 2)]
-    keep, given = weigh(bit, x, dq, key_grad, value_grad)
-    *back, given, token_three = tie(*back, given, token_grad[-2])
-    came = lax.ppermute(given, AXES, across)
-    back.append(homeward(token_three, order[-2]))
-    late = keep + came.astype(F32)
-    pieces, send, join = start(stages[1], late)
-    late = join(send(pieces))
-    pieces, send, join = start(stages[2], late)
+    two = homeward(two, order[0])
+    *came, two = tie(*came, two)
+    late = added(join(came))
+    early = added(early_join(early_came))
+
+    along = members // 2
+    shares = (early.shape[0] // along, late.shape[0] // along)
+    both = jnp.concatenate(
+        [early.reshape(along, shares[0], width), late.reshape(along, shares[1], width)], axis=1
+    ).reshape(-1, width)
+    pieces, send, join = start(stages[2], [both])
     came = send(pieces)
-    *came, back[-1] = tie(*came, back[-1])
-    late = join(came)
-    shares = (early.shape[0], late.shape[0])
-    both = jnp.concatenate([early, late])
+    grad_tokens = jnp.zeros((blocks, rows, width), F32)
+    grad_tokens = put(grad_tokens, three.astype(F32), order[1])
+    *came, grad_tokens, one = tie(*came, grad_tokens, one)
+    both = added(join(came))
+
     pieces, send, join = start(stages[3], both)
-    both = join(send(pieces))
+    *home, live, one, pieces[0] = tie(*home, live, one, pieces[0])
+    came = send(pieces)
+    one = homeward(one, order[2])
+    grad_tokens = put(grad_tokens, two.astype(F32), order[0])
+    *came, one, grad_tokens = tie(*came, one, grad_tokens)
+    both = join(came)
+
     pieces, send, join = start(stages[4], both)
-    *pieces, token_far = tie(*pieces, token_grad[-1])
+    *pieces, last = tie(*pieces, last)
     came = send(pieces)
-    went = homeward(token_far, far)
-    *home, live, came[0] = tie(*home, live, came[0])
+    last = homeward(last, far)
+    grad_tokens = put(grad_tokens, one.astype(F32), order[2])
     layer_out = jnp.zeros((blocks, rows, width), BF16)
-    grad_tokens = jnp.zeros((blocks, rows, width), F32)
     for block, r in zip(home, order, strict=True):
         layer_out = put(layer_out, jnp.where(block_of(live, r), block, 0).astype(BF16), r)
-    for block, r in zip(back, order, strict=False):
-        grad_tokens = put(grad_tokens, block.astype(F32), r)
-    *came, went = tie(*came, went)
+    *came, last, layer_out, grad_tokens = tie(*came, last, layer_out, grad_tokens)
     both = join(came)
-    pieces, send, join = start(stages[5], both)
-    both = join(send(pieces)).reshape(-1, sum(shares), width)
-    early = both[:, : shares[0]].reshape(-1, width).astype(F32)
-    late = both[:, shares[0] :].reshape(-1, width).astype(F32)
-    grad_tokens = put(grad_tokens, went.astype(F32), far)
-
     hidden = inner_weight.shape[1]
-    inner_at = [early[at : at + width] for at in range(width, width + hidden, width)]
-    vectors = early[width + 2 * hidden :]
+    counts = (groups, members // 2)
+    mine = [index.astype(jnp.int32) for _, index, _ in stages_of]
+    came = lax.ppermute(both, AXES, across)
+    sums = unpack(jnp.stack(mine), both, counts, shares, hidden)
+    grad_tokens = put(grad_tokens, last.astype(F32), far)
+    came, grad_tokens, *sums = tie(came, grad_tokens, *sums)
+    theirs = jnp.stack([1 - mine[0], *mine[1:]])
+    *sums, vectors = unpack(theirs, came, counts, shares, hidden, sums)
     return (
         layer_out,
         grad_tokens,
-        late[:width],
-        late[width : 2 * width],
-        late[2 * width :],
-        early[:width],
-        jnp.concatenate(inner_at, axis=1),
+        *sums[:5],
         vectors[5 : 5 + hidden // width].reshape(hidden),
-        early[width + hidden : width + 2 * hidden],
+        sums[5],
         vectors[4],
         vectors[0],
         vectors[1],

time: 396 us -> 389 us (0.982)
  starting transfers between devices: 66.2 us -> 51.1 us
  Pallas kernels: 200 us -> 212 us
  local copies, waits for them, and re-layouts: 22.7 us -> 16.2 us
    pallas_call x10 -> x14, Pallas kernels: 200 us -> 212 us  [kernel_call(): pl.pallas_call(run, grid=grid, in_specs=[pl.BlockSpec(memory_space=index)...]
    ppermute x19 -> x15, waiting for transfers between devices: 34.7 us -> 24.9 us  [swap(): lax.ppermute(array, AXES, [(number(g, c), number(*move(g, c, s))) for g,...]
    ppermute x3, starting transfers between devices: 11 us -> 1.69 us  [gathered_plan(): other = [lax.ppermute(block, AXES, across) for block in own]]
    ppermute x8, waiting for transfers between devices: 23.5 us -> 32.3 us  [outward(): return lax.ppermute(block, AXES, route(r))]
    dynamic_update_slice x8, other arithmetic: 1.27 us -> 9.58 us  [put(): lax.dynamic_update_index_in_dim(whole, block, lax.rem(place + r, blocks), 0)]
    ppermute x19 -> x15, starting transfers between devices: 27.3 us -> 20.3 us  [swap(): lax.ppermute(array, AXES, [(number(g, c), number(*move(g, c, s))) for g,...]
    select_n x4 -> x0, other arithmetic: 6.77 us -> none  [gather_join(): jnp.where(turned, shares[s ^ step], shares[s])]
    ppermute x8, waiting for transfers between devices: 18.8 us -> 25.5 us  [homeward(): return lax.ppermute(block, AXES, route(r, True))]
  transfers between devices with their start and end apart: 42 -> 39, of which waited for: 17 -> 10; matrix products, arithmetic and copies ran while one was open for 2% -> 5% of each run, Pallas kernels for 41% -> 42%
where the time goes in v3:
time: 389 us; the launch traced here: 383 us
  Pallas kernels  212 us (54%)
  waiting for transfers between devices  82.7 us (21%)
  starting transfers between devices  51.1 us (13%)
  other arithmetic  18.7 us (5%)
  local copies, waits for them, and re-layouts  16.2 us (4%)
    pallas_call x14, Pallas kernels, kernel_call(): pl.pallas_call(run, grid=grid, in_specs=[pl.BlockSpec(memory_space=index)...  212 us
    ppermute x8, waiting for transfers between devices, outward(): return lax.ppermute(block, AXES, route(r))  32.3 us
    ppermute x8, waiting for transfers between devices, homeward(): return lax.ppermute(block, AXES, route(r, True))  25.5 us
    ppermute x15, waiting for transfers between devices, swap(): lax.ppermute(array, AXES, [(number(g, c), number(*move(g, c, s))) for g,...  24.9 us
    ppermute x15, starting transfers between devices, swap(): lax.ppermute(array, AXES, [(number(g, c), number(*move(g, c, s))) for g,...  20.3 us
    ppermute x8, starting transfers between devices, homeward(): return lax.ppermute(block, AXES, route(r, True))  16.2 us
    ppermute x8, starting transfers between devices, outward(): return lax.ppermute(block, AXES, route(r))  12.4 us
    dynamic_update_slice x8, other arithmetic, put(): lax.dynamic_update_index_in_dim(whole, block, lax.rem(place + r, blocks), 0)  9.58 us
  transfers between devices with their start and end apart: 39, of which 10 were waited for; matrix products, arithmetic and copies ran while one was open for 5% of the time, Pallas kernels for 42%

profile of v3, /device:TPU:0, one launch (start us, length us, event | category | flops | bytes accessed | tf_op | source)
XLA Modules:
  0.0 382.7 jit_solution(886091841561769105)
XLA Ops:
  8.3 12.1 %collective-permute-done.5.refs_0_ = bf16[528,512]{1,0:T(8,128)(2,1)} collective-permute-done((bf16[528,512]{1,0:T(8,128)(2,1)S(1)}, bf16[528,512]{1,0:T(8,128)(2,1)}, u32[]{:S(2)}, u32[]{:S(2)}) %collective-permute-start.5) | collective-permute-done | bytes 540704 | tf_op jit(solution)/shard_map/ppermute | solution.py:970
  21.6 10.7 %collective-permute-done.3.refs_0_ = bf16[528,512]{1,0:T(8,128)(2,1)} collective-permute-done((bf16[528,512]{1,0:T(8,128)(2,1)S(1)}, bf16[528,512]{1,0:T(8,128)(2,1)}, u32[]{:S(2)}, u32[]{:S(2)}) %collective-permute-start.3) | collective-permute-done | bytes 540704 | tf_op jit(solution)/shard_map/ppermute | solution.py:970
  34.3 4.9 %shard_map.254 = (bf16[4,2112,128]{2,1,0:T(8,128)(2,1)}, bf16[4,2,4,512,128]{4,3,2,1,0:T(8,128)(2,1)}, bf16[4,2,4,512,128]{4,3,2,1,0:T(8,128)(2,1)}, bf16[4,528,512]{2,1,0:T(8,128)(2,1)}) custom-call(bf16[528,512]{1,0:T(8,128)(2,1)} %collective-permute-done.5.refs_0_, bf16[528,512]{1,0:T(8,128)(2,1)} %copy-done.25, bf16[512,512]{1,0:T(8,128)(2,1)} %refs_4_.15, ...), custom_call_target="tpu_custom_call" | custom-call | flops 1350565888 | bytes 4227072 | tf_op jit(solution)/shard_map/pallas_call | solution.py:291
  40.0 4.9 %shard_map.255 = (bf16[4,2112,128]{2,1,0:T(8,128)(2,1)}, bf16[4,2,4,512,128]{4,3,2,1,0:T(8,128)(2,1)}, bf16[4,2,4,512,128]{4,3,2,1,0:T(8,128)(2,1)}, bf16[4,528,512]{2,1,0:T(8,128)(2,1)}) custom-call(bf16[528,512]{1,0:T(8,128)(2,1)} %collective-permute-done.3.refs_0_, ...), custom_call_target="tpu_custom_call", output_to_operand_aliasing={{0}: (5, {}), {1}: (6, {}), {2}: (7, {}), {3}: (8, {})} | custom-call | flops 1350565888 | bytes 4227072 | tf_op jit(solution)/shard_map/pallas_call | solution.py:291
  45.8 5.1 %shard_map.256 = (bf16[4,2112,128]{2,1,0:T(8,128)(2,1)}, bf16[4,2,4,512,128]{4,3,2,1,0:T(8,128)(2,1)}, bf16[4,2,4,512,128]{4,3,2,1,0:T(8,128)(2,1)}, bf16[4,528,512]{2,1,0:T(8,128)(2,1)}) custom-call(bf16[528,512]{1,0:T(8,128)(2,1)} %copy-done.12, ...), custom_call_target="tpu_custom_call", output_to_operand_aliasing={{0}: (5, {}), {1}: (6, {}), {2}: (7, {}), {3}: (8, {})} | custom-call | flops 1350565888 | bytes 4227072 | tf_op jit(solution)/shard_map/pallas_call | solution.py:291
  50.8 9.5 %collective-permute-done.refs_0_ = bf16[528,512]{1,0:T(8,128)(2,1)} collective-permute-done((bf16[528,512]{1,0:T(8,128)(2,1)S(1)}, bf16[528,512]{1,0:T(8,128)(2,1)}, u32[]{:S(2)}, u32[]{:S(2)}) %collective-permute-start) | collective-permute-done | bytes 540704 | tf_op jit(solution)/shard_map/ppermute | solution.py:970
  65.5 4.9 %shard_map.257 = (bf16[4,2112,128]{2,1,0:T(8,128)(2,1)}, bf16[4,2,4,512,128]{4,3,2,1,0:T(8,128)(2,1)}, bf16[4,2,4,512,128]{4,3,2,1,0:T(8,128)(2,1)}, bf16[4,528,512]{2,1,0:T(8,128)(2,1)}) custom-call(bf16[528,512]{1,0:T(8,128)(2,1)} %collective-permute-done.refs_0_, ...), custom_call_target="tpu_custom_call", output_to_operand_aliasing={{0}: (5, {}), {1}: (6, {}), {2}: (7, {}), {3}: (8, {})} | custom-call | flops 1350565888 | bytes 4227072 | tf_op jit(solution)/shard_map/pallas_call | solution.py:291
  70.4 3.8 collective-permute-start.9
  76.3 52.0 %shard_map.258 = (bf16[4,2112,4096]{2,1,0:T(8,128)(2,1)}, f32[2112,512]{1,0:T(8,128)}, f32[4,2112,128]{2,1,0:T(8,128)}) custom-call(bf16[4,2112,128]{2,1,0:T(8,128)(2,1)} %get-tuple-element.176.refs_0_, bf16[4,4096,128]{2,1,0:T(8,128)(2,1)} %bitcast.64, bf16[4,4096,128]{2,1,0:T(8,128)(2,1)} %bitcast.67), custom_call_target="tpu_custom_call" | custom-call | flops 35433480192 | bytes 69206016 | tf_op jit(solution)/shard_map/pallas_call | solution.py:291
  129.3 36.8 %shard_map.259 = (bf16[528,512]{1,0:T(8,128)(2,1)}, bf16[528,512]{1,0:T(8,128)(2,1)}, bf16[528,512]{1,0:T(8,128)(2,1)}, bf16[528,512]{1,0:T(8,128)(2,1)}, bf16[2...) custom-call(s32[1]{0:T(128)} %bitcast.refs_0_, ...), custom_call_target="tpu_custom_call" | custom-call | flops 16609443840 | bytes 45088768 | tf_op jit(solution)/shard_map/pallas_call | solution.py:291
  168.1 5.8 %collective-permute-start.14 = (bf16[528,512]{1,0:T(8,128)(2,1)}, bf16[528,512]{1,0:T(8,128)(2,1)}, u32[]{:S(2)}, u32[]{:S(2)}) collective-permute-start(bf16[528,512]{1,0:T(8,128)(2,1)} %get-tuple-element.199), channel_id=1, source_target_pairs={{0,0},{8,1},{2,2},{10,3},{4,4},{12,5},{6,6},{14,7},{1,8},{9,9},{3,... | collective-permute-start | bytes 1622024 | tf_op jit(solution)/shard_map/ppermute | solution.py:973
  174.1 36.7 %shard_map.260 = (bf16[2,4,2048,128]{3,2,1,0:T(8,128)(2,1)}, f32[4,2112,128]{2,1,0:T(8,128)}) custom-call(bf16[4,2112,128]{2,1,0:T(8,128)(2,1)} %get-tuple-element.176.refs_0_, bf16[4,2112,128]{2,1,0:T(8,128)(2,1)} %get-tuple-element.214.refs_1_, f32[4,2112,128]{2,1,0:T(8,128)} %get-tuple-element.202.refs_2_, ...), custom_call_target="tpu_custom_call" | custom-call | flops 26575110144 | bytes 34603008 | tf_op jit(solution)/shard_map/pallas_call | solution.py:291
  220.6 36.5 %shard_map.261 = (bf16[2,4,2048,128]{3,2,1,0:T(8,128)(2,1)}, bf16[4,2112,128]{2,1,0:T(8,128)(2,1)}) custom-call(bf16[4,2112,128]{2,1,0:T(8,128)(2,1)} %get-tuple-element.176.refs_0_, bf16[4,2112,128]{2,1,0:T(8,128)(2,1)} %get-tuple-element.214.refs_1_, f32[4,2112,128]{2,1,0:T(8,128)} %get-tuple-element.202.refs_2_, ...), custom_call_target="tpu_custom_call" | custom-call | flops 26575110144 | bytes 34603008 | tf_op jit(solution)/shard_map/pallas_call | solution.py:291
  257.1 4.3 %shard_map.262 = bf16[528,512]{1,0:T(8,128)(2,1)} custom-call(bf16[4,528,512]{2,1,0:T(8,128)(2,1)} %bitcast.74, bf16[4,4,528,128]{3,2,1,0:T(8,128)(2,1)} %bitcast.70, bf16[2,4,4,512,128]{4,3,2,1,0:T(8,128)(2,1)} %bitcast.61, bf16[2,4,4,512,128]{4,3,2,1,0:T(8,128)(2,1)} %bitcast.16.refs_3_, bf16[512,512]{1,0:T(8,128)(2,1)} %refs_4_.15, ...), custom_call_target="tpu_custom_call" | custom-call | flops 813694976 | bytes 4767744 | tf_op jit(solution)/shard_map/pallas_call | solution.py:291
  261.5 5.5 %shard_map.263 = (bf16[528,512]{1,0:T(8,128)(2,1)}, bf16[528,512]{1,0:T(8,128)(2,1)}) custom-call(bf16[4,528,512]{2,1,0:T(8,128)(2,1)} %bitcast.75, bf16[4,4,528,128]{3,2,1,0:T(8,128)(2,1)} %bitcast.71, bf16[2,4,4,512,128]{4,3,2,1,0:T(8,128)(2,1)} %bitcast.62, bf16[2,4,4,512,128]{4,3,2,1,0:T(8,128)(2,1)} %bitcast.16.refs_3_, bf16[512,512]{1,0:T(8,128)(2,1)} %refs_4_.15, ...), custom_call_target="tpu_custom_call" | custom-call | flops 1627389952 | bytes 9535488 | tf_op jit(solution)/shard_map/pallas_call | solution.py:291
  267.0 8.7 %shard_map.264 = (f32[768,512]{1,0:T(8,128)}, bf16[768,512]{1,0:T(8,128)(2,1)}) custom-call(s32[1]{0:T(128)} %bitcast.refs_0_, bf16[4,528,512]{2,1,0:T(8,128)(2,1)} %get-tuple-element.227.refs_1_, bf16[4,2112,128]{2,1,0:T(8,128)(2,1)} %get-tuple-element.221.refs_2_, bf16[2,4,2048,128]{3,2,1,0:T(8,128)(2,1)} %get-tuple-element.222.refs_3_, ...), custom_call_target="tpu_custom_call" | custom-call | flops 3254779904 | bytes 12713984 | tf_op jit(solution)/shard_map/pallas_call | solution.py:291
  278.4 4.1 %shard_map.265 = bf16[528,512]{1,0:T(8,128)(2,1)} custom-call(bf16[4,528,512]{2,1,0:T(8,128)(2,1)} %bitcast.76, bf16[4,4,528,128]{3,2,1,0:T(8,128)(2,1)} %bitcast.72, bf16[2,4,4,512,128]{4,3,2,1,0:T(8,128)(2,1)} %bitcast.63, bf16[2,4,4,512,128]{4,3,2,1,0:T(8,128)(2,1)} %bitcast.16.refs_3_, bf16[512,512]{1,0:T(8,128)(2,1)} %refs_4_.15, ...), custom_call_target="tpu_custom_call" | custom-call | flops 813694976 | bytes 4767744 | tf_op jit(solution)/shard_map/pallas_call | solution.py:291
  291.5 7.2 %collective-permute-done.23 = bf16[192,512]{1,0:T(8,128)(2,1)S(1)} collective-permute-done((bf16[192,512]{1,0:T(8,128)(2,1)}, bf16[192,512]{1,0:T(8,128)(2,1)S(1)}, u32[]{:S(2)}, u32[]{:S(2)}) %collective-permute-start.23) | collective-permute-done | bytes 196640 | tf_op jit(solution)/shard_map/ppermute | solution.py:891
  298.7 6.3 %collective-permute-done.25 = bf16[192,512]{1,0:T(8,128)(2,1)S(1)} collective-permute-done((bf16[192,512]{1,0:T(8,128)(2,1)}, bf16[192,512]{1,0:T(8,128)(2,1)S(1)}, u32[]{:S(2)}, u32[]{:S(2)}) %collective-permute-start.25) | collective-permute-done | bytes 196640 | tf_op jit(solution)/shard_map/ppermute | solution.py:891
  306.7 4.1 %collective-permute-start.29 = (bf16[144,512]{1,0:T(8,128)(2,1)S(1)}, bf16[144,512]{1,0:T(8,128)(2,1)S(1)}, u32[]{:S(2)}, u32[]{:S(2)}) collective-permute-start(bf16[144,512]{1,0:T(8,128)(2,1)S(1)} %get-tuple-element.320), channel_id=1, source_target_pairs={{0,6},{1,7},{2,4},{3,5},{4,2},{5,3},{6,0},{7,1},{8,14},{9,15},{10,... | collective-permute-start | bytes 442376 | tf_op jit(solution)/shard_map/ppermute | solution.py:891
  315.6 4.8 %collective-permute-done.28 = bf16[144,512]{1,0:T(8,128)(2,1)S(1)} collective-permute-done((bf16[144,512]{1,0:T(8,128)(2,1)S(1)}, bf16[144,512]{1,0:T(8,128)(2,1)S(1)}, u32[]{:S(2)}, u32[]{:S(2)}) %collective-permute-start.28) | collective-permute-done | bytes 147488 | tf_op jit(solution)/shard_map/ppermute | solution.py:891
  342.3 22.8 %collective-permute-done.37 = bf16[528,512]{1,0:T(8,128)(2,1)S(1)} collective-permute-done((bf16[528,512]{1,0:T(8,128)(2,1)S(1)}, bf16[528,512]{1,0:T(8,128)(2,1)S(1)}, u32[]{:S(2)}, u32[]{:S(2)}) %collective-permute-start.37) | collective-permute-done | bytes 540704 | tf_op jit(solution)/shard_map/ppermute | solution.py:973
  370.4 4.2 %shard_map.266 = (f32[512,512]{1,0:T(8,128)}, f32[512,512]{1,0:T(8,128)}, f32[512,512]{1,0:T(8,128)}, f32[512,512]{1,0:T(8,128)}, f32[512,1024]{1,0:T(8,128)}, /*index=5*/f32[1024,512]{1,0:T(8,128)}, f32[16,512]{1,0:T(8,128)}) custom-call(s32[3]{0:T(128)} %get-tuple-element.328.refs_0_, bf16[2304,512]{1,0:T(8,128)(2,1)} %copy-done.1), custom_call_target="tpu_custom_call" | custom-call | bytes 7077888 | tf_op jit(solution)/shard_map/pallas_call | solution.py:291
  375.7 3.9 %shard_map.267 = (f32[512,512]{1,0:T(8,128)}, f32[512,512]{1,0:T(8,128)}, f32[512,512]{1,0:T(8,128)}, f32[512,512]{1,0:T(8,128)}, f32[512,1024]{1,0:T(8,128)}, /*index=5*/f32[1024,512]{1,0:T(8,128)}, f32[16,512]{1,0:T(8,128)}) custom-call(s32[3]{0:T(128)} %get-tuple-element.329.refs_0_, ...), custom_call_target="tpu_custom_call", output_to_operand_aliasing={{0}: (2, {}), {1}: (3, {}), {2}: (4, {}), {3}: (5, {}), {4}... | custom-call | bytes 7077888 | tf_op jit(solution)/shard_map/pallas_call | solution.py:291
  (162 shorter events, 81.5 us)
Async XLA Ops:
  2.5 17.9 %collective-permute-start.5 = (bf16[528,512]{1,0:T(8,128)(2,1)S(1)}, bf16[528,512]{1,0:T(8,128)(2,1)}, u32[]{:S(2)}, u32[]{:S(2)}) collective-permute-start(bf16[528,512]{1,0:T(8,128)(2,1)S(1)} %get-tuple-element.316), channel_id=1, source_target_pairs={{0,2},{1,10},{2,4},{3,12},{4,6},{5,14},{6,0},{7,8},{8,3},{9,11},{1... | collective-permute-start | bytes 1622024 | tf_op jit(solution)/shard_map/ppermute | solution.py:970
  5.5 26.7 %collective-permute-start.3 = (bf16[528,512]{1,0:T(8,128)(2,1)S(1)}, bf16[528,512]{1,0:T(8,128)(2,1)}, u32[]{:S(2)}, u32[]{:S(2)}) collective-permute-start(bf16[528,512]{1,0:T(8,128)(2,1)S(1)} %get-tuple-element.319), channel_id=1, source_target_pairs={{0,6},{1,14},{2,0},{3,8},{4,2},{5,10},{6,4},{7,12},{8,7},{9,15},{1... | collective-permute-start | bytes 1622024 | tf_op jit(solution)/shard_map/ppermute | solution.py:970
  7.6 24.7 %collective-permute-start.1 = (bf16[528,512]{1,0:T(8,128)(2,1)S(1)}, bf16[528,512]{1,0:T(8,128)(2,1)S(1)}, u32[]{:S(2)}, u32[]{:S(2)}) collective-permute-start(bf16[528,512]{1,0:T(8,128)(2,1)S(1)} %get-tuple-element.317), channel_id=1, source_target_pairs={{0,0},{1,8},{2,2},{3,10},{4,4},{5,12},{6,6},{7,14},{8,1},{9,9},{10... | collective-permute-start | bytes 1622024 | tf_op jit(solution)/shard_map/ppermute | solution.py:970
  32.8 27.5 %collective-permute-start = (bf16[528,512]{1,0:T(8,128)(2,1)S(1)}, bf16[528,512]{1,0:T(8,128)(2,1)}, u32[]{:S(2)}, u32[]{:S(2)}) collective-permute-start(bf16[528,512]{1,0:T(8,128)(2,1)S(1)} %get-tuple-element.318), channel_id=1, source_target_pairs={{0,4},{1,12},{2,6},{3,14},{4,0},{5,8},{6,2},{7,10},{8,5},{9,13},{1... | collective-permute-start | bytes 1622024 | tf_op jit(solution)/shard_map/ppermute | solution.py:970
  70.4 57.9 %collective-permute-start.8 = (bf16[528,512]{1,0:T(8,128)(2,1)S(1)}, bf16[528,512]{1,0:T(8,128)(2,1)S(1)}, u32[]{:S(2)}, u32[]{:S(2)}) collective-permute-start(bf16[528,512]{1,0:T(8,128)(2,1)S(1)} %get-tuple-element.181), channel_id=1, source_target_pairs={{0,2},{1,10},{2,4},{3,12},{4,6},{5,14},{6,0},{7,8},{8,3},{9,11},{1... | collective-permute-start | bytes 1622024 | tf_op jit(solution)/shard_map/ppermute | solution.py:970
  70.4 57.9 %collective-permute-start.9 = (bf16[528,512]{1,0:T(8,128)(2,1)S(1)}, bf16[528,512]{1,0:T(8,128)(2,1)S(1)}, u32[]{:S(2)}, u32[]{:S(2)}) collective-permute-start(bf16[528,512]{1,0:T(8,128)(2,1)S(1)} %get-tuple-element.182), channel_id=1, source_target_pairs={{0,6},{1,14},{2,0},{3,8},{4,2},{5,10},{6,4},{7,12},{8,7},{9,15},{1... | collective-permute-start | bytes 1622024 | tf_op jit(solution)/shard_map/ppermute | solution.py:970
  74.2 54.1 %collective-permute-start.10 = (bf16[528,512]{1,0:T(8,128)(2,1)S(1)}, bf16[528,512]{1,0:T(8,128)(2,1)}, u32[]{:S(2)}, u32[]{:S(2)}) collective-permute-start(bf16[528,512]{1,0:T(8,128)(2,1)S(1)} %get-tuple-element.183), channel_id=1, source_target_pairs={{0,0},{1,8},{2,2},{3,10},{4,4},{5,12},{6,6},{7,14},{8,1},{9,9},{10... | collective-permute-start | bytes 1622024 | tf_op jit(solution)/shard_map/ppermute | solution.py:970
  76.2 52.2 %collective-permute-start.11 = (bf16[528,512]{1,0:T(8,128)(2,1)S(1)}, bf16[528,512]{1,0:T(8,128)(2,1)}, u32[]{:S(2)}, u32[]{:S(2)}) collective-permute-start(bf16[528,512]{1,0:T(8,128)(2,1)S(1)} %get-tuple-element.184), channel_id=1, source_target_pairs={{0,4},{1,12},{2,6},{3,14},{4,0},{5,8},{6,2},{7,10},{8,5},{9,13},{1... | collective-permute-start | bytes 1622024 | tf_op jit(solution)/shard_map/ppermute | solution.py:970
  166.1 44.7 %collective-permute-start.12 = (bf16[528,512]{1,0:T(8,128)(2,1)}, bf16[528,512]{1,0:T(8,128)(2,1)}, u32[]{:S(2)}, u32[]{:S(2)}) collective-permute-start(bf16[528,512]{1,0:T(8,128)(2,1)} %get-tuple-element.197), channel_id=1, source_target_pairs={{2,0},{10,1},{4,2},{12,3},{6,4},{14,5},{0,6},{8,7},{3,8},{11,9},{5... | collective-permute-start | bytes 1622024 | tf_op jit(solution)/shard_map/ppermute | solution.py:973
  166.6 44.1 %collective-permute-start.13 = (bf16[528,512]{1,0:T(8,128)(2,1)}, bf16[528,512]{1,0:T(8,128)(2,1)S(1)}, u32[]{:S(2)}, u32[]{:S(2)}) collective-permute-start(bf16[528,512]{1,0:T(8,128)(2,1)} %get-tuple-element.198), channel_id=1, source_target_pairs={{6,0},{14,1},{0,2},{8,3},{2,4},{10,5},{4,6},{12,7},{7,8},{15,9},{1... | collective-permute-start | bytes 1622024 | tf_op jit(solution)/shard_map/ppermute | solution.py:973
  168.1 42.6 %collective-permute-start.14 = (bf16[528,512]{1,0:T(8,128)(2,1)}, bf16[528,512]{1,0:T(8,128)(2,1)}, u32[]{:S(2)}, u32[]{:S(2)}) collective-permute-start(bf16[528,512]{1,0:T(8,128)(2,1)} %get-tuple-element.199), channel_id=1, source_target_pairs={{0,0},{8,1},{2,2},{10,3},{4,4},{12,5},{6,6},{14,7},{1,8},{9,9},{3,... | collective-permute-start | bytes 1622024 | tf_op jit(solution)/shard_map/ppermute | solution.py:973
  173.9 36.9 %collective-permute-start.15 = (bf16[1536,512]{1,0:T(8,128)(2,1)}, bf16[1536,512]{1,0:T(8,128)(2,1)}, u32[]{:S(2)}, u32[]{:S(2)}) collective-permute-start(bf16[1536,512]{1,0:T(8,128)(2,1)} %get-tuple-element.200), channel_id=1, source_target_pairs={{0,8},{1,9},{2,10},{3,11},{4,12},{5,13},{6,14},{7,15},{8,0},{9,1},... | collective-permute-start | bytes 4718600 | tf_op jit(solution)/shard_map/ppermute | solution.py:1031
  213.4 43.6 %collective-permute-start.20 = (bf16[2,4,2048,128]{3,2,1,0:T(8,128)(2,1)}, bf16[2,4,2048,128]{3,2,1,0:T(8,128)(2,1)}, u32[]{:S(2)}, u32[]{:S(2)}) collective-permute-start(bf16[2,4,2048,128]{3,2,1,0:T(8,128)(2,1)} %get-tuple-element.213), channel_id=1, source_target_pairs={{0,8},{1,9},{2,10},{3,11},{4,12},{5,13},{6,14},{7,15},{8,0},{9,1},... | collective-permute-start | bytes 12582920 | tf_op jit(solution)/shard_map/ppermute | solution.py:1037
  213.8 43.2 %collective-permute-start.16 = (bf16[384,512]{1,0:T(8,128)(2,1)}, bf16[384,512]{1,0:T(8,128)(2,1)S(1)}, u32[]{:S(2)}, u32[]{:S(2)}) collective-permute-start(bf16[384,512]{1,0:T(8,128)(2,1)} %get-tuple-element.209), channel_id=1, source_target_pairs={{0,1},{1,0},{2,3},{3,2},{4,5},{5,4},{6,7},{7,6},{8,9},{9,8},{10,11... | collective-permute-start | bytes 1179656 | tf_op jit(solution)/shard_map/ppermute | solution.py:891
  215.1 41.9 %collective-permute-start.17 = (bf16[384,512]{1,0:T(8,128)(2,1)}, bf16[384,512]{1,0:T(8,128)(2,1)}, u32[]{:S(2)}, u32[]{:S(2)}) collective-permute-start(bf16[384,512]{1,0:T(8,128)(2,1)} %get-tuple-element.210), channel_id=1, source_target_pairs={{0,16},{1,17},{2,18},{3,19},{4,20},{5,21},{6,22},{7,23},{8,24},{9,... | collective-permute-start | bytes 1179656 | tf_op jit(solution)/shard_map/ppermute | solution.py:891
  216.6 40.4 %collective-permute-start.18 = (bf16[384,512]{1,0:T(8,128)(2,1)}, bf16[384,512]{1,0:T(8,128)(2,1)}, u32[]{:S(2)}, u32[]{:S(2)}) collective-permute-start(bf16[384,512]{1,0:T(8,128)(2,1)} %get-tuple-element.211), channel_id=1, source_target_pairs={{0,17},{1,16},{2,19},{3,18},{4,21},{5,20},{6,23},{7,22},{8,25},{9,... | collective-permute-start | bytes 1179656 | tf_op jit(solution)/shard_map/ppermute | solution.py:891
  217.3 39.8 %collective-permute-start.19 = (bf16[528,512]{1,0:T(8,128)(2,1)}, bf16[528,512]{1,0:T(8,128)(2,1)S(1)}, u32[]{:S(2)}, u32[]{:S(2)}) collective-permute-start(bf16[528,512]{1,0:T(8,128)(2,1)} %get-tuple-element.212), channel_id=1, source_target_pairs={{4,0},{12,1},{6,2},{14,3},{0,4},{8,5},{2,6},{10,7},{5,8},{13,9},{7... | collective-permute-start | bytes 1622024 | tf_op jit(solution)/shard_map/ppermute | solution.py:973
  261.5 16.9 %collective-permute-start.21 = (bf16[528,512]{1,0:T(8,128)(2,1)}, bf16[528,512]{1,0:T(8,128)(2,1)}, u32[]{:S(2)}, u32[]{:S(2)}) collective-permute-start(bf16[528,512]{1,0:T(8,128)(2,1)} %shard_map.262), channel_id=1, source_target_pairs={{6,0},{14,1},{0,2},{8,3},{2,4},{10,5},{4,6},{12,7},{7,8},{15,9},{1... | collective-permute-start | bytes 1622024 | tf_op jit(solution)/shard_map/ppermute | solution.py:973
  284.9 20.2 %collective-permute-start.26 = (bf16[528,512]{1,0:T(8,128)(2,1)}, bf16[528,512]{1,0:T(8,128)(2,1)}, u32[]{:S(2)}, u32[]{:S(2)}) collective-permute-start(bf16[528,512]{1,0:T(8,128)(2,1)} %get-tuple-element.238), channel_id=1, source_target_pairs={{2,0},{10,1},{4,2},{12,3},{6,4},{14,5},{0,6},{8,7},{3,8},{11,9},{5... | collective-permute-start | bytes 1622024 | tf_op jit(solution)/shard_map/ppermute | solution.py:973
  289.3 15.7 %collective-permute-start.25 = (bf16[192,512]{1,0:T(8,128)(2,1)}, bf16[192,512]{1,0:T(8,128)(2,1)S(1)}, u32[]{:S(2)}, u32[]{:S(2)}) collective-permute-start(bf16[192,512]{1,0:T(8,128)(2,1)} %get-tuple-element.237), channel_id=1, source_target_pairs={{0,17},{1,16},{2,19},{3,18},{4,21},{5,20},{6,23},{7,22},{8,25},{9,... | collective-permute-start | bytes 589832 | tf_op jit(solution)/shard_map/ppermute | solution.py:891
  334.7 30.4 %collective-permute-start.34 = (bf16[576,512]{1,0:T(8,128)(2,1)S(1)}, bf16[576,512]{1,0:T(8,128)(2,1)S(1)}, u32[]{:S(2)}, u32[]{:S(2)}) collective-permute-start(bf16[576,512]{1,0:T(8,128)(2,1)S(1)} %pad_maximum_fusion.1), channel_id=1, source_target_pairs={{0,1},{1,0},{2,3},{3,2},{4,5},{5,4},{6,7},{7,6},{8,9},{9,8},{10,11... | collective-permute-start | bytes 1769480 | tf_op jit(solution)/shard_map/ppermute | solution.py:891
  336.8 28.4 %collective-permute-start.35 = (bf16[576,512]{1,0:T(8,128)(2,1)S(1)}, bf16[576,512]{1,0:T(8,128)(2,1)S(1)}, u32[]{:S(2)}, u32[]{:S(2)}) collective-permute-start(bf16[576,512]{1,0:T(8,128)(2,1)S(1)} %pad_maximum_fusion.1), channel_id=1, source_target_pairs={{0,16},{1,17},{2,18},{3,19},{4,20},{5,21},{6,22},{7,23},{8,24},{9,... | collective-permute-start | bytes 1769480 | tf_op jit(solution)/shard_map/ppermute | solution.py:891
  337.3 31.5 %collective-permute-start.36 = (bf16[576,512]{1,0:T(8,128)(2,1)S(1)}, bf16[576,512]{1,0:T(8,128)(2,1)S(1)}, u32[]{:S(2)}, u32[]{:S(2)}) collective-permute-start(bf16[576,512]{1,0:T(8,128)(2,1)S(1)} %pad_maximum_fusion.1), channel_id=1, source_target_pairs={{0,17},{1,16},{2,19},{3,18},{4,21},{5,20},{6,23},{7,22},{8,25},{9,... | collective-permute-start | bytes 1769480 | tf_op jit(solution)/shard_map/ppermute | solution.py:891
  338.3 26.9 %collective-permute-start.37 = (bf16[528,512]{1,0:T(8,128)(2,1)S(1)}, bf16[528,512]{1,0:T(8,128)(2,1)S(1)}, u32[]{:S(2)}, u32[]{:S(2)}) collective-permute-start(bf16[528,512]{1,0:T(8,128)(2,1)S(1)} %copy-done.10), channel_id=1, source_target_pairs={{4,0},{12,1},{6,2},{14,3},{0,4},{8,5},{2,6},{10,7},{5,8},{13,9},{7... | collective-permute-start | bytes 1622024 | tf_op jit(solution)/shard_map/ppermute | solution.py:973
  (41 other events, 421.9 us)

commit v4 on v3

--- a/solution.py
+++ b/solution.py
@@ -269,6 +269,7 @@
 MIB = 2**20
 AXES = ("grp", "ctx")
 LANES = 128
+VECTORS = 16
 ROWS_STEP = 528
 
 
@@ -308,13 +309,23 @@
     )(*operands, *into)
 
 
-def project_kernel(context, scale, own, other, wq, wk, wv, q_out, k_out, v_out, x_out):
-    rows = own[...]
-    x_out[0] = rows
-    queries = (dot(rows, wq[...], 1, 0) * scale).astype(BF16)
-    for h in range(HEADS):
-        q_out[h] = queries[:, h * HD : (h + 1) * HD]
-    for side, keys_of in enumerate((rows[:context], other[:context])):
+def project_kernel(context, scale, with_own, *refs):
+    if with_own:
+        own, wq, refs = refs[0], refs[1], refs[2:]
+        rows = own[...]
+    others = len(refs) - 6 if with_own else len(refs) - 4
+    other_refs, (wk, wv), refs = refs[:others], refs[others : others + 2], refs[others + 2 :]
+    k_out, v_out = refs[:2]
+    sides = []
+    if with_own:
+        q_out, x_out = refs[2:]
+        x_out[0] = rows
+        queries = (dot(rows, wq[...], 1, 0) * scale).astype(BF16)
+        for h in range(HEADS):
+            q_out[h] = queries[:, h * HD : (h + 1) * HD]
+        sides.append(rows[:context])
+    sides += [ref[:context] for ref in other_refs]
+    for side, keys_of in enumerate(sides):
         keys = dot(keys_of, wk[...], 1, 0).astype(BF16)
         values = dot(keys_of, wv[...], 1, 0).astype(BF16)
         for h in range(HEADS):
@@ -323,30 +334,36 @@
 
 
 def project(own, other, place, blocks, context, kinds, scale, into):
-    rows, width = own.shape
+    given = [array for array in (own, other) if array is not None]
+    rows, width = given[0].shape
     fixed = lambda b: (0, 0)
+    whole = ((width, width), fixed)
+    sides = len(given)
     key_spec = (
-        (HEADS, 2, 1, context, HD),
-        lambda b: (0, 0, place, 0, 0),
+        (HEADS, sides, 1, context, HD),
+        lambda b: (0, int(own is None), place, 0, 0),
         (HEADS, 2, blocks, context, HD),
         BF16,
     )
+    row_specs = [
+        ((HEADS, rows, HD), lambda b: (0, place, 0), (HEADS, blocks * rows, HD), BF16),
+        ((1, rows, width), lambda b: (place, 0, 0), (blocks, rows, width), BF16),
+    ]
+    row_in = [((rows, width), fixed)]
+    with_own = own is not None
+    wq, wk, wv = kinds
     return kernel_call(
-        partial(project_kernel, context, scale),
+        partial(project_kernel, context, scale, with_own),
         (1,),
-        [((rows, width), fixed)] * 2 + [((width, width), fixed)] * 3,
-        [
-            ((HEADS, rows, HD), lambda b: (0, place, 0), (HEADS, blocks * rows, HD), BF16),
-            key_spec,
-            key_spec,
-            ((1, rows, width), lambda b: (place, 0, 0), (blocks, rows, width), BF16),
-        ],
+        (row_in + [whole]) * with_own + row_in * (other is not None) + [whole] * 2,
+        [key_spec] * 2 + row_specs * with_own,
         [],
         2 * width * width * (rows + 4 * context),
         4 * width * (rows + 3 * context),
-        own,
-        other,
-        *kinds,
+        *([own, wq] if with_own else []),
+        *([other] if other is not None else []),
+        wk,
+        wv,
         into=into,
     )
 
@@ -470,7 +487,8 @@
     sums, sending, cot, out, arrived, left = refs[5:]
     t = pl.program_id(0)
     width, hidden_width = w1.shape
-    rows, half = x_ref.shape[0], sending.shape[0]
+    rows, half = x_ref.shape[0], (width + 2 * hidden_width) // 2
+    vector_rows = sums.shape[0] - 2 * half
     block = cot.shape[0] // blocks
     load = [
         pltpu.make_async_copy(ref, cot.at[pl.ds(j * block, block)], arrived.at[j])
@@ -505,6 +523,8 @@
     second_sum = hidden + dot(activated, w2[...], 1, 0) + b2[...].astype(F32)
     result, normed_two, inverse_two = norm_forward(second_sum, gain_two, s2[...].astype(F32))
     out[here, :] = result.astype(BF16)
+    for j, copy in enumerate(store):
+        pl.when(t == ((j + 1) * block - 1) // rows)(copy.start)
     upstream = cot[here, :].astype(F32)
     second_grad, gain_two_sum, shift_two_sum = norm_backward(
         upstream, normed_two, inverse_two, gain_two
@@ -547,14 +567,21 @@
     def _():
         bit = bit_ref[0]
         keep = pltpu.make_async_copy(
-            sums.at[pl.ds(pl.multiple_of(bit * half, 16), half)], keep_ref, arrived.at[0]
-        )
-        sending[...] = sums[pl.ds(pl.multiple_of((1 - bit) * half, 16), half)].astype(BF16)
-        send = pltpu.make_async_copy(sending, send_ref, arrived.at[1])
-        copies = [*store, keep, send]
-        for copy in copies:
+            sums.at[pl.ds(pl.multiple_of(bit * half, 16), half)],
+            keep_ref.at[pl.ds(0, half)],
+            arrived.at[0],
+        )
+        keep_vectors = pltpu.make_async_copy(
+            sums.at[pl.ds(2 * half, vector_rows)],
+            keep_ref.at[pl.ds(half, vector_rows)],
+            arrived.at[1],
+        )
+        sending[:half] = sums[pl.ds(pl.multiple_of((1 - bit) * half, 16), half)].astype(BF16)
+        sending[half:] = sums[2 * half :].astype(BF16)
+        send = pltpu.make_async_copy(sending, send_ref, arrived.at[2])
+        for copy in (keep, keep_vectors, send):
             copy.start()
-        for copy in copies:
+        for copy in (*store, keep, keep_vectors, send):
             copy.wait()
 
 
@@ -565,7 +592,7 @@
     hidden = weights[1].shape[1]
     by_row = ((rows, width), lambda t: (t, 0))
     by_head = ((HEADS, rows, HD), lambda t: (0, t, 0))
-    count = -(-(width + 2 * hidden + 8) // 512) * 512
+    half = width // 2 + hidden
     *out, first_grad, grads, delta, keep, send = kernel_call(
         partial(dense_kernel, blocks, steps),
         (steps,),
@@ -577,12 +604,12 @@
             (*by_row, (total, width), BF16),
             (*by_head, (HEADS, total, HD), BF16),
             (*by_head, (HEADS, total, HD), F32),
-            (None, pl.ANY, (count // 2, width), F32),
-            (None, pl.ANY, (count // 2, width), BF16),
+            (None, pl.ANY, (half + VECTORS, width), F32),
+            (None, pl.ANY, (half + VECTORS, width), BF16),
         ],
         [
-            pltpu.VMEM((count, width), F32),
-            pltpu.VMEM((count // 2, width), BF16),
+            pltpu.VMEM((2 * half + VECTORS, width), F32),
+            pltpu.VMEM((half + VECTORS, width), BF16),
             pltpu.VMEM((total, width), BF16),
             pltpu.VMEM((total, width), BF16),
             pltpu.SemaphoreType.DMA((blocks,)),
@@ -802,8 +829,8 @@
 
 
 def unpack_kernel(counts, shares, place_ref, half_ref, *refs):
-    outs, (early, late, left) = refs[:7], refs[7:]
-    grad_query, grad_key, grad_value, grad_output, grad_inner, grad_outer, vectors = outs
+    outs, (early, late, left) = refs[:6], refs[6:]
+    grad_query, grad_key, grad_value, grad_output, grad_inner, grad_outer = outs
     first, second = shares
     across, along = counts
     share = first + second
@@ -818,7 +845,6 @@
                 at + first : at + share
             ].astype(F32)
     width, hidden = grad_inner.shape
-    middle = late.shape[0] - width
 
     def copy_out(pieces):
         copies = [
@@ -830,30 +856,34 @@
         for copy in copies:
             copy.wait()
 
-    @pl.when(place_ref[0] == 0)
-    def _():
-        pieces = [(late, 0, width, grad_query), (late, width, middle, grad_key.at[:middle])]
-        pieces.append((early, 0, width, grad_output))
-        for j in range(0, hidden, width):
-            pieces.append((early, width + j, width, grad_inner.at[:, pl.ds(j, width)]))
-        copy_out(pieces)
-
-    @pl.when(place_ref[0] == 1)
-    def _():
-        copy_out(
-            [
-                (late, 0, width - middle, grad_key.at[middle:]),
-                (late, width - middle, width, grad_value),
-                (early, 0, hidden, grad_outer),
-                (early, hidden, vectors.shape[0], vectors),
-            ]
-        )
+    late_refs = [grad_query, grad_key, grad_value]
+    early_refs = [grad_output]
+    early_refs += [grad_inner.at[:, pl.ds(j, width)] for j in range(0, hidden, width)]
+    early_refs += [grad_outer.at[pl.ds(j, width)] for j in range(0, hidden, width)]
+
+    def pieces(source, refs, start):
+        end = start + source.shape[0]
+        for j, ref in enumerate(refs):
+            low, high = max(start, j * width), min(end, (j + 1) * width)
+            if low < high:
+                yield source, low - start, high - low, ref.at[pl.ds(low - j * width, high - low)]
+
+    for core in range(2):
+
+        @pl.when(place_ref[0] == core)
+        def _(core=core):
+            copy_out(
+                [
+                    *pieces(late, late_refs, core * late.shape[0]),
+                    *pieces(early, early_refs, core * early.shape[0]),
+                ]
+            )
 
 
 def unpack(places, half, counts, shares, hidden, into=()):
     width = half.shape[1]
     total = counts[0] * counts[1]
-    shapes = [(width, width)] * 4 + [(width, hidden), (hidden, width), (16, width)]
+    shapes = [(width, width)] * 4 + [(width, hidden), (hidden, width)]
     return kernel_call(
         partial(unpack_kernel, counts, shares),
         (1,),
@@ -862,7 +892,7 @@
         [
             pltpu.VMEM((total * shares[0], width), F32),
             pltpu.VMEM((total * shares[1], width), F32),
-            pltpu.SemaphoreType.DMA((3 + hidden // width,)),
+            pltpu.SemaphoreType.DMA((4 + 2 * hidden // width,)),
         ],
         0,
         6 * half.size,
@@ -892,13 +922,17 @@
             array, AXES, [(number(g, c), number(*move(g, c, s))) for g, c in places]
         )
 
-    def reduce_pieces(stage, parts):
+    def reduce_pieces(stage, parts, below=0):
         count, index, _ = stage
-        piece = parts[0].shape[0] // count
+        rows = parts[0].shape[0] - below
+        piece = rows // count
 
         def take(s):
             at = (index ^ s) * piece
-            return sum(lax.dynamic_slice_in_dim(part, at, piece).astype(F32) for part in parts)
+            taken = sum(lax.dynamic_slice_in_dim(part, at, piece).astype(F32) for part in parts)
+            if not below:
+                return taken
+            return jnp.concatenate([taken, sum(part[rows:].astype(F32) for part in parts)])
 
         return [take(0)] + [take(s).astype(BF16) for s in range(1, count)]
 
@@ -988,12 +1022,11 @@
     qkvx = ()
     for j in range(blocks - 1):
         qkvx = project(own[j], other[j], j, blocks, context, kinds, scale * log2e, qkvx)
-    own_far, *qkvx = tie(own_far, *qkvx)
+    own_far, *kvqx = tie(own_far, *qkvx)
     other_far = lax.ppermute(own_far, AXES, across)
-    qkvx = project(
-        own_far, other_far, blocks - 1, blocks, context, kinds, scale * log2e, qkvx
-    )
-    q, k, v, x = qkvx
+    *kv, q, x = project(own_far, None, blocks - 1, blocks, context, kinds, scale * log2e, kvqx)
+    other_far, *kv = tie(other_far, *kv)
+    k, v = project(None, other_far, blocks - 1, blocks, context, kinds, scale * log2e, kv)
     k, v = (array.reshape(HEADS, 2 * blocks * context, HD) for array in (k, v))
 
     *cots, q = tie(*[block_of(masked, r) for r in order], q)
@@ -1022,17 +1055,17 @@
 
     added = lambda parts: sum(part.astype(F32) for part in parts)
 
-    def start(stage, part):
+    def start(stage, *part):
         pieces_of, send, join = stage
-        mine, *pieces = pieces_of(part)
+        mine, *pieces = pieces_of(*part)
         return pieces, lambda pieces: send([mine] + pieces), partial(join, mine)
 
     *out, given, grads = tie(*out, given, grads)
     came = lax.ppermute(given, AXES, across)
-    home = [homeward(out[j], r) for j, r in enumerate(order[:-1])]
+    home = [homeward(out[j], r) for j, r in enumerate(order[:-2])]
     kv_other, dq = attention_backward(q, grads, delta, p, k, v, scale_k, 1.0, chunk, 2, 2)
     *home, came, kv_other, grads = tie(*home, came, kv_other, grads)
-    pieces, send, early_join = start(stages[1], [keep, came])
+    pieces, send, early_join = start(stages[1], [keep, came], VECTORS)
     *pieces, kv_other, far_out, grads = tie(*pieces, kv_other, out[-1], grads)
     kv_came = lax.ppermute(kv_other, AXES, across)
     early_came = send(pieces)
@@ -1063,16 +1096,25 @@
     early = added(early_join(early_came))
 
     along = members // 2
-    shares = (early.shape[0] // along, late.shape[0] // along)
+    shares = ((early.shape[0] - VECTORS) // along, late.shape[0] // along)
     both = jnp.concatenate(
-        [early.reshape(along, shares[0], width), late.reshape(along, shares[1], width)], axis=1
+        [
+            early[:-VECTORS].reshape(along, shares[0], width),
+            late.reshape(along, shares[1], width),
+            jnp.broadcast_to(early[-VECTORS:], (along, VECTORS, width)),
+        ],
+        axis=1,
     ).reshape(-1, width)
     pieces, send, join = start(stages[2], [both])
+    *pieces, zero_out = tie(*pieces, out[-2])
     came = send(pieces)
+    zero_home = homeward(zero_out, order[-2])
     grad_tokens = jnp.zeros((blocks, rows, width), F32)
     grad_tokens = put(grad_tokens, three.astype(F32), order[1])
-    *came, grad_tokens, one = tie(*came, grad_tokens, one)
+    *came, zero_home, grad_tokens, one = tie(*came, zero_home, grad_tokens, one)
+    home.insert(blocks - 2, zero_home)
     both = added(join(came))
+    both, vectors = both[:-VECTORS], both[-VECTORS:]
 
     pieces, send, join = start(stages[3], both)
     *home, live, one, pieces[0] = tie(*home, live, one, pieces[0])
@@ -1100,7 +1142,7 @@
     grad_tokens = put(grad_tokens, last.astype(F32), far)
     came, grad_tokens, *sums = tie(came, grad_tokens, *sums)
     theirs = jnp.stack([1 - mine[0], *mine[1:]])
-    *sums, vectors = unpack(theirs, came, counts, shares, hidden, sums)
+    sums = unpack(theirs, came, counts, shares, hidden, sums)
     return (
         layer_out,
         grad_tokens,

time: 389 us -> 381 us (0.979)
  waiting for transfers between devices: 82.7 us -> 60.5 us
  starting transfers between devices: 51.1 us -> 68.4 us
  other arithmetic: 18.7 us -> 14.3 us
    ppermute x8, waiting for transfers between devices: 25.5 us -> 1.61 us  [homeward(): return lax.ppermute(block, AXES, route(r, True))]
    ppermute x15, waiting for transfers between devices: 24.9 us -> 44.3 us  [swap(): lax.ppermute(array, AXES, [(number(g, c), number(*move(g, c, s))) for g,...]
    ppermute x8, waiting for transfers between devices: 32.3 us -> 14.5 us  [outward(): return lax.ppermute(block, AXES, route(r))]
    ppermute x8, starting transfers between devices: 12.4 us -> 23.1 us  [outward(): return lax.ppermute(block, AXES, route(r))]
    convert_element_type x2 -> x1, other arithmetic: 4.98 us -> 0.89 us  [reduce_pieces(): return [take(0)] + [take(s).astype(BF16) for s in range(1, count)]]
    pallas_call x14 -> x15, Pallas kernels: 212 us -> 214 us  [kernel_call(): pl.pallas_call(run, grid=grid, in_specs=[pl.BlockSpec(memory_space=index)...]
  transfers between devices with their start and end apart: 39 -> 39, of which waited for: 10 -> 10; matrix products, arithmetic and copies ran while one was open for 5% -> 5% of each run, Pallas kernels for 42% -> 45%
where the time goes in v4:
time: 381 us; the launch traced here: 375 us
  Pallas kernels  214 us (56%)
  starting transfers between devices  68.4 us (18%)
  waiting for transfers between devices  60.5 us (16%)
  local copies, waits for them, and re-layouts  16.1 us (4%)
  other arithmetic  14.3 us (4%)
    pallas_call x15, Pallas kernels, kernel_call(): pl.pallas_call(run, grid=grid, in_specs=[pl.BlockSpec(memory_space=index)...  214 us
    ppermute x15, waiting for transfers between devices, swap(): lax.ppermute(array, AXES, [(number(g, c), number(*move(g, c, s))) for g,...  44.3 us
    ppermute x8, starting transfers between devices, outward(): return lax.ppermute(block, AXES, route(r))  23.1 us
    ppermute x15, starting transfers between devices, swap(): lax.ppermute(array, AXES, [(number(g, c), number(*move(g, c, s))) for g,...  21.8 us
    ppermute x8, starting transfers between devices, homeward(): return lax.ppermute(block, AXES, route(r, True))  15.9 us
    ppermute x8, waiting for transfers between devices, outward(): return lax.ppermute(block, AXES, route(r))  14.5 us
  transfers between devices with their start and end apart: 39, of which 10 were waited for; matrix products, arithmetic and copies ran while one was open for 5% of the time, Pallas kernels for 45%

profile of v4, /device:TPU:0, one launch (start us, length us, event | category | flops | bytes accessed | tf_op | source)
XLA Modules:
  0.0 374.9 jit_solution(15026127386380221147)
XLA Ops:
  8.4 12.1 %collective-permute-done.5.refs_0_ = bf16[528,512]{1,0:T(8,128)(2,1)} collective-permute-done((bf16[528,512]{1,0:T(8,128)(2,1)S(1)}, bf16[528,512]{1,0:T(8,128)(2,1)}, u32[]{:S(2)}, u32[]{:S(2)}) %collective-permute-start.5) | collective-permute-done | bytes 540704 | tf_op jit(solution)/shard_map/ppermute | solution.py:1004
  21.7 11.4 %collective-permute-start = (bf16[528,512]{1,0:T(8,128)(2,1)S(1)}, bf16[528,512]{1,0:T(8,128)(2,1)S(1)}, u32[]{:S(2)}, u32[]{:S(2)}) collective-permute-start(bf16[528,512]{1,0:T(8,128)(2,1)S(1)} %get-tuple-element.333), channel_id=1, source_target_pairs={{0,4},{1,12},{2,6},{3,14},{4,0},{5,8},{6,2},{7,10},{8,5},{9,13},{1... | collective-permute-start | bytes 1622024 | tf_op jit(solution)/shard_map/ppermute | solution.py:1004
  38.2 4.9 %shard_map.254 = (bf16[4,2,4,512,128]{4,3,2,1,0:T(8,128)(2,1)}, bf16[4,2,4,512,128]{4,3,2,1,0:T(8,128)(2,1)}, bf16[4,2112,128]{2,1,0:T(8,128)(2,1)}, bf16[4,528,512]{2,1,0:T(8,128)(2,1)}) custom-call(bf16[528,512]{1,0:T(8,128)(2,1)} %collective-permute-done.5.refs_0_, bf16[512,512]{1,0:T(8,128)(2,1)} %refs_4_.13, ...), custom_call_target="tpu_custom_call" | custom-call | flops 1350565888 | bytes 4227072 | tf_op jit(solution)/shard_map/pallas_call | solution.py:292
  43.9 4.9 %shard_map.255 = (bf16[4,2,4,512,128]{4,3,2,1,0:T(8,128)(2,1)}, bf16[4,2,4,512,128]{4,3,2,1,0:T(8,128)(2,1)}, bf16[4,2112,128]{2,1,0:T(8,128)(2,1)}, bf16[4,528,512]{2,1,0:T(8,128)(2,1)}) custom-call(bf16[528,512]{1,0:T(8,128)(2,1)} %collective-permute-done.3.refs_0_, ...), custom_call_target="tpu_custom_call", output_to_operand_aliasing={{0}: (5, {}), {1}: (6, {}), {2}: (7, {}), {3}: (8, {})} | custom-call | flops 1350565888 | bytes 4227072 | tf_op jit(solution)/shard_map/pallas_call | solution.py:292
  49.7 5.0 %shard_map.256 = (bf16[4,2,4,512,128]{4,3,2,1,0:T(8,128)(2,1)}, bf16[4,2,4,512,128]{4,3,2,1,0:T(8,128)(2,1)}, bf16[4,2112,128]{2,1,0:T(8,128)(2,1)}, bf16[4,528,512]{2,1,0:T(8,128)(2,1)}) custom-call(bf16[528,512]{1,0:T(8,128)(2,1)} %copy-done.16, ...), custom_call_target="tpu_custom_call", output_to_operand_aliasing={{0}: (5, {}), {1}: (6, {}), {2}: (7, {}), {3}: (8, {})} | custom-call | flops 1350565888 | bytes 4227072 | tf_op jit(solution)/shard_map/pallas_call | solution.py:292
  59.5 3.8 %shard_map.257 = (bf16[4,2,4,512,128]{4,3,2,1,0:T(8,128)(2,1)}, bf16[4,2,4,512,128]{4,3,2,1,0:T(8,128)(2,1)}, bf16[4,2112,128]{2,1,0:T(8,128)(2,1)}, bf16[4,528,512]{2,1,0:T(8,128)(2,1)}) custom-call(bf16[528,512]{1,0:T(8,128)(2,1)} %copy-done.15, ...), custom_call_target="tpu_custom_call", output_to_operand_aliasing={{0}: (4, {}), {1}: (5, {}), {2}: (6, {}), {3}: (7, {})} | custom-call | flops 1350565888 | bytes 4227072 | tf_op jit(solution)/shard_map/pallas_call | solution.py:292
  63.6 3.6 collective-permute-start.9
  73.1 52.0 %shard_map.259 = (bf16[4,2112,4096]{2,1,0:T(8,128)(2,1)}, f32[2112,512]{1,0:T(8,128)}, f32[4,2112,128]{2,1,0:T(8,128)}) custom-call(bf16[4,2112,128]{2,1,0:T(8,128)(2,1)} %get-tuple-element.182.refs_0_, bf16[4,4096,128]{2,1,0:T(8,128)(2,1)} %bitcast.64, bf16[4,4096,128]{2,1,0:T(8,128)(2,1)} %bitcast.67), custom_call_target="tpu_custom_call" | custom-call | flops 35433480192 | bytes 69206016 | tf_op jit(solution)/shard_map/pallas_call | solution.py:292
  126.0 36.6 %shard_map.260 = (bf16[528,512]{1,0:T(8,128)(2,1)}, bf16[528,512]{1,0:T(8,128)(2,1)}, bf16[528,512]{1,0:T(8,128)(2,1)}, bf16[528,512]{1,0:T(8,128)(2,1)}, bf16[2...) custom-call(s32[1]{0:T(128)} %bitcast.refs_0_, ...), custom_call_target="tpu_custom_call" | custom-call | flops 16609443840 | bytes 45088768 | tf_op jit(solution)/shard_map/pallas_call | solution.py:292
  167.8 36.6 %shard_map.261 = (bf16[2,4,2048,128]{3,2,1,0:T(8,128)(2,1)}, f32[4,2112,128]{2,1,0:T(8,128)}) custom-call(bf16[4,2112,128]{2,1,0:T(8,128)(2,1)} %get-tuple-element.182.refs_0_, bf16[4,2112,128]{2,1,0:T(8,128)(2,1)} %get-tuple-element.224.refs_1_, f32[4,2112,128]{2,1,0:T(8,128)} %get-tuple-element.212.refs_2_, ...), custom_call_target="tpu_custom_call" | custom-call | flops 26575110144 | bytes 34603008 | tf_op jit(solution)/shard_map/pallas_call | solution.py:292
  214.9 36.5 %shard_map.262 = (bf16[2,4,2048,128]{3,2,1,0:T(8,128)(2,1)}, bf16[4,2112,128]{2,1,0:T(8,128)(2,1)}) custom-call(bf16[4,2112,128]{2,1,0:T(8,128)(2,1)} %get-tuple-element.182.refs_0_, bf16[4,2112,128]{2,1,0:T(8,128)(2,1)} %get-tuple-element.224.refs_1_, f32[4,2112,128]{2,1,0:T(8,128)} %get-tuple-element.212.refs_2_, ...), custom_call_target="tpu_custom_call" | custom-call | flops 26575110144 | bytes 34603008 | tf_op jit(solution)/shard_map/pallas_call | solution.py:292
  252.3 4.1 %shard_map.263 = bf16[528,512]{1,0:T(8,128)(2,1)} custom-call(bf16[4,528,512]{2,1,0:T(8,128)(2,1)} %bitcast.74, bf16[4,4,528,128]{3,2,1,0:T(8,128)(2,1)} %bitcast.70, bf16[2,4,4,512,128]{4,3,2,1,0:T(8,128)(2,1)} %bitcast.61, bf16[2,4,4,512,128]{4,3,2,1,0:T(8,128)(2,1)} %bitcast.16.refs_3_, bf16[512,512]{1,0:T(8,128)(2,1)} %refs_4_.13, ...), custom_call_target="tpu_custom_call" | custom-call | flops 813694976 | bytes 4767744 | tf_op jit(solution)/shard_map/pallas_call | solution.py:292
  257.4 5.5 %shard_map.264 = (bf16[528,512]{1,0:T(8,128)(2,1)}, bf16[528,512]{1,0:T(8,128)(2,1)}) custom-call(bf16[4,528,512]{2,1,0:T(8,128)(2,1)} %bitcast.75, bf16[4,4,528,128]{3,2,1,0:T(8,128)(2,1)} %bitcast.71, bf16[2,4,4,512,128]{4,3,2,1,0:T(8,128)(2,1)} %bitcast.62, bf16[2,4,4,512,128]{4,3,2,1,0:T(8,128)(2,1)} %bitcast.16.refs_3_, bf16[512,512]{1,0:T(8,128)(2,1)} %refs_4_.13, ...), custom_call_target="tpu_custom_call" | custom-call | flops 1627389952 | bytes 9535488 | tf_op jit(solution)/shard_map/pallas_call | solution.py:292
  262.9 8.7 %shard_map.265 = (f32[768,512]{1,0:T(8,128)}, bf16[768,512]{1,0:T(8,128)(2,1)}) custom-call(s32[1]{0:T(128)} %bitcast.refs_0_, bf16[4,528,512]{2,1,0:T(8,128)(2,1)} %get-tuple-element.237.refs_1_, bf16[4,2112,128]{2,1,0:T(8,128)(2,1)} %get-tuple-element.231.refs_2_, bf16[2,4,2048,128]{3,2,1,0:T(8,128)(2,1)} %get-tuple-element.232.refs_3_, ...), custom_call_target="tpu_custom_call" | custom-call | flops 3254779904 | bytes 12713984 | tf_op jit(solution)/shard_map/pallas_call | solution.py:292
  274.0 4.3 %shard_map.266 = bf16[528,512]{1,0:T(8,128)(2,1)} custom-call(bf16[4,528,512]{2,1,0:T(8,128)(2,1)} %bitcast.76, bf16[4,4,528,128]{3,2,1,0:T(8,128)(2,1)} %bitcast.72, bf16[2,4,4,512,128]{4,3,2,1,0:T(8,128)(2,1)} %bitcast.63, bf16[2,4,4,512,128]{4,3,2,1,0:T(8,128)(2,1)} %bitcast.16.refs_3_, bf16[512,512]{1,0:T(8,128)(2,1)} %refs_4_.13, ...), custom_call_target="tpu_custom_call" | custom-call | flops 813694976 | bytes 4767744 | tf_op jit(solution)/shard_map/pallas_call | solution.py:292
  285.7 7.3 %collective-permute-done.22 = bf16[192,512]{1,0:T(8,128)(2,1)S(1)} collective-permute-done((bf16[192,512]{1,0:T(8,128)(2,1)}, bf16[192,512]{1,0:T(8,128)(2,1)S(1)}, u32[]{:S(2)}, u32[]{:S(2)}) %collective-permute-start.22) | collective-permute-done | bytes 196640 | tf_op jit(solution)/shard_map/ppermute | solution.py:921
  292.9 6.3 %collective-permute-done.24 = bf16[192,512]{1,0:T(8,128)(2,1)S(1)} collective-permute-done((bf16[192,512]{1,0:T(8,128)(2,1)}, bf16[192,512]{1,0:T(8,128)(2,1)S(1)}, u32[]{:S(2)}, u32[]{:S(2)}) %collective-permute-start.24) | collective-permute-done | bytes 196640 | tf_op jit(solution)/shard_map/ppermute | solution.py:921
  300.2 5.8 %collective-permute-start.29 = (bf16[528,512]{1,0:T(8,128)(2,1)}, bf16[528,512]{1,0:T(8,128)(2,1)}, u32[]{:S(2)}, u32[]{:S(2)}) collective-permute-start(bf16[528,512]{1,0:T(8,128)(2,1)} %get-tuple-element.256), channel_id=1, source_target_pairs={{0,0},{8,1},{2,2},{10,3},{4,4},{12,5},{6,6},{14,7},{1,8},{9,9},{3,... | collective-permute-start | bytes 1622024 | tf_op jit(solution)/shard_map/ppermute | solution.py:1007
  330.4 3.7 collective-permute-start.34
  338.8 8.1 %collective-permute-done.34 = bf16[512,512]{1,0:T(8,128)(2,1)S(1)} collective-permute-done((bf16[512,512]{1,0:T(8,128)(2,1)S(1)}, bf16[512,512]{1,0:T(8,128)(2,1)S(1)}, u32[]{:S(2)}, u32[]{:S(2)}) %collective-permute-start.34) | collective-permute-done | bytes 524320 | tf_op jit(solution)/shard_map/ppermute | solution.py:921
  346.9 4.9 %collective-permute-done.35 = bf16[512,512]{1,0:T(8,128)(2,1)S(1)} collective-permute-done((bf16[512,512]{1,0:T(8,128)(2,1)S(1)}, bf16[512,512]{1,0:T(8,128)(2,1)S(1)}, u32[]{:S(2)}, u32[]{:S(2)}) %collective-permute-start.35) | collective-permute-done | bytes 524320 | tf_op jit(solution)/shard_map/ppermute | solution.py:921
  351.8 11.5 %collective-permute-done.36 = bf16[512,512]{1,0:T(8,128)(2,1)S(1)} collective-permute-done((bf16[512,512]{1,0:T(8,128)(2,1)S(1)}, bf16[512,512]{1,0:T(8,128)(2,1)S(1)}, u32[]{:S(2)}, u32[]{:S(2)}) %collective-permute-start.36) | collective-permute-done | bytes 524320 | tf_op jit(solution)/shard_map/ppermute | solution.py:921
  365.6 3.9 %shard_map.267 = (f32[512,512]{1,0:T(8,128)}, f32[512,512]{1,0:T(8,128)}, f32[512,512]{1,0:T(8,128)}, f32[512,512]{1,0:T(8,128)}, f32[512,1024]{1,0:T(8,128)}, /*index=5*/f32[1024,512]{1,0:T(8,128)}) custom-call(s32[3]{0:T(128)} %get-tuple-element.346.refs_0_, bf16[2048,512]{1,0:T(8,128)(2,1)} %copy-done.1), custom_call_target="tpu_custom_call" | custom-call | bytes 6291456 | tf_op jit(solution)/shard_map/pallas_call | solution.py:292
  370.7 4.0 %shard_map.268 = (f32[512,512]{1,0:T(8,128)}, f32[512,512]{1,0:T(8,128)}, f32[512,512]{1,0:T(8,128)}, f32[512,512]{1,0:T(8,128)}, f32[512,1024]{1,0:T(8,128)}, /*index=5*/f32[1024,512]{1,0:T(8,128)}) custom-call(s32[3]{0:T(128)} %get-tuple-element.347.refs_0_, ...), custom_call_target="tpu_custom_call", output_to_operand_aliasing={{0}: (2, {}), {1}: (3, {}), {2}: (4, {}), {3}: (5, {}), {4}... | custom-call | bytes 6291456 | tf_op jit(solution)/shard_map/pallas_call | solution.py:292
  (179 shorter events, 87.7 us)
Async XLA Ops:
  2.6 17.9 %collective-permute-start.5 = (bf16[528,512]{1,0:T(8,128)(2,1)S(1)}, bf16[528,512]{1,0:T(8,128)(2,1)}, u32[]{:S(2)}, u32[]{:S(2)}) collective-permute-start(bf16[528,512]{1,0:T(8,128)(2,1)S(1)} %get-tuple-element.331), channel_id=1, source_target_pairs={{0,2},{1,10},{2,4},{3,12},{4,6},{5,14},{6,0},{7,8},{8,3},{9,11},{1... | collective-permute-start | bytes 1622024 | tf_op jit(solution)/shard_map/ppermute | solution.py:1004
  5.6 31.0 %collective-permute-start.3 = (bf16[528,512]{1,0:T(8,128)(2,1)S(1)}, bf16[528,512]{1,0:T(8,128)(2,1)}, u32[]{:S(2)}, u32[]{:S(2)}) collective-permute-start(bf16[528,512]{1,0:T(8,128)(2,1)S(1)} %get-tuple-element.334), channel_id=1, source_target_pairs={{0,6},{1,14},{2,0},{3,8},{4,2},{5,10},{6,4},{7,12},{8,7},{9,15},{1... | collective-permute-start | bytes 1622024 | tf_op jit(solution)/shard_map/ppermute | solution.py:1004
  7.7 30.3 %collective-permute-start.1 = (bf16[528,512]{1,0:T(8,128)(2,1)S(1)}, bf16[528,512]{1,0:T(8,128)(2,1)S(1)}, u32[]{:S(2)}, u32[]{:S(2)}) collective-permute-start(bf16[528,512]{1,0:T(8,128)(2,1)S(1)} %get-tuple-element.332), channel_id=1, source_target_pairs={{0,0},{1,8},{2,2},{3,10},{4,4},{5,12},{6,6},{7,14},{8,1},{9,9},{10... | collective-permute-start | bytes 1622024 | tf_op jit(solution)/shard_map/ppermute | solution.py:1004
  20.5 17.8 %collective-permute-start.6 = (bf16[528,512]{1,0:T(8,128)(2,1)}, bf16[528,512]{1,0:T(8,128)(2,1)}, u32[]{:S(2)}, u32[]{:S(2)}) collective-permute-start(bf16[528,512]{1,0:T(8,128)(2,1)} %collective-permute-done.5.refs_0_), channel_id=1, source_target_pairs={{0,8},{1,9},{2,10},{3,11},{4,12},{5,13},{6,14},{7,15},{8,0},{9,1},... | collective-permute-start | bytes 1622024 | tf_op jit(solution)/shard_map/ppermute | solution.py:1021
  21.7 35.5 %collective-permute-start = (bf16[528,512]{1,0:T(8,128)(2,1)S(1)}, bf16[528,512]{1,0:T(8,128)(2,1)S(1)}, u32[]{:S(2)}, u32[]{:S(2)}) collective-permute-start(bf16[528,512]{1,0:T(8,128)(2,1)S(1)} %get-tuple-element.333), channel_id=1, source_target_pairs={{0,4},{1,12},{2,6},{3,14},{4,0},{5,8},{6,2},{7,10},{8,5},{9,13},{1... | collective-permute-start | bytes 1622024 | tf_op jit(solution)/shard_map/ppermute | solution.py:1004
  63.4 61.8 %collective-permute-start.8 = (bf16[528,512]{1,0:T(8,128)(2,1)S(1)}, bf16[528,512]{1,0:T(8,128)(2,1)S(1)}, u32[]{:S(2)}, u32[]{:S(2)}) collective-permute-start(bf16[528,512]{1,0:T(8,128)(2,1)S(1)} %get-tuple-element.192), channel_id=1, source_target_pairs={{0,2},{1,10},{2,4},{3,12},{4,6},{5,14},{6,0},{7,8},{8,3},{9,11},{1... | collective-permute-start | bytes 1622024 | tf_op jit(solution)/shard_map/ppermute | solution.py:1004
  63.6 61.6 %collective-permute-start.9 = (bf16[528,512]{1,0:T(8,128)(2,1)S(1)}, bf16[528,512]{1,0:T(8,128)(2,1)}, u32[]{:S(2)}, u32[]{:S(2)}) collective-permute-start(bf16[528,512]{1,0:T(8,128)(2,1)S(1)} %get-tuple-element.193), channel_id=1, source_target_pairs={{0,6},{1,14},{2,0},{3,8},{4,2},{5,10},{6,4},{7,12},{8,7},{9,15},{1... | collective-permute-start | bytes 1622024 | tf_op jit(solution)/shard_map/ppermute | solution.py:1004
  67.2 58.0 %collective-permute-start.10 = (bf16[528,512]{1,0:T(8,128)(2,1)S(1)}, bf16[528,512]{1,0:T(8,128)(2,1)}, u32[]{:S(2)}, u32[]{:S(2)}) collective-permute-start(bf16[528,512]{1,0:T(8,128)(2,1)S(1)} %get-tuple-element.194), channel_id=1, source_target_pairs={{0,0},{1,8},{2,2},{3,10},{4,4},{5,12},{6,6},{7,14},{8,1},{9,9},{10... | collective-permute-start | bytes 1622024 | tf_op jit(solution)/shard_map/ppermute | solution.py:1004
  69.2 56.0 %collective-permute-start.11 = (bf16[528,512]{1,0:T(8,128)(2,1)S(1)}, bf16[528,512]{1,0:T(8,128)(2,1)}, u32[]{:S(2)}, u32[]{:S(2)}) collective-permute-start(bf16[528,512]{1,0:T(8,128)(2,1)S(1)} %get-tuple-element.195), channel_id=1, source_target_pairs={{0,4},{1,12},{2,6},{3,14},{4,0},{5,8},{6,2},{7,10},{8,5},{9,13},{1... | collective-permute-start | bytes 1622024 | tf_op jit(solution)/shard_map/ppermute | solution.py:1004
  162.6 41.9 %collective-permute-start.12 = (bf16[528,512]{1,0:T(8,128)(2,1)}, bf16[528,512]{1,0:T(8,128)(2,1)S(1)}, u32[]{:S(2)}, u32[]{:S(2)}) collective-permute-start(bf16[528,512]{1,0:T(8,128)(2,1)} %get-tuple-element.208), channel_id=1, source_target_pairs={{2,0},{10,1},{4,2},{12,3},{6,4},{14,5},{0,6},{8,7},{3,8},{11,9},{5... | collective-permute-start | bytes 1622024 | tf_op jit(solution)/shard_map/ppermute | solution.py:1007
  164.0 40.5 %collective-permute-start.13 = (bf16[528,512]{1,0:T(8,128)(2,1)}, bf16[528,512]{1,0:T(8,128)(2,1)S(1)}, u32[]{:S(2)}, u32[]{:S(2)}) collective-permute-start(bf16[528,512]{1,0:T(8,128)(2,1)} %get-tuple-element.209), channel_id=1, source_target_pairs={{6,0},{14,1},{0,2},{8,3},{2,4},{10,5},{4,6},{12,7},{7,8},{15,9},{1... | collective-permute-start | bytes 1622024 | tf_op jit(solution)/shard_map/ppermute | solution.py:1007
  164.6 39.9 %collective-permute-start.14 = (bf16[1296,512]{1,0:T(8,128)(2,1)}, bf16[1296,512]{1,0:T(8,128)(2,1)}, u32[]{:S(2)}, u32[]{:S(2)}) collective-permute-start(bf16[1296,512]{1,0:T(8,128)(2,1)} %get-tuple-element.210), channel_id=1, source_target_pairs={{0,8},{1,9},{2,10},{3,11},{4,12},{5,13},{6,14},{7,15},{8,0},{9,1},... | collective-permute-start | bytes 3981320 | tf_op jit(solution)/shard_map/ppermute | solution.py:1064
  208.4 43.0 %collective-permute-start.19 = (bf16[2,4,2048,128]{3,2,1,0:T(8,128)(2,1)}, bf16[2,4,2048,128]{3,2,1,0:T(8,128)(2,1)}, u32[]{:S(2)}, u32[]{:S(2)}) collective-permute-start(bf16[2,4,2048,128]{3,2,1,0:T(8,128)(2,1)} %get-tuple-element.223), channel_id=1, source_target_pairs={{0,8},{1,9},{2,10},{3,11},{4,12},{5,13},{6,14},{7,15},{8,0},{9,1},... | collective-permute-start | bytes 12582920 | tf_op jit(solution)/shard_map/ppermute | solution.py:1070
  208.5 42.9 %collective-permute-start.15 = (bf16[336,512]{1,0:T(8,128)(2,1)S(1)}, bf16[336,512]{1,0:T(8,128)(2,1)}, u32[]{:S(2)}, u32[]{:S(2)}) collective-permute-start(bf16[336,512]{1,0:T(8,128)(2,1)S(1)} %get-tuple-element.219), channel_id=1, source_target_pairs={{0,1},{1,0},{2,3},{3,2},{4,5},{5,4},{6,7},{7,6},{8,9},{9,8},{10,11... | collective-permute-start | bytes 1032200 | tf_op jit(solution)/shard_map/ppermute | solution.py:921
  209.4 42.0 %collective-permute-start.16 = (bf16[336,512]{1,0:T(8,128)(2,1)S(1)}, bf16[336,512]{1,0:T(8,128)(2,1)}, u32[]{:S(2)}, u32[]{:S(2)}) collective-permute-start(bf16[336,512]{1,0:T(8,128)(2,1)S(1)} %get-tuple-element.220), channel_id=1, source_target_pairs={{0,16},{1,17},{2,18},{3,19},{4,20},{5,21},{6,22},{7,23},{8,24},{9,... | collective-permute-start | bytes 1032200 | tf_op jit(solution)/shard_map/ppermute | solution.py:921
  210.9 40.5 %collective-permute-start.17 = (bf16[336,512]{1,0:T(8,128)(2,1)S(1)}, bf16[336,512]{1,0:T(8,128)(2,1)S(1)}, u32[]{:S(2)}, u32[]{:S(2)}) collective-permute-start(bf16[336,512]{1,0:T(8,128)(2,1)S(1)} %get-tuple-element.221), channel_id=1, source_target_pairs={{0,17},{1,16},{2,19},{3,18},{4,21},{5,20},{6,23},{7,22},{8,25},{9,... | collective-permute-start | bytes 1032200 | tf_op jit(solution)/shard_map/ppermute | solution.py:921
  212.0 39.4 %collective-permute-start.18 = (bf16[528,512]{1,0:T(8,128)(2,1)}, bf16[528,512]{1,0:T(8,128)(2,1)S(1)}, u32[]{:S(2)}, u32[]{:S(2)}) collective-permute-start(bf16[528,512]{1,0:T(8,128)(2,1)} %get-tuple-element.222), channel_id=1, source_target_pairs={{4,0},{12,1},{6,2},{14,3},{0,4},{8,5},{2,6},{10,7},{5,8},{13,9},{7... | collective-permute-start | bytes 1622024 | tf_op jit(solution)/shard_map/ppermute | solution.py:1007
  256.4 16.7 %collective-permute-start.20 = (bf16[528,512]{1,0:T(8,128)(2,1)}, bf16[528,512]{1,0:T(8,128)(2,1)S(1)}, u32[]{:S(2)}, u32[]{:S(2)}) collective-permute-start(bf16[528,512]{1,0:T(8,128)(2,1)} %shard_map.263), channel_id=1, source_target_pairs={{6,0},{14,1},{0,2},{8,3},{2,4},{10,5},{4,6},{12,7},{7,8},{15,9},{1... | collective-permute-start | bytes 1622024 | tf_op jit(solution)/shard_map/ppermute | solution.py:1007
  279.2 20.0 %collective-permute-start.25 = (bf16[528,512]{1,0:T(8,128)(2,1)}, bf16[528,512]{1,0:T(8,128)(2,1)S(1)}, u32[]{:S(2)}, u32[]{:S(2)}) collective-permute-start(bf16[528,512]{1,0:T(8,128)(2,1)} %get-tuple-element.248), channel_id=1, source_target_pairs={{2,0},{10,1},{4,2},{12,3},{6,4},{14,5},{0,6},{8,7},{3,8},{11,9},{5... | collective-permute-start | bytes 1622024 | tf_op jit(solution)/shard_map/ppermute | solution.py:1007
  300.2 18.0 %collective-permute-start.29 = (bf16[528,512]{1,0:T(8,128)(2,1)}, bf16[528,512]{1,0:T(8,128)(2,1)}, u32[]{:S(2)}, u32[]{:S(2)}) collective-permute-start(bf16[528,512]{1,0:T(8,128)(2,1)} %get-tuple-element.256), channel_id=1, source_target_pairs={{0,0},{8,1},{2,2},{10,3},{4,4},{12,5},{6,6},{14,7},{1,8},{9,9},{3,... | collective-permute-start | bytes 1622024 | tf_op jit(solution)/shard_map/ppermute | solution.py:1007
  330.4 16.5 %collective-permute-start.34 = (bf16[512,512]{1,0:T(8,128)(2,1)S(1)}, bf16[512,512]{1,0:T(8,128)(2,1)S(1)}, u32[]{:S(2)}, u32[]{:S(2)}) collective-permute-start(bf16[512,512]{1,0:T(8,128)(2,1)S(1)} %pad_maximum_fusion.4), channel_id=1, source_target_pairs={{0,1},{1,0},{2,3},{3,2},{4,5},{5,4},{6,7},{7,6},{8,9},{9,8},{10,11... | collective-permute-start | bytes 1572872 | tf_op jit(solution)/shard_map/ppermute | solution.py:921
  334.1 17.7 %collective-permute-start.35 = (bf16[512,512]{1,0:T(8,128)(2,1)S(1)}, bf16[512,512]{1,0:T(8,128)(2,1)S(1)}, u32[]{:S(2)}, u32[]{:S(2)}) collective-permute-start(bf16[512,512]{1,0:T(8,128)(2,1)S(1)} %pad_maximum_fusion.4), channel_id=1, source_target_pairs={{0,16},{1,17},{2,18},{3,19},{4,20},{5,21},{6,22},{7,23},{8,24},{9,... | collective-permute-start | bytes 1572872 | tf_op jit(solution)/shard_map/ppermute | solution.py:921
  334.6 28.7 %collective-permute-start.36 = (bf16[512,512]{1,0:T(8,128)(2,1)S(1)}, bf16[512,512]{1,0:T(8,128)(2,1)S(1)}, u32[]{:S(2)}, u32[]{:S(2)}) collective-permute-start(bf16[512,512]{1,0:T(8,128)(2,1)S(1)} %pad_maximum_fusion.4), channel_id=1, source_target_pairs={{0,17},{1,16},{2,19},{3,18},{4,21},{5,20},{6,23},{7,22},{8,25},{9,... | collective-permute-start | bytes 1572872 | tf_op jit(solution)/shard_map/ppermute | solution.py:921
  335.7 27.7 %collective-permute-start.37 = (bf16[528,512]{1,0:T(8,128)(2,1)S(1)}, bf16[528,512]{1,0:T(8,128)(2,1)S(1)}, u32[]{:S(2)}, u32[]{:S(2)}) collective-permute-start(bf16[528,512]{1,0:T(8,128)(2,1)S(1)} %copy-done.14), channel_id=1, source_target_pairs={{4,0},{12,1},{6,2},{14,3},{0,4},{8,5},{2,6},{10,7},{5,8},{13,9},{7... | collective-permute-start | bytes 1622024 | tf_op jit(solution)/shard_map/ppermute | solution.py:1007
  (46 other events, 555.9 us)

commit v5 on v4

--- a/solution.py
+++ b/solution.py
@@ -630,64 +630,50 @@
 def backward_kernel(scale_k, scale_q, carried, q_ref, g_ref, d_ref, p_ref, k_ref, v_ref, *refs):
     if carried:
         before, refs = refs[0], refs[1:]
-    kv_ref, dq_ref, dq_sum, ds, q_t, g_t = refs
-    c = pl.program_id(1)
-
-    @pl.when(c == 0)
-    def _():
-        q_t[...] = q_ref[0].T
-        g_t[...] = g_ref[0].T
-        dq_sum[...] = before[0] if carried else jnp.zeros_like(dq_sum)
-
+    kv_ref, dq_ref, ds = refs
     keys, values = k_ref[0], v_ref[0]
-    chunk = keys.shape[0]
     for start in range(0, p_ref.shape[1], ROWS_STEP):
         at = slice(start, start + ROWS_STEP)
         soft_grad = dot(g_ref[0, at, :], values, 1, 1)
-        delta = jnp.concatenate([d_ref[0, at, :]] * (chunk // LANES), axis=1)
+        delta = jnp.concatenate([d_ref[0, at, :]] * (keys.shape[0] // LANES), axis=1)
         score_grad = (p_ref[0, at, :].astype(F32) * (soft_grad - delta)).astype(BF16)
         ds[at, :] = score_grad
-        dq_sum[at, :] += dot(score_grad, keys, 1, 0)
-    dv = dot(g_t[...], p_ref[0], 1, 0).T
-    dk = dot(q_t[...], ds[...], 1, 0).T * scale_k
+        query_grad = dot(score_grad, keys, 1, 0)
+        if carried:
+            query_grad = query_grad + before[0, at, :]
+        dq_ref[0, at, :] = (query_grad * scale_q).astype(dq_ref.dtype)
+    dv = dot(g_ref[0].T, p_ref[0], 1, 0).T
+    dk = dot(q_ref[0].T, ds[...], 1, 0).T * scale_k
     kv_ref[0, 0] = dk.astype(BF16)
     kv_ref[1, 0] = dv.astype(BF16)
 
-    @pl.when(c == pl.num_programs(1) - 1)
-    def _():
-        dq_ref[0] = (dq_sum[...] * scale_q).astype(dq_ref.dtype)
-
-
-def attention_backward(q, g, d, p, k, v, scale_k, scale_q, chunk, first, chunks, before=None):
+
+def attention_backward(q, g, d, p, k, v, scale_k, scale_q, half, before=None):
     heads, total, hd = q.shape
-    row = lambda h, c: (h, 0, 0)
-    key = lambda h, c: (h, c + first, 0)
+    keys = k.shape[1] // 2
+    row = lambda h: (h, 0, 0)
+    key = lambda h: (h, half, 0)
     by_row = ((1, total, hd), row)
     carried = before is not None
     return kernel_call(
         partial(backward_kernel, scale_k, scale_q, carried),
-        (heads, chunks),
+        (heads,),
         [
             by_row,
             by_row,
             by_row,
-            ((1, total, chunk), lambda h, c: (h, 0, c + first)),
-            ((1, chunk, hd), key),
-            ((1, chunk, hd), key),
+            ((1, total, keys), lambda h: (h, 0, half)),
+            ((1, keys, hd), key),
+            ((1, keys, hd), key),
         ]
         + [by_row] * carried,
         [
-            ((2, 1, chunk, hd), lambda h, c: (0, h, c, 0), (2, heads, chunks * chunk, hd), BF16),
+            ((2, 1, keys, hd), lambda h: (0, h, 0, 0), (2, heads, keys, hd), BF16),
             (*by_row, (heads, total, hd), BF16 if carried else F32),
         ],
-        [
-            pltpu.VMEM((total, hd), F32),
-            pltpu.VMEM((total, chunk), BF16),
-            pltpu.VMEM((hd, total), BF16),
-            pltpu.VMEM((hd, total), BF16),
-        ],
-        12 * heads * total * chunk * chunks * hd,
-        2 * heads * total * chunk * chunks,
+        [pltpu.VMEM((total, keys), BF16)],
+        12 * heads * total * keys * hd,
+        2 * heads * total * keys,
         q,
         g,
         d,
@@ -1051,7 +1037,6 @@
 
     stages, stages_of = summing(groups, members)
     scale_k = 1.0 / log2e
-    chunk = blocks * context // 2
 
     added = lambda parts: sum(part.astype(F32) for part in parts)
 
@@ -1063,15 +1048,19 @@
     *out, given, grads = tie(*out, given, grads)
     came = lax.ppermute(given, AXES, across)
     home = [homeward(out[j], r) for j, r in enumerate(order[:-2])]
-    kv_other, dq = attention_backward(q, grads, delta, p, k, v, scale_k, 1.0, chunk, 2, 2)
+    kv_other, dq = attention_backward(q, grads, delta, p, k, v, scale_k, 1.0, 1)
     *home, came, kv_other, grads = tie(*home, came, kv_other, grads)
-    pieces, send, early_join = start(stages[1], [keep, came], VECTORS)
+    early_parts = [keep, came]
+    pieces, send, _ = start(stages[1], early_parts, VECTORS)
     *pieces, kv_other, far_out, grads = tie(*pieces, kv_other, out[-1], grads)
     kv_came = lax.ppermute(kv_other, AXES, across)
     early_came = send(pieces)
     home.append(homeward(far_out, far))
-    kv_own, dq = attention_backward(q, grads, delta, p, k, v, scale_k, scale, chunk, 0, 2, dq)
-    *early_came, home[-1], kv_came, kv_own = tie(*early_came, home[-1], kv_came, kv_own)
+    kv_own, dq = attention_backward(q, grads, delta, p, k, v, scale_k, scale, 0, dq)
+    *early_came, home[-1], kv_came, kv_own, keep, came = tie(
+        *early_came, home[-1], kv_came, kv_own, *early_parts
+    )
+    early_parts = [keep, came]
 
     token_of = lambda places, after: finish(
         places, after, kv_own, kv_came, dq, kinds, blocks
@@ -1093,7 +1082,7 @@
     two = homeward(two, order[0])
     *came, two = tie(*came, two)
     late = added(join(came))
-    early = added(early_join(early_came))
+    early = added([stages[1][0](list(early_parts), VECTORS)[0], *early_came])
 
     along = members // 2
     shares = ((early.shape[0] - VECTORS) // along, late.shape[0] // along)

time: 381 us -> 377 us (0.990)
  no operation moved by 1% of the time
where the time goes in v5:
time: 377 us; the launch traced here: 372 us
  Pallas kernels  211 us (56%)
  starting transfers between devices  64.7 us (17%)
  waiting for transfers between devices  63.3 us (17%)
  other arithmetic  15.9 us (4%)
  local copies, waits for them, and re-layouts  15.1 us (4%)
    pallas_call x15, Pallas kernels, kernel_call(): pl.pallas_call(run, grid=grid, in_specs=[pl.BlockSpec(memory_space=index)...  211 us
    ppermute x15, waiting for transfers between devices, swap(): lax.ppermute(array, AXES, [(number(g, c), number(*move(g, c, s))) for g,...  47.1 us
    ppermute x8, starting transfers between devices, outward(): return lax.ppermute(block, AXES, route(r))  22.8 us
    ppermute x15, starting transfers between devices, swap(): lax.ppermute(array, AXES, [(number(g, c), number(*move(g, c, s))) for g,...  21 us
    ppermute x8, waiting for transfers between devices, outward(): return lax.ppermute(block, AXES, route(r))  14.6 us
    ppermute x8, starting transfers between devices, homeward(): return lax.ppermute(block, AXES, route(r, True))  12.7 us
  transfers between devices with their start and end apart: 39, of which 10 were waited for; matrix products, arithmetic and copies ran while one was open for 5% of the time, Pallas kernels for 45%

profile of v5, /device:TPU:0, one launch (start us, length us, event | category | flops | bytes accessed | tf_op | source)
XLA Modules:
  0.0 371.7 jit_solution(14419810802582392194)
XLA Ops:
  8.4 12.1 %collective-permute-done.5.refs_0_ = bf16[528,512]{1,0:T(8,128)(2,1)} collective-permute-done((bf16[528,512]{1,0:T(8,128)(2,1)S(1)}, bf16[528,512]{1,0:T(8,128)(2,1)}, u32[]{:S(2)}, u32[]{:S(2)}) %collective-permute-start.5) | collective-permute-done | bytes 540704 | tf_op jit(solution)/shard_map/ppermute | solution.py:990
  21.7 11.4 %collective-permute-start = (bf16[528,512]{1,0:T(8,128)(2,1)S(1)}, bf16[528,512]{1,0:T(8,128)(2,1)S(1)}, u32[]{:S(2)}, u32[]{:S(2)}) collective-permute-start(bf16[528,512]{1,0:T(8,128)(2,1)S(1)} %get-tuple-element.334), channel_id=1, source_target_pairs={{0,4},{1,12},{2,6},{3,14},{4,0},{5,8},{6,2},{7,10},{8,5},{9,13},{1... | collective-permute-start | bytes 1622024 | tf_op jit(solution)/shard_map/ppermute | solution.py:990
  38.2 4.9 %shard_map.254 = (bf16[4,2,4,512,128]{4,3,2,1,0:T(8,128)(2,1)}, bf16[4,2,4,512,128]{4,3,2,1,0:T(8,128)(2,1)}, bf16[4,2112,128]{2,1,0:T(8,128)(2,1)}, bf16[4,528,512]{2,1,0:T(8,128)(2,1)}) custom-call(bf16[528,512]{1,0:T(8,128)(2,1)} %collective-permute-done.5.refs_0_, bf16[512,512]{1,0:T(8,128)(2,1)} %refs_4_.13, ...), custom_call_target="tpu_custom_call" | custom-call | flops 1350565888 | bytes 4227072 | tf_op jit(solution)/shard_map/pallas_call | solution.py:292
  43.9 4.9 %shard_map.255 = (bf16[4,2,4,512,128]{4,3,2,1,0:T(8,128)(2,1)}, bf16[4,2,4,512,128]{4,3,2,1,0:T(8,128)(2,1)}, bf16[4,2112,128]{2,1,0:T(8,128)(2,1)}, bf16[4,528,512]{2,1,0:T(8,128)(2,1)}) custom-call(bf16[528,512]{1,0:T(8,128)(2,1)} %collective-permute-done.3.refs_0_, ...), custom_call_target="tpu_custom_call", output_to_operand_aliasing={{0}: (5, {}), {1}: (6, {}), {2}: (7, {}), {3}: (8, {})} | custom-call | flops 1350565888 | bytes 4227072 | tf_op jit(solution)/shard_map/pallas_call | solution.py:292
  49.6 5.0 %shard_map.256 = (bf16[4,2,4,512,128]{4,3,2,1,0:T(8,128)(2,1)}, bf16[4,2,4,512,128]{4,3,2,1,0:T(8,128)(2,1)}, bf16[4,2112,128]{2,1,0:T(8,128)(2,1)}, bf16[4,528,512]{2,1,0:T(8,128)(2,1)}) custom-call(bf16[528,512]{1,0:T(8,128)(2,1)} %copy-done.17, ...), custom_call_target="tpu_custom_call", output_to_operand_aliasing={{0}: (5, {}), {1}: (6, {}), {2}: (7, {}), {3}: (8, {})} | custom-call | flops 1350565888 | bytes 4227072 | tf_op jit(solution)/shard_map/pallas_call | solution.py:292
  59.5 3.8 %shard_map.257 = (bf16[4,2,4,512,128]{4,3,2,1,0:T(8,128)(2,1)}, bf16[4,2,4,512,128]{4,3,2,1,0:T(8,128)(2,1)}, bf16[4,2112,128]{2,1,0:T(8,128)(2,1)}, bf16[4,528,512]{2,1,0:T(8,128)(2,1)}) custom-call(bf16[528,512]{1,0:T(8,128)(2,1)} %copy-done.16, ...), custom_call_target="tpu_custom_call", output_to_operand_aliasing={{0}: (4, {}), {1}: (5, {}), {2}: (6, {}), {3}: (7, {})} | custom-call | flops 1350565888 | bytes 4227072 | tf_op jit(solution)/shard_map/pallas_call | solution.py:292
  63.6 3.6 collective-permute-start.9
  72.8 52.0 %shard_map.259 = (bf16[4,2112,4096]{2,1,0:T(8,128)(2,1)}, f32[2112,512]{1,0:T(8,128)}, f32[4,2112,128]{2,1,0:T(8,128)}) custom-call(bf16[4,2112,128]{2,1,0:T(8,128)(2,1)} %get-tuple-element.184.refs_0_, bf16[4,4096,128]{2,1,0:T(8,128)(2,1)} %bitcast.64, bf16[4,4096,128]{2,1,0:T(8,128)(2,1)} %bitcast.67), custom_call_target="tpu_custom_call" | custom-call | flops 35433480192 | bytes 69206016 | tf_op jit(solution)/shard_map/pallas_call | solution.py:292
  125.6 36.6 %shard_map.260 = (bf16[528,512]{1,0:T(8,128)(2,1)}, bf16[528,512]{1,0:T(8,128)(2,1)}, bf16[528,512]{1,0:T(8,128)(2,1)}, bf16[528,512]{1,0:T(8,128)(2,1)}, bf16[2...) custom-call(s32[1]{0:T(128)} %bitcast.refs_0_, ...), custom_call_target="tpu_custom_call" | custom-call | flops 16609443840 | bytes 45088768 | tf_op jit(solution)/shard_map/pallas_call | solution.py:292
  167.5 35.4 %shard_map.261 = (bf16[2,4,2048,128]{3,2,1,0:T(8,128)(2,1)}, f32[4,2112,128]{2,1,0:T(8,128)}) custom-call(bf16[4,2112,128]{2,1,0:T(8,128)(2,1)} %get-tuple-element.184.refs_0_, bf16[4,2112,128]{2,1,0:T(8,128)(2,1)} %get-tuple-element.226.refs_1_, f32[4,2112,128]{2,1,0:T(8,128)} %get-tuple-element.214.refs_2_, ...), custom_call_target="tpu_custom_call" | custom-call | flops 26575110144 | bytes 34603008 | tf_op jit(solution)/shard_map/pallas_call | solution.py:292
  212.6 35.0 %shard_map.262 = (bf16[2,4,2048,128]{3,2,1,0:T(8,128)(2,1)}, bf16[4,2112,128]{2,1,0:T(8,128)(2,1)}) custom-call(bf16[4,2112,128]{2,1,0:T(8,128)(2,1)} %get-tuple-element.184.refs_0_, bf16[4,2112,128]{2,1,0:T(8,128)(2,1)} %get-tuple-element.226.refs_1_, f32[4,2112,128]{2,1,0:T(8,128)} %get-tuple-element.214.refs_2_, ...), custom_call_target="tpu_custom_call" | custom-call | flops 26575110144 | bytes 34603008 | tf_op jit(solution)/shard_map/pallas_call | solution.py:292
  248.5 4.1 %shard_map.263 = bf16[528,512]{1,0:T(8,128)(2,1)} custom-call(bf16[4,528,512]{2,1,0:T(8,128)(2,1)} %bitcast.74, bf16[4,4,528,128]{3,2,1,0:T(8,128)(2,1)} %bitcast.70, bf16[2,4,4,512,128]{4,3,2,1,0:T(8,128)(2,1)} %bitcast.61, bf16[2,4,4,512,128]{4,3,2,1,0:T(8,128)(2,1)} %bitcast.16.refs_3_, bf16[512,512]{1,0:T(8,128)(2,1)} %refs_4_.13, ...), custom_call_target="tpu_custom_call" | custom-call | flops 813694976 | bytes 4767744 | tf_op jit(solution)/shard_map/pallas_call | solution.py:292
  253.7 5.4 %shard_map.264 = (bf16[528,512]{1,0:T(8,128)(2,1)}, bf16[528,512]{1,0:T(8,128)(2,1)}) custom-call(bf16[4,528,512]{2,1,0:T(8,128)(2,1)} %bitcast.75, bf16[4,4,528,128]{3,2,1,0:T(8,128)(2,1)} %bitcast.71, bf16[2,4,4,512,128]{4,3,2,1,0:T(8,128)(2,1)} %bitcast.62, bf16[2,4,4,512,128]{4,3,2,1,0:T(8,128)(2,1)} %bitcast.16.refs_3_, bf16[512,512]{1,0:T(8,128)(2,1)} %refs_4_.13, ...), custom_call_target="tpu_custom_call" | custom-call | flops 1627389952 | bytes 9535488 | tf_op jit(solution)/shard_map/pallas_call | solution.py:292
  259.1 8.7 %shard_map.265 = (f32[768,512]{1,0:T(8,128)}, bf16[768,512]{1,0:T(8,128)(2,1)}) custom-call(s32[1]{0:T(128)} %bitcast.refs_0_, bf16[4,528,512]{2,1,0:T(8,128)(2,1)} %get-tuple-element.241.refs_1_, bf16[4,2112,128]{2,1,0:T(8,128)(2,1)} %get-tuple-element.235.refs_2_, bf16[2,4,2048,128]{3,2,1,0:T(8,128)(2,1)} %get-tuple-element.236.refs_3_, ...), custom_call_target="tpu_custom_call" | custom-call | flops 3254779904 | bytes 12713984 | tf_op jit(solution)/shard_map/pallas_call | solution.py:292
  270.2 4.2 %shard_map.266 = bf16[528,512]{1,0:T(8,128)(2,1)} custom-call(bf16[4,528,512]{2,1,0:T(8,128)(2,1)} %bitcast.76, bf16[4,4,528,128]{3,2,1,0:T(8,128)(2,1)} %bitcast.72, bf16[2,4,4,512,128]{4,3,2,1,0:T(8,128)(2,1)} %bitcast.63, bf16[2,4,4,512,128]{4,3,2,1,0:T(8,128)(2,1)} %bitcast.16.refs_3_, bf16[512,512]{1,0:T(8,128)(2,1)} %refs_4_.13, ...), custom_call_target="tpu_custom_call" | custom-call | flops 813694976 | bytes 4767744 | tf_op jit(solution)/shard_map/pallas_call | solution.py:292
  284.0 7.7 %collective-permute-done.22 = bf16[192,512]{1,0:T(8,128)(2,1)S(1)} collective-permute-done((bf16[192,512]{1,0:T(8,128)(2,1)S(1)}, bf16[192,512]{1,0:T(8,128)(2,1)S(1)}, u32[]{:S(2)}, u32[]{:S(2)}) %collective-permute-start.22) | collective-permute-done | bytes 196640 | tf_op jit(solution)/shard_map/ppermute | solution.py:907
  291.7 5.0 %collective-permute-done.24 = bf16[192,512]{1,0:T(8,128)(2,1)S(1)} collective-permute-done((bf16[192,512]{1,0:T(8,128)(2,1)S(1)}, bf16[192,512]{1,0:T(8,128)(2,1)S(1)}, u32[]{:S(2)}, u32[]{:S(2)}) %collective-permute-start.24) | collective-permute-done | bytes 196640 | tf_op jit(solution)/shard_map/ppermute | solution.py:907
  308.2 5.9 %collective-permute-done.27 = bf16[144,512]{1,0:T(8,128)(2,1)S(1)} collective-permute-done((bf16[144,512]{1,0:T(8,128)(2,1)S(1)}, bf16[144,512]{1,0:T(8,128)(2,1)S(1)}, u32[]{:S(2)}, u32[]{:S(2)}) %collective-permute-start.27) | collective-permute-done | bytes 147488 | tf_op jit(solution)/shard_map/ppermute | solution.py:907
  323.6 5.0 %collective-permute-done.30 = bf16[128,512]{1,0:T(8,128)(2,1)S(1)} collective-permute-done((bf16[128,512]{1,0:T(8,128)(2,1)S(1)}, bf16[128,512]{1,0:T(8,128)(2,1)S(1)}, u32[]{:S(2)}, u32[]{:S(2)}) %collective-permute-start.30) | collective-permute-done | bytes 131104 | tf_op jit(solution)/shard_map/ppermute | solution.py:907
  336.3 6.9 %collective-permute-done.34 = bf16[512,512]{1,0:T(8,128)(2,1)S(1)} collective-permute-done((bf16[512,512]{1,0:T(8,128)(2,1)S(1)}, bf16[512,512]{1,0:T(8,128)(2,1)S(1)}, u32[]{:S(2)}, u32[]{:S(2)}) %collective-permute-start.34) | collective-permute-done | bytes 524320 | tf_op jit(solution)/shard_map/ppermute | solution.py:907
  343.2 7.8 %collective-permute-done.35 = bf16[512,512]{1,0:T(8,128)(2,1)S(1)} collective-permute-done((bf16[512,512]{1,0:T(8,128)(2,1)S(1)}, bf16[512,512]{1,0:T(8,128)(2,1)S(1)}, u32[]{:S(2)}, u32[]{:S(2)}) %collective-permute-start.35) | collective-permute-done | bytes 524320 | tf_op jit(solution)/shard_map/ppermute | solution.py:907
  351.0 8.7 %collective-permute-done.36 = bf16[512,512]{1,0:T(8,128)(2,1)S(1)} collective-permute-done((bf16[512,512]{1,0:T(8,128)(2,1)S(1)}, bf16[512,512]{1,0:T(8,128)(2,1)S(1)}, u32[]{:S(2)}, u32[]{:S(2)}) %collective-permute-start.36) | collective-permute-done | bytes 524320 | tf_op jit(solution)/shard_map/ppermute | solution.py:907
  362.4 3.9 %shard_map.267 = (f32[512,512]{1,0:T(8,128)}, f32[512,512]{1,0:T(8,128)}, f32[512,512]{1,0:T(8,128)}, f32[512,512]{1,0:T(8,128)}, f32[512,1024]{1,0:T(8,128)}, /*index=5*/f32[1024,512]{1,0:T(8,128)}) custom-call(s32[3]{0:T(128)} %get-tuple-element.347.refs_0_, bf16[2048,512]{1,0:T(8,128)(2,1)} %copy-done.1), custom_call_target="tpu_custom_call" | custom-call | bytes 6291456 | tf_op jit(solution)/shard_map/pallas_call | solution.py:292
  367.5 4.0 %shard_map.268 = (f32[512,512]{1,0:T(8,128)}, f32[512,512]{1,0:T(8,128)}, f32[512,512]{1,0:T(8,128)}, f32[512,512]{1,0:T(8,128)}, f32[512,1024]{1,0:T(8,128)}, /*index=5*/f32[1024,512]{1,0:T(8,128)}) custom-call(s32[3]{0:T(128)} %get-tuple-element.348.refs_0_, ...), custom_call_target="tpu_custom_call", output_to_operand_aliasing={{0}: (2, {}), {1}: (3, {}), {2}: (4, {}), {3}: (5, {}), {4}... | custom-call | bytes 6291456 | tf_op jit(solution)/shard_map/pallas_call | solution.py:292
  (187 shorter events, 87.9 us)
Async XLA Ops:
  2.6 17.9 %collective-permute-start.5 = (bf16[528,512]{1,0:T(8,128)(2,1)S(1)}, bf16[528,512]{1,0:T(8,128)(2,1)}, u32[]{:S(2)}, u32[]{:S(2)}) collective-permute-start(bf16[528,512]{1,0:T(8,128)(2,1)S(1)} %get-tuple-element.332), channel_id=1, source_target_pairs={{0,2},{1,10},{2,4},{3,12},{4,6},{5,14},{6,0},{7,8},{8,3},{9,11},{1... | collective-permute-start | bytes 1622024 | tf_op jit(solution)/shard_map/ppermute | solution.py:990
  5.6 31.0 %collective-permute-start.3 = (bf16[528,512]{1,0:T(8,128)(2,1)S(1)}, bf16[528,512]{1,0:T(8,128)(2,1)}, u32[]{:S(2)}, u32[]{:S(2)}) collective-permute-start(bf16[528,512]{1,0:T(8,128)(2,1)S(1)} %get-tuple-element.335), channel_id=1, source_target_pairs={{0,6},{1,14},{2,0},{3,8},{4,2},{5,10},{6,4},{7,12},{8,7},{9,15},{1... | collective-permute-start | bytes 1622024 | tf_op jit(solution)/shard_map/ppermute | solution.py:990
  7.7 30.3 %collective-permute-start.1 = (bf16[528,512]{1,0:T(8,128)(2,1)S(1)}, bf16[528,512]{1,0:T(8,128)(2,1)S(1)}, u32[]{:S(2)}, u32[]{:S(2)}) collective-permute-start(bf16[528,512]{1,0:T(8,128)(2,1)S(1)} %get-tuple-element.333), channel_id=1, source_target_pairs={{0,0},{1,8},{2,2},{3,10},{4,4},{5,12},{6,6},{7,14},{8,1},{9,9},{10... | collective-permute-start | bytes 1622024 | tf_op jit(solution)/shard_map/ppermute | solution.py:990
  20.5 17.7 %collective-permute-start.6 = (bf16[528,512]{1,0:T(8,128)(2,1)}, bf16[528,512]{1,0:T(8,128)(2,1)}, u32[]{:S(2)}, u32[]{:S(2)}) collective-permute-start(bf16[528,512]{1,0:T(8,128)(2,1)} %collective-permute-done.5.refs_0_), channel_id=1, source_target_pairs={{0,8},{1,9},{2,10},{3,11},{4,12},{5,13},{6,14},{7,15},{8,0},{9,1},... | collective-permute-start | bytes 1622024 | tf_op jit(solution)/shard_map/ppermute | solution.py:1007
  21.7 35.5 %collective-permute-start = (bf16[528,512]{1,0:T(8,128)(2,1)S(1)}, bf16[528,512]{1,0:T(8,128)(2,1)S(1)}, u32[]{:S(2)}, u32[]{:S(2)}) collective-permute-start(bf16[528,512]{1,0:T(8,128)(2,1)S(1)} %get-tuple-element.334), channel_id=1, source_target_pairs={{0,4},{1,12},{2,6},{3,14},{4,0},{5,8},{6,2},{7,10},{8,5},{9,13},{1... | collective-permute-start | bytes 1622024 | tf_op jit(solution)/shard_map/ppermute | solution.py:990
  63.4 61.5 %collective-permute-start.8 = (bf16[528,512]{1,0:T(8,128)(2,1)S(1)}, bf16[528,512]{1,0:T(8,128)(2,1)S(1)}, u32[]{:S(2)}, u32[]{:S(2)}) collective-permute-start(bf16[528,512]{1,0:T(8,128)(2,1)S(1)} %get-tuple-element.194), channel_id=1, source_target_pairs={{0,2},{1,10},{2,4},{3,12},{4,6},{5,14},{6,0},{7,8},{8,3},{9,11},{1... | collective-permute-start | bytes 1622024 | tf_op jit(solution)/shard_map/ppermute | solution.py:990
  63.6 61.2 %collective-permute-start.9 = (bf16[528,512]{1,0:T(8,128)(2,1)S(1)}, bf16[528,512]{1,0:T(8,128)(2,1)}, u32[]{:S(2)}, u32[]{:S(2)}) collective-permute-start(bf16[528,512]{1,0:T(8,128)(2,1)S(1)} %get-tuple-element.195), channel_id=1, source_target_pairs={{0,6},{1,14},{2,0},{3,8},{4,2},{5,10},{6,4},{7,12},{8,7},{9,15},{1... | collective-permute-start | bytes 1622024 | tf_op jit(solution)/shard_map/ppermute | solution.py:990
  67.2 57.7 %collective-permute-start.10 = (bf16[528,512]{1,0:T(8,128)(2,1)S(1)}, bf16[528,512]{1,0:T(8,128)(2,1)}, u32[]{:S(2)}, u32[]{:S(2)}) collective-permute-start(bf16[528,512]{1,0:T(8,128)(2,1)S(1)} %get-tuple-element.196), channel_id=1, source_target_pairs={{0,0},{1,8},{2,2},{3,10},{4,4},{5,12},{6,6},{7,14},{8,1},{9,9},{10... | collective-permute-start | bytes 1622024 | tf_op jit(solution)/shard_map/ppermute | solution.py:990
  68.9 56.0 %collective-permute-start.11 = (bf16[528,512]{1,0:T(8,128)(2,1)S(1)}, bf16[528,512]{1,0:T(8,128)(2,1)}, u32[]{:S(2)}, u32[]{:S(2)}) collective-permute-start(bf16[528,512]{1,0:T(8,128)(2,1)S(1)} %get-tuple-element.197), channel_id=1, source_target_pairs={{0,4},{1,12},{2,6},{3,14},{4,0},{5,8},{6,2},{7,10},{8,5},{9,13},{1... | collective-permute-start | bytes 1622024 | tf_op jit(solution)/shard_map/ppermute | solution.py:990
  162.3 40.6 %collective-permute-start.12 = (bf16[528,512]{1,0:T(8,128)(2,1)}, bf16[528,512]{1,0:T(8,128)(2,1)S(1)}, u32[]{:S(2)}, u32[]{:S(2)}) collective-permute-start(bf16[528,512]{1,0:T(8,128)(2,1)} %get-tuple-element.210), channel_id=1, source_target_pairs={{2,0},{10,1},{4,2},{12,3},{6,4},{14,5},{0,6},{8,7},{3,8},{11,9},{5... | collective-permute-start | bytes 1622024 | tf_op jit(solution)/shard_map/ppermute | solution.py:993
  163.7 39.2 %collective-permute-start.13 = (bf16[528,512]{1,0:T(8,128)(2,1)}, bf16[528,512]{1,0:T(8,128)(2,1)S(1)}, u32[]{:S(2)}, u32[]{:S(2)}) collective-permute-start(bf16[528,512]{1,0:T(8,128)(2,1)} %get-tuple-element.211), channel_id=1, source_target_pairs={{6,0},{14,1},{0,2},{8,3},{2,4},{10,5},{4,6},{12,7},{7,8},{15,9},{1... | collective-permute-start | bytes 1622024 | tf_op jit(solution)/shard_map/ppermute | solution.py:993
  164.4 38.6 %collective-permute-start.14 = (bf16[1296,512]{1,0:T(8,128)(2,1)}, bf16[1296,512]{1,0:T(8,128)(2,1)}, u32[]{:S(2)}, u32[]{:S(2)}) collective-permute-start(bf16[1296,512]{1,0:T(8,128)(2,1)} %get-tuple-element.212), channel_id=1, source_target_pairs={{0,8},{1,9},{2,10},{3,11},{4,12},{5,13},{6,14},{7,15},{8,0},{9,1},... | collective-permute-start | bytes 3981320 | tf_op jit(solution)/shard_map/ppermute | solution.py:1049
  206.2 41.4 %collective-permute-start.19 = (bf16[2,4,2048,128]{3,2,1,0:T(8,128)(2,1)}, bf16[2,4,2048,128]{3,2,1,0:T(8,128)(2,1)}, u32[]{:S(2)}, u32[]{:S(2)}) collective-permute-start(bf16[2,4,2048,128]{3,2,1,0:T(8,128)(2,1)} %get-tuple-element.225), channel_id=1, source_target_pairs={{0,8},{1,9},{2,10},{3,11},{4,12},{5,13},{6,14},{7,15},{8,0},{9,1},... | collective-permute-start | bytes 12582920 | tf_op jit(solution)/shard_map/ppermute | solution.py:1056
  206.2 41.4 %collective-permute-start.15 = (bf16[336,512]{1,0:T(8,128)(2,1)}, bf16[336,512]{1,0:T(8,128)(2,1)S(1)}, u32[]{:S(2)}, u32[]{:S(2)}) collective-permute-start(bf16[336,512]{1,0:T(8,128)(2,1)} %get-tuple-element.221), channel_id=1, source_target_pairs={{0,1},{1,0},{2,3},{3,2},{4,5},{5,4},{6,7},{7,6},{8,9},{9,8},{10,11... | collective-permute-start | bytes 1032200 | tf_op jit(solution)/shard_map/ppermute | solution.py:907
  207.1 40.5 %collective-permute-start.16 = (bf16[336,512]{1,0:T(8,128)(2,1)}, bf16[336,512]{1,0:T(8,128)(2,1)S(1)}, u32[]{:S(2)}, u32[]{:S(2)}) collective-permute-start(bf16[336,512]{1,0:T(8,128)(2,1)} %get-tuple-element.222), channel_id=1, source_target_pairs={{0,16},{1,17},{2,18},{3,19},{4,20},{5,21},{6,22},{7,23},{8,24},{9,... | collective-permute-start | bytes 1032200 | tf_op jit(solution)/shard_map/ppermute | solution.py:907
  208.6 39.0 %collective-permute-start.17 = (bf16[336,512]{1,0:T(8,128)(2,1)}, bf16[336,512]{1,0:T(8,128)(2,1)}, u32[]{:S(2)}, u32[]{:S(2)}) collective-permute-start(bf16[336,512]{1,0:T(8,128)(2,1)} %get-tuple-element.223), channel_id=1, source_target_pairs={{0,17},{1,16},{2,19},{3,18},{4,21},{5,20},{6,23},{7,22},{8,25},{9,... | collective-permute-start | bytes 1032200 | tf_op jit(solution)/shard_map/ppermute | solution.py:907
  209.8 37.9 %collective-permute-start.18 = (bf16[528,512]{1,0:T(8,128)(2,1)}, bf16[528,512]{1,0:T(8,128)(2,1)S(1)}, u32[]{:S(2)}, u32[]{:S(2)}) collective-permute-start(bf16[528,512]{1,0:T(8,128)(2,1)} %get-tuple-element.224), channel_id=1, source_target_pairs={{4,0},{12,1},{6,2},{14,3},{0,4},{8,5},{2,6},{10,7},{5,8},{13,9},{7... | collective-permute-start | bytes 1622024 | tf_op jit(solution)/shard_map/ppermute | solution.py:993
  252.7 16.7 %collective-permute-start.20 = (bf16[528,512]{1,0:T(8,128)(2,1)}, bf16[528,512]{1,0:T(8,128)(2,1)S(1)}, u32[]{:S(2)}, u32[]{:S(2)}) collective-permute-start(bf16[528,512]{1,0:T(8,128)(2,1)} %shard_map.263), channel_id=1, source_target_pairs={{6,0},{14,1},{0,2},{8,3},{2,4},{10,5},{4,6},{12,7},{7,8},{15,9},{1... | collective-permute-start | bytes 1622024 | tf_op jit(solution)/shard_map/ppermute | solution.py:993
  276.0 20.7 %collective-permute-start.25 = (bf16[528,512]{1,0:T(8,128)(2,1)S(1)}, bf16[528,512]{1,0:T(8,128)(2,1)S(1)}, u32[]{:S(2)}, u32[]{:S(2)}) collective-permute-start(bf16[528,512]{1,0:T(8,128)(2,1)S(1)} %copy-done.32), channel_id=1, source_target_pairs={{2,0},{10,1},{4,2},{12,3},{6,4},{14,5},{0,6},{8,7},{3,8},{11,9},{5... | collective-permute-start | bytes 1622024 | tf_op jit(solution)/shard_map/ppermute | solution.py:993
  298.2 15.9 %collective-permute-start.29 = (bf16[528,512]{1,0:T(8,128)(2,1)}, bf16[528,512]{1,0:T(8,128)(2,1)S(1)}, u32[]{:S(2)}, u32[]{:S(2)}) collective-permute-start(bf16[528,512]{1,0:T(8,128)(2,1)} %get-tuple-element.260), channel_id=1, source_target_pairs={{0,0},{8,1},{2,2},{10,3},{4,4},{12,5},{6,6},{14,7},{1,8},{9,9},{3,... | collective-permute-start | bytes 1622024 | tf_op jit(solution)/shard_map/ppermute | solution.py:993
  328.6 14.5 %collective-permute-start.34 = (bf16[512,512]{1,0:T(8,128)(2,1)S(1)}, bf16[512,512]{1,0:T(8,128)(2,1)S(1)}, u32[]{:S(2)}, u32[]{:S(2)}) collective-permute-start(bf16[512,512]{1,0:T(8,128)(2,1)S(1)} %pad_maximum_fusion.4), channel_id=1, source_target_pairs={{0,1},{1,0},{2,3},{3,2},{4,5},{5,4},{6,7},{7,6},{8,9},{9,8},{10,11... | collective-permute-start | bytes 1572872 | tf_op jit(solution)/shard_map/ppermute | solution.py:907
  330.4 20.7 %collective-permute-start.35 = (bf16[512,512]{1,0:T(8,128)(2,1)S(1)}, bf16[512,512]{1,0:T(8,128)(2,1)S(1)}, u32[]{:S(2)}, u32[]{:S(2)}) collective-permute-start(bf16[512,512]{1,0:T(8,128)(2,1)S(1)} %pad_maximum_fusion.4), channel_id=1, source_target_pairs={{0,16},{1,17},{2,18},{3,19},{4,20},{5,21},{6,22},{7,23},{8,24},{9,... | collective-permute-start | bytes 1572872 | tf_op jit(solution)/shard_map/ppermute | solution.py:907
  330.9 28.9 %collective-permute-start.36 = (bf16[512,512]{1,0:T(8,128)(2,1)S(1)}, bf16[512,512]{1,0:T(8,128)(2,1)S(1)}, u32[]{:S(2)}, u32[]{:S(2)}) collective-permute-start(bf16[512,512]{1,0:T(8,128)(2,1)S(1)} %pad_maximum_fusion.4), channel_id=1, source_target_pairs={{0,17},{1,16},{2,19},{3,18},{4,21},{5,20},{6,23},{7,22},{8,25},{9,... | collective-permute-start | bytes 1572872 | tf_op jit(solution)/shard_map/ppermute | solution.py:907
  332.2 27.6 %collective-permute-start.37 = (bf16[528,512]{1,0:T(8,128)(2,1)S(1)}, bf16[528,512]{1,0:T(8,128)(2,1)S(1)}, u32[]{:S(2)}, u32[]{:S(2)}) collective-permute-start(bf16[528,512]{1,0:T(8,128)(2,1)S(1)} %copy-done.15), channel_id=1, source_target_pairs={{4,0},{12,1},{6,2},{14,3},{0,4},{8,5},{2,6},{10,7},{5,8},{13,9},{7... | collective-permute-start | bytes 1622024 | tf_op jit(solution)/shard_map/ppermute | solution.py:993
  (49 other events, 587.2 us)

commit v6 on v5

--- a/solution.py
+++ b/solution.py
@@ -1065,22 +1065,18 @@
     token_of = lambda places, after: finish(
         places, after, kv_own, kv_came, dq, kinds, blocks
     )
-    three = token_of([1], first_grad)[0]
-    three, first_grad = tie(three, first_grad)
-    three = homeward(three, order[1])
-    one, two = token_of([2, 0], first_grad)
-    one, two, x = tie(one, two, x)
     keep, given = weigh(bit, x, dq, kv_own, kv_came)
-    three, given, first_grad = tie(three, given, first_grad)
+    given, first_grad = tie(given, first_grad)
     came = lax.ppermute(given, AXES, across)
-    last = token_of([3], first_grad)[0]
-    came, last = tie(came, last)
+    two, three = token_of([0, 1], first_grad)
+    came, two, three, first_grad = tie(came, two, three, first_grad)
 
     pieces, send, join = start(stages[1], [keep, came])
-    *pieces, two = tie(*pieces, two)
+    *pieces, two, three, first_grad = tie(*pieces, two, three, first_grad)
     came = send(pieces)
-    two = homeward(two, order[0])
-    *came, two = tie(*came, two)
+    two, three = homeward(two, order[0]), homeward(three, order[1])
+    one, last = token_of([2, 3], first_grad)
+    *came, two, three, one, last = tie(*came, two, three, one, last)
     late = added(join(came))
     early = added([stages[1][0](list(early_parts), VECTORS)[0], *early_came])
 

time: 377 us -> 375 us (level)
    pallas_call x15 -> x14, Pallas kernels: 211 us -> 208 us  [kernel_call(): pl.pallas_call(run, grid=grid, in_specs=[pl.BlockSpec(memory_space=index)...]
  transfers between devices with their start and end apart: 39 -> 39, of which waited for: 10 -> 9; matrix products, arithmetic and copies ran while one was open for 5% -> 5% of each run, Pallas kernels for 45% -> 43%
where the time goes in v6:
time: 375 us; the launch traced here: 369 us
  Pallas kernels  208 us (55%)
  waiting for transfers between devices  65.4 us (17%)
  starting transfers between devices  62.8 us (17%)
  other arithmetic  17.6 us (5%)
  local copies, waits for them, and re-layouts  13.4 us (4%)
    pallas_call x14, Pallas kernels, kernel_call(): pl.pallas_call(run, grid=grid, in_specs=[pl.BlockSpec(memory_space=index)...  208 us
    ppermute x15, waiting for transfers between devices, swap(): lax.ppermute(array, AXES, [(number(g, c), number(*move(g, c, s))) for g,...  48.6 us
    ppermute x8, starting transfers between devices, outward(): return lax.ppermute(block, AXES, route(r))  22.8 us
    ppermute x15, starting transfers between devices, swap(): lax.ppermute(array, AXES, [(number(g, c), number(*move(g, c, s))) for g,...  20.8 us
    ppermute x8, waiting for transfers between devices, outward(): return lax.ppermute(block, AXES, route(r))  14.6 us
    ppermute x8, starting transfers between devices, homeward(): return lax.ppermute(block, AXES, route(r, True))  11.4 us
  transfers between devices with their start and end apart: 39, of which 9 were waited for; matrix products, arithmetic and copies ran while one was open for 5% of the time, Pallas kernels for 43%

profile of v6, /device:TPU:0, one launch (start us, length us, event | category | flops | bytes accessed | tf_op | source)
XLA Modules:
  0.0 369.1 jit_solution(18378773905972002046)
XLA Ops:
  8.4 12.1 %collective-permute-done.5.refs_0_ = bf16[528,512]{1,0:T(8,128)(2,1)} collective-permute-done((bf16[528,512]{1,0:T(8,128)(2,1)S(1)}, bf16[528,512]{1,0:T(8,128)(2,1)}, u32[]{:S(2)}, u32[]{:S(2)}) %collective-permute-start.5) | collective-permute-done | bytes 540704 | tf_op jit(solution)/shard_map/ppermute | solution.py:990
  21.7 11.4 %collective-permute-start = (bf16[528,512]{1,0:T(8,128)(2,1)S(1)}, bf16[528,512]{1,0:T(8,128)(2,1)S(1)}, u32[]{:S(2)}, u32[]{:S(2)}) collective-permute-start(bf16[528,512]{1,0:T(8,128)(2,1)S(1)} %get-tuple-element.340), channel_id=1, source_target_pairs={{0,4},{1,12},{2,6},{3,14},{4,0},{5,8},{6,2},{7,10},{8,5},{9,13},{1... | collective-permute-start | bytes 1622024 | tf_op jit(solution)/shard_map/ppermute | solution.py:990
  38.2 4.9 %shard_map.254 = (bf16[4,2,4,512,128]{4,3,2,1,0:T(8,128)(2,1)}, bf16[4,2,4,512,128]{4,3,2,1,0:T(8,128)(2,1)}, bf16[4,2112,128]{2,1,0:T(8,128)(2,1)}, bf16[4,528,512]{2,1,0:T(8,128)(2,1)}) custom-call(bf16[528,512]{1,0:T(8,128)(2,1)} %collective-permute-done.5.refs_0_, bf16[512,512]{1,0:T(8,128)(2,1)} %refs_4_.11, ...), custom_call_target="tpu_custom_call" | custom-call | flops 1350565888 | bytes 4227072 | tf_op jit(solution)/shard_map/pallas_call | solution.py:292
  43.9 4.9 %shard_map.255 = (bf16[4,2,4,512,128]{4,3,2,1,0:T(8,128)(2,1)}, bf16[4,2,4,512,128]{4,3,2,1,0:T(8,128)(2,1)}, bf16[4,2112,128]{2,1,0:T(8,128)(2,1)}, bf16[4,528,512]{2,1,0:T(8,128)(2,1)}) custom-call(bf16[528,512]{1,0:T(8,128)(2,1)} %collective-permute-done.3.refs_0_, ...), custom_call_target="tpu_custom_call", output_to_operand_aliasing={{0}: (5, {}), {1}: (6, {}), {2}: (7, {}), {3}: (8, {})} | custom-call | flops 1350565888 | bytes 4227072 | tf_op jit(solution)/shard_map/pallas_call | solution.py:292
  49.6 5.0 %shard_map.256 = (bf16[4,2,4,512,128]{4,3,2,1,0:T(8,128)(2,1)}, bf16[4,2,4,512,128]{4,3,2,1,0:T(8,128)(2,1)}, bf16[4,2112,128]{2,1,0:T(8,128)(2,1)}, bf16[4,528,512]{2,1,0:T(8,128)(2,1)}) custom-call(bf16[528,512]{1,0:T(8,128)(2,1)} %copy-done.15, ...), custom_call_target="tpu_custom_call", output_to_operand_aliasing={{0}: (5, {}), {1}: (6, {}), {2}: (7, {}), {3}: (8, {})} | custom-call | flops 1350565888 | bytes 4227072 | tf_op jit(solution)/shard_map/pallas_call | solution.py:292
  59.5 3.9 %shard_map.257 = (bf16[4,2,4,512,128]{4,3,2,1,0:T(8,128)(2,1)}, bf16[4,2,4,512,128]{4,3,2,1,0:T(8,128)(2,1)}, bf16[4,2112,128]{2,1,0:T(8,128)(2,1)}, bf16[4,528,512]{2,1,0:T(8,128)(2,1)}) custom-call(bf16[528,512]{1,0:T(8,128)(2,1)} %copy-done.14, ...), custom_call_target="tpu_custom_call", output_to_operand_aliasing={{0}: (4, {}), {1}: (5, {}), {2}: (6, {}), {3}: (7, {})} | custom-call | flops 1350565888 | bytes 4227072 | tf_op jit(solution)/shard_map/pallas_call | solution.py:292
  63.6 3.6 collective-permute-start.9
  72.8 52.0 %shard_map.259 = (bf16[4,2112,4096]{2,1,0:T(8,128)(2,1)}, f32[2112,512]{1,0:T(8,128)}, f32[4,2112,128]{2,1,0:T(8,128)}) custom-call(bf16[4,2112,128]{2,1,0:T(8,128)(2,1)} %get-tuple-element.187.refs_0_, bf16[4,4096,128]{2,1,0:T(8,128)(2,1)} %bitcast.60, bf16[4,4096,128]{2,1,0:T(8,128)(2,1)} %bitcast.63), custom_call_target="tpu_custom_call" | custom-call | flops 35433480192 | bytes 69206016 | tf_op jit(solution)/shard_map/pallas_call | solution.py:292
  125.7 36.6 %shard_map.260 = (bf16[528,512]{1,0:T(8,128)(2,1)}, bf16[528,512]{1,0:T(8,128)(2,1)}, bf16[528,512]{1,0:T(8,128)(2,1)}, bf16[528,512]{1,0:T(8,128)(2,1)}, bf16[2...) custom-call(s32[1]{0:T(128)} %bitcast.refs_0_, ...), custom_call_target="tpu_custom_call" | custom-call | flops 16609443840 | bytes 45088768 | tf_op jit(solution)/shard_map/pallas_call | solution.py:292
  164.3 3.1 collective-permute-start.14
  167.5 35.4 %shard_map.261 = (bf16[2,4,2048,128]{3,2,1,0:T(8,128)(2,1)}, f32[4,2112,128]{2,1,0:T(8,128)}) custom-call(bf16[4,2112,128]{2,1,0:T(8,128)(2,1)} %get-tuple-element.187.refs_0_, bf16[4,2112,128]{2,1,0:T(8,128)(2,1)} %get-tuple-element.229.refs_1_, f32[4,2112,128]{2,1,0:T(8,128)} %get-tuple-element.217.refs_2_, ...), custom_call_target="tpu_custom_call" | custom-call | flops 26575110144 | bytes 34603008 | tf_op jit(solution)/shard_map/pallas_call | solution.py:292
  212.6 35.0 %shard_map.262 = (bf16[2,4,2048,128]{3,2,1,0:T(8,128)(2,1)}, bf16[4,2112,128]{2,1,0:T(8,128)(2,1)}) custom-call(bf16[4,2112,128]{2,1,0:T(8,128)(2,1)} %get-tuple-element.187.refs_0_, bf16[4,2112,128]{2,1,0:T(8,128)(2,1)} %get-tuple-element.229.refs_1_, f32[4,2112,128]{2,1,0:T(8,128)} %get-tuple-element.217.refs_2_, ...), custom_call_target="tpu_custom_call" | custom-call | flops 26575110144 | bytes 34603008 | tf_op jit(solution)/shard_map/pallas_call | solution.py:292
  247.6 9.0 %shard_map.263 = (f32[768,512]{1,0:T(8,128)}, bf16[768,512]{1,0:T(8,128)(2,1)}) custom-call(s32[1]{0:T(128)} %bitcast.refs_0_, bf16[4,528,512]{2,1,0:T(8,128)(2,1)} %get-tuple-element.185.refs_1_, bf16[4,2112,128]{2,1,0:T(8,128)(2,1)} %get-tuple-element.237.refs_2_, bf16[2,4,2048,128]{3,2,1,0:T(8,128)(2,1)} %get-tuple-element.238.refs_3_, ...), custom_call_target="tpu_custom_call" | custom-call | flops 3254779904 | bytes 12713984 | tf_op jit(solution)/shard_map/pallas_call | solution.py:292
  256.9 5.2 %shard_map.264 = (bf16[528,512]{1,0:T(8,128)(2,1)}, bf16[528,512]{1,0:T(8,128)(2,1)}) custom-call(bf16[4,528,512]{2,1,0:T(8,128)(2,1)} %bitcast.71, bf16[4,4,528,128]{3,2,1,0:T(8,128)(2,1)} %bitcast.69, bf16[2,4,4,512,128]{4,3,2,1,0:T(8,128)(2,1)} %bitcast.66, bf16[2,4,4,512,128]{4,3,2,1,0:T(8,128)(2,1)} %bitcast.16.refs_3_, bf16[512,512]{1,0:T(8,128)(2,1)} %refs_4_.11, ...), custom_call_target="tpu_custom_call" | custom-call | flops 1627389952 | bytes 9535488 | tf_op jit(solution)/shard_map/pallas_call | solution.py:292
  273.3 5.4 %shard_map.265 = (bf16[528,512]{1,0:T(8,128)(2,1)}, bf16[528,512]{1,0:T(8,128)(2,1)}) custom-call(bf16[4,528,512]{2,1,0:T(8,128)(2,1)} %bitcast.72, bf16[4,4,528,128]{3,2,1,0:T(8,128)(2,1)} %bitcast.70, bf16[2,4,4,512,128]{4,3,2,1,0:T(8,128)(2,1)} %bitcast.67, bf16[2,4,4,512,128]{4,3,2,1,0:T(8,128)(2,1)} %bitcast.16.refs_3_, bf16[512,512]{1,0:T(8,128)(2,1)} %refs_4_.11, ...), custom_call_target="tpu_custom_call" | custom-call | flops 1627389952 | bytes 9535488 | tf_op jit(solution)/shard_map/pallas_call | solution.py:292
  280.6 9.1 %collective-permute-done.23 = bf16[192,512]{1,0:T(8,128)(2,1)S(1)} collective-permute-done((bf16[192,512]{1,0:T(8,128)(2,1)}, bf16[192,512]{1,0:T(8,128)(2,1)S(1)}, u32[]{:S(2)}, u32[]{:S(2)}) %collective-permute-start.23) | collective-permute-done | bytes 196640 | tf_op jit(solution)/shard_map/ppermute | solution.py:907
  296.3 3.6 collective-permute-start.27
  304.7 6.2 %collective-permute-done.27 = bf16[144,512]{1,0:T(8,128)(2,1)S(1)} collective-permute-done((bf16[144,512]{1,0:T(8,128)(2,1)S(1)}, bf16[144,512]{1,0:T(8,128)(2,1)S(1)}, u32[]{:S(2)}, u32[]{:S(2)}) %collective-permute-start.27) | collective-permute-done | bytes 147488 | tf_op jit(solution)/shard_map/ppermute | solution.py:907
  311.0 4.5 %collective-permute-start.31 = (bf16[128,512]{1,0:T(8,128)(2,1)S(1)}, bf16[128,512]{1,0:T(8,128)(2,1)S(1)}, u32[]{:S(2)}, u32[]{:S(2)}) collective-permute-start(bf16[128,512]{1,0:T(8,128)(2,1)S(1)} %get-tuple-element.277), channel_id=1, source_target_pairs={{0,4},{1,5},{2,6},{3,7},{4,0},{5,1},{6,2},{7,3},{8,12},{9,13},{10,... | collective-permute-start | bytes 393224 | tf_op jit(solution)/shard_map/ppermute | solution.py:907
  319.7 6.3 %collective-permute-done.30 = bf16[128,512]{1,0:T(8,128)(2,1)S(1)} collective-permute-done((bf16[128,512]{1,0:T(8,128)(2,1)S(1)}, bf16[128,512]{1,0:T(8,128)(2,1)S(1)}, u32[]{:S(2)}, u32[]{:S(2)}) %collective-permute-start.30) | collective-permute-done | bytes 131104 | tf_op jit(solution)/shard_map/ppermute | solution.py:907
  332.6 8.4 %collective-permute-done.34 = bf16[512,512]{1,0:T(8,128)(2,1)S(1)} collective-permute-done((bf16[512,512]{1,0:T(8,128)(2,1)S(1)}, bf16[512,512]{1,0:T(8,128)(2,1)S(1)}, u32[]{:S(2)}, u32[]{:S(2)}) %collective-permute-start.34) | collective-permute-done | bytes 524320 | tf_op jit(solution)/shard_map/ppermute | solution.py:907
  341.0 16.7 %collective-permute-done.36 = bf16[512,512]{1,0:T(8,128)(2,1)S(1)} collective-permute-done((bf16[512,512]{1,0:T(8,128)(2,1)S(1)}, bf16[512,512]{1,0:T(8,128)(2,1)S(1)}, u32[]{:S(2)}, u32[]{:S(2)}) %collective-permute-start.36) | collective-permute-done | bytes 524320 | tf_op jit(solution)/shard_map/ppermute | solution.py:907
  359.9 3.9 %shard_map.266 = (f32[512,512]{1,0:T(8,128)}, f32[512,512]{1,0:T(8,128)}, f32[512,512]{1,0:T(8,128)}, f32[512,512]{1,0:T(8,128)}, f32[512,1024]{1,0:T(8,128)}, /*index=5*/f32[1024,512]{1,0:T(8,128)}) custom-call(s32[3]{0:T(128)} %get-tuple-element.353.refs_0_, bf16[2048,512]{1,0:T(8,128)(2,1)} %copy-done.2), custom_call_target="tpu_custom_call" | custom-call | bytes 6291456 | tf_op jit(solution)/shard_map/pallas_call | solution.py:292
  364.9 4.0 %shard_map.267 = (f32[512,512]{1,0:T(8,128)}, f32[512,512]{1,0:T(8,128)}, f32[512,512]{1,0:T(8,128)}, f32[512,512]{1,0:T(8,128)}, f32[512,1024]{1,0:T(8,128)}, /*index=5*/f32[1024,512]{1,0:T(8,128)}) custom-call(s32[3]{0:T(128)} %get-tuple-element.354.refs_0_, ...), custom_call_target="tpu_custom_call", output_to_operand_aliasing={{0}: (2, {}), {1}: (3, {}), {2}: (4, {}), {3}: (5, {}), {4}... | custom-call | bytes 6291456 | tf_op jit(solution)/shard_map/pallas_call | solution.py:292
  (183 shorter events, 77.2 us)
Async XLA Ops:
  2.6 17.9 %collective-permute-start.5 = (bf16[528,512]{1,0:T(8,128)(2,1)S(1)}, bf16[528,512]{1,0:T(8,128)(2,1)}, u32[]{:S(2)}, u32[]{:S(2)}) collective-permute-start(bf16[528,512]{1,0:T(8,128)(2,1)S(1)} %get-tuple-element.338), channel_id=1, source_target_pairs={{0,2},{1,10},{2,4},{3,12},{4,6},{5,14},{6,0},{7,8},{8,3},{9,11},{1... | collective-permute-start | bytes 1622024 | tf_op jit(solution)/shard_map/ppermute | solution.py:990
  5.6 31.0 %collective-permute-start.3 = (bf16[528,512]{1,0:T(8,128)(2,1)S(1)}, bf16[528,512]{1,0:T(8,128)(2,1)}, u32[]{:S(2)}, u32[]{:S(2)}) collective-permute-start(bf16[528,512]{1,0:T(8,128)(2,1)S(1)} %get-tuple-element.341), channel_id=1, source_target_pairs={{0,6},{1,14},{2,0},{3,8},{4,2},{5,10},{6,4},{7,12},{8,7},{9,15},{1... | collective-permute-start | bytes 1622024 | tf_op jit(solution)/shard_map/ppermute | solution.py:990
  7.7 30.3 %collective-permute-start.1 = (bf16[528,512]{1,0:T(8,128)(2,1)S(1)}, bf16[528,512]{1,0:T(8,128)(2,1)S(1)}, u32[]{:S(2)}, u32[]{:S(2)}) collective-permute-start(bf16[528,512]{1,0:T(8,128)(2,1)S(1)} %get-tuple-element.339), channel_id=1, source_target_pairs={{0,0},{1,8},{2,2},{3,10},{4,4},{5,12},{6,6},{7,14},{8,1},{9,9},{10... | collective-permute-start | bytes 1622024 | tf_op jit(solution)/shard_map/ppermute | solution.py:990
  20.5 17.7 %collective-permute-start.6 = (bf16[528,512]{1,0:T(8,128)(2,1)}, bf16[528,512]{1,0:T(8,128)(2,1)}, u32[]{:S(2)}, u32[]{:S(2)}) collective-permute-start(bf16[528,512]{1,0:T(8,128)(2,1)} %collective-permute-done.5.refs_0_), channel_id=1, source_target_pairs={{0,8},{1,9},{2,10},{3,11},{4,12},{5,13},{6,14},{7,15},{8,0},{9,1},... | collective-permute-start | bytes 1622024 | tf_op jit(solution)/shard_map/ppermute | solution.py:1007
  21.7 35.5 %collective-permute-start = (bf16[528,512]{1,0:T(8,128)(2,1)S(1)}, bf16[528,512]{1,0:T(8,128)(2,1)S(1)}, u32[]{:S(2)}, u32[]{:S(2)}) collective-permute-start(bf16[528,512]{1,0:T(8,128)(2,1)S(1)} %get-tuple-element.340), channel_id=1, source_target_pairs={{0,4},{1,12},{2,6},{3,14},{4,0},{5,8},{6,2},{7,10},{8,5},{9,13},{1... | collective-permute-start | bytes 1622024 | tf_op jit(solution)/shard_map/ppermute | solution.py:990
  63.4 61.5 %collective-permute-start.8 = (bf16[528,512]{1,0:T(8,128)(2,1)S(1)}, bf16[528,512]{1,0:T(8,128)(2,1)S(1)}, u32[]{:S(2)}, u32[]{:S(2)}) collective-permute-start(bf16[528,512]{1,0:T(8,128)(2,1)S(1)} %get-tuple-element.197), channel_id=1, source_target_pairs={{0,2},{1,10},{2,4},{3,12},{4,6},{5,14},{6,0},{7,8},{8,3},{9,11},{1... | collective-permute-start | bytes 1622024 | tf_op jit(solution)/shard_map/ppermute | solution.py:990
  63.6 61.2 %collective-permute-start.9 = (bf16[528,512]{1,0:T(8,128)(2,1)S(1)}, bf16[528,512]{1,0:T(8,128)(2,1)}, u32[]{:S(2)}, u32[]{:S(2)}) collective-permute-start(bf16[528,512]{1,0:T(8,128)(2,1)S(1)} %get-tuple-element.198), channel_id=1, source_target_pairs={{0,6},{1,14},{2,0},{3,8},{4,2},{5,10},{6,4},{7,12},{8,7},{9,15},{1... | collective-permute-start | bytes 1622024 | tf_op jit(solution)/shard_map/ppermute | solution.py:990
  67.2 57.7 %collective-permute-start.10 = (bf16[528,512]{1,0:T(8,128)(2,1)S(1)}, bf16[528,512]{1,0:T(8,128)(2,1)}, u32[]{:S(2)}, u32[]{:S(2)}) collective-permute-start(bf16[528,512]{1,0:T(8,128)(2,1)S(1)} %get-tuple-element.199), channel_id=1, source_target_pairs={{0,0},{1,8},{2,2},{3,10},{4,4},{5,12},{6,6},{7,14},{8,1},{9,9},{10... | collective-permute-start | bytes 1622024 | tf_op jit(solution)/shard_map/ppermute | solution.py:990
  68.9 56.0 %collective-permute-start.11 = (bf16[528,512]{1,0:T(8,128)(2,1)S(1)}, bf16[528,512]{1,0:T(8,128)(2,1)}, u32[]{:S(2)}, u32[]{:S(2)}) collective-permute-start(bf16[528,512]{1,0:T(8,128)(2,1)S(1)} %get-tuple-element.200), channel_id=1, source_target_pairs={{0,4},{1,12},{2,6},{3,14},{4,0},{5,8},{6,2},{7,10},{8,5},{9,13},{1... | collective-permute-start | bytes 1622024 | tf_op jit(solution)/shard_map/ppermute | solution.py:990
  162.3 40.6 %collective-permute-start.12 = (bf16[528,512]{1,0:T(8,128)(2,1)}, bf16[528,512]{1,0:T(8,128)(2,1)S(1)}, u32[]{:S(2)}, u32[]{:S(2)}) collective-permute-start(bf16[528,512]{1,0:T(8,128)(2,1)} %get-tuple-element.213), channel_id=1, source_target_pairs={{2,0},{10,1},{4,2},{12,3},{6,4},{14,5},{0,6},{8,7},{3,8},{11,9},{5... | collective-permute-start | bytes 1622024 | tf_op jit(solution)/shard_map/ppermute | solution.py:993
  163.7 39.2 %collective-permute-start.13 = (bf16[528,512]{1,0:T(8,128)(2,1)}, bf16[528,512]{1,0:T(8,128)(2,1)S(1)}, u32[]{:S(2)}, u32[]{:S(2)}) collective-permute-start(bf16[528,512]{1,0:T(8,128)(2,1)} %get-tuple-element.214), channel_id=1, source_target_pairs={{6,0},{14,1},{0,2},{8,3},{2,4},{10,5},{4,6},{12,7},{7,8},{15,9},{1... | collective-permute-start | bytes 1622024 | tf_op jit(solution)/shard_map/ppermute | solution.py:993
  164.3 38.6 %collective-permute-start.14 = (bf16[1296,512]{1,0:T(8,128)(2,1)}, bf16[1296,512]{1,0:T(8,128)(2,1)}, u32[]{:S(2)}, u32[]{:S(2)}) collective-permute-start(bf16[1296,512]{1,0:T(8,128)(2,1)} %get-tuple-element.215), channel_id=1, source_target_pairs={{0,8},{1,9},{2,10},{3,11},{4,12},{5,13},{6,14},{7,15},{8,0},{9,1},... | collective-permute-start | bytes 3981320 | tf_op jit(solution)/shard_map/ppermute | solution.py:1049
  206.2 41.5 %collective-permute-start.19 = (bf16[2,4,2048,128]{3,2,1,0:T(8,128)(2,1)}, bf16[2,4,2048,128]{3,2,1,0:T(8,128)(2,1)}, u32[]{:S(2)}, u32[]{:S(2)}) collective-permute-start(bf16[2,4,2048,128]{3,2,1,0:T(8,128)(2,1)} %get-tuple-element.228), channel_id=1, source_target_pairs={{0,8},{1,9},{2,10},{3,11},{4,12},{5,13},{6,14},{7,15},{8,0},{9,1},... | collective-permute-start | bytes 12582920 | tf_op jit(solution)/shard_map/ppermute | solution.py:1056
  206.2 41.4 %collective-permute-start.15 = (bf16[336,512]{1,0:T(8,128)(2,1)}, bf16[336,512]{1,0:T(8,128)(2,1)S(1)}, u32[]{:S(2)}, u32[]{:S(2)}) collective-permute-start(bf16[336,512]{1,0:T(8,128)(2,1)} %get-tuple-element.224), channel_id=1, source_target_pairs={{0,1},{1,0},{2,3},{3,2},{4,5},{5,4},{6,7},{7,6},{8,9},{9,8},{10,11... | collective-permute-start | bytes 1032200 | tf_op jit(solution)/shard_map/ppermute | solution.py:907
  207.0 40.5 %collective-permute-start.16 = (bf16[336,512]{1,0:T(8,128)(2,1)}, bf16[336,512]{1,0:T(8,128)(2,1)S(1)}, u32[]{:S(2)}, u32[]{:S(2)}) collective-permute-start(bf16[336,512]{1,0:T(8,128)(2,1)} %get-tuple-element.225), channel_id=1, source_target_pairs={{0,16},{1,17},{2,18},{3,19},{4,20},{5,21},{6,22},{7,23},{8,24},{9,... | collective-permute-start | bytes 1032200 | tf_op jit(solution)/shard_map/ppermute | solution.py:907
  208.6 39.0 %collective-permute-start.17 = (bf16[336,512]{1,0:T(8,128)(2,1)}, bf16[336,512]{1,0:T(8,128)(2,1)}, u32[]{:S(2)}, u32[]{:S(2)}) collective-permute-start(bf16[336,512]{1,0:T(8,128)(2,1)} %get-tuple-element.226), channel_id=1, source_target_pairs={{0,17},{1,16},{2,19},{3,18},{4,21},{5,20},{6,23},{7,22},{8,25},{9,... | collective-permute-start | bytes 1032200 | tf_op jit(solution)/shard_map/ppermute | solution.py:907
  209.7 37.9 %collective-permute-start.18 = (bf16[528,512]{1,0:T(8,128)(2,1)}, bf16[528,512]{1,0:T(8,128)(2,1)S(1)}, u32[]{:S(2)}, u32[]{:S(2)}) collective-permute-start(bf16[528,512]{1,0:T(8,128)(2,1)} %get-tuple-element.227), channel_id=1, source_target_pairs={{4,0},{12,1},{6,2},{14,3},{0,4},{8,5},{2,6},{10,7},{5,8},{13,9},{7... | collective-permute-start | bytes 1622024 | tf_op jit(solution)/shard_map/ppermute | solution.py:993
  265.1 24.6 %collective-permute-start.24 = (bf16[528,512]{1,0:T(8,128)(2,1)}, bf16[528,512]{1,0:T(8,128)(2,1)S(1)}, u32[]{:S(2)}, u32[]{:S(2)}) collective-permute-start(bf16[528,512]{1,0:T(8,128)(2,1)} %get-tuple-element.254), channel_id=1, source_target_pairs={{2,0},{10,1},{4,2},{12,3},{6,4},{14,5},{0,6},{8,7},{3,8},{11,9},{5... | collective-permute-start | bytes 1622024 | tf_op jit(solution)/shard_map/ppermute | solution.py:993
  267.5 24.5 %collective-permute-start.25 = (bf16[528,512]{1,0:T(8,128)(2,1)}, bf16[528,512]{1,0:T(8,128)(2,1)}, u32[]{:S(2)}, u32[]{:S(2)}) collective-permute-start(bf16[528,512]{1,0:T(8,128)(2,1)} %get-tuple-element.255), channel_id=1, source_target_pairs={{6,0},{14,1},{0,2},{8,3},{2,4},{10,5},{4,6},{12,7},{7,8},{15,9},{1... | collective-permute-start | bytes 1622024 | tf_op jit(solution)/shard_map/ppermute | solution.py:993
  271.3 18.4 %collective-permute-start.23 = (bf16[192,512]{1,0:T(8,128)(2,1)}, bf16[192,512]{1,0:T(8,128)(2,1)S(1)}, u32[]{:S(2)}, u32[]{:S(2)}) collective-permute-start(bf16[192,512]{1,0:T(8,128)(2,1)} %get-tuple-element.253), channel_id=1, source_target_pairs={{0,17},{1,16},{2,19},{3,18},{4,21},{5,20},{6,23},{7,22},{8,25},{9,... | collective-permute-start | bytes 589832 | tf_op jit(solution)/shard_map/ppermute | solution.py:907
  293.3 17.5 %collective-permute-start.29 = (bf16[528,512]{1,0:T(8,128)(2,1)}, bf16[528,512]{1,0:T(8,128)(2,1)S(1)}, u32[]{:S(2)}, u32[]{:S(2)}) collective-permute-start(bf16[528,512]{1,0:T(8,128)(2,1)} %get-tuple-element.266), channel_id=1, source_target_pairs={{0,0},{8,1},{2,2},{10,3},{4,4},{12,5},{6,6},{14,7},{1,8},{9,9},{3,... | collective-permute-start | bytes 1622024 | tf_op jit(solution)/shard_map/ppermute | solution.py:993
  311.0 15.1 %collective-permute-start.31 = (bf16[128,512]{1,0:T(8,128)(2,1)S(1)}, bf16[128,512]{1,0:T(8,128)(2,1)S(1)}, u32[]{:S(2)}, u32[]{:S(2)}) collective-permute-start(bf16[128,512]{1,0:T(8,128)(2,1)S(1)} %get-tuple-element.277), channel_id=1, source_target_pairs={{0,4},{1,5},{2,6},{3,7},{4,0},{5,1},{6,2},{7,3},{8,12},{9,13},{10,... | collective-permute-start | bytes 393224 | tf_op jit(solution)/shard_map/ppermute | solution.py:907
  327.3 30.3 %collective-permute-start.36 = (bf16[512,512]{1,0:T(8,128)(2,1)S(1)}, bf16[512,512]{1,0:T(8,128)(2,1)S(1)}, u32[]{:S(2)}, u32[]{:S(2)}) collective-permute-start(bf16[512,512]{1,0:T(8,128)(2,1)S(1)} %pad_maximum_fusion.4), channel_id=1, source_target_pairs={{0,17},{1,16},{2,19},{3,18},{4,21},{5,20},{6,23},{7,22},{8,25},{9,... | collective-permute-start | bytes 1572872 | tf_op jit(solution)/shard_map/ppermute | solution.py:907
  329.7 28.0 %collective-permute-start.37 = (bf16[528,512]{1,0:T(8,128)(2,1)S(1)}, bf16[528,512]{1,0:T(8,128)(2,1)S(1)}, u32[]{:S(2)}, u32[]{:S(2)}) collective-permute-start(bf16[528,512]{1,0:T(8,128)(2,1)S(1)} %copy-done.29), channel_id=1, source_target_pairs={{4,0},{12,1},{6,2},{14,3},{0,4},{8,5},{2,6},{10,7},{5,8},{13,9},{7... | collective-permute-start | bytes 1622024 | tf_op jit(solution)/shard_map/ppermute | solution.py:993
  (48 other events, 625.4 us)
